TPU v7x, 32 devices: a whole 2x2x4 slice. The times are simulated.
32 devices in a mesh: dp: 8 (over y, x, core), seq: 4 (over z).
Axes of the slice: x: 2, y: 2, z: 4, core: 2. Of those that a mesh axis runs over, the one named last changes fastest.
Arguments:
- tokens: bfloat16 [16, 1024, 2048], P('dp', 'seq'), may hold values from -6 to 6
- lengths: int32 [16, 4], P('dp'), may hold values from 1 to 1021, as said below
- w_qkv: bfloat16 [2048, 1920], P(('dp', 'seq')), may hold values from -0.125 to 0.125
- w_out: bfloat16 [1280, 2048], P(('dp', 'seq')), may hold values from -2.5 to 2.5
- w_gate_up: bfloat16 [2048, 12288], P(('dp', 'seq')), may hold values from -0.125 to 0.125
- w_down: bfloat16 [6144, 2048], P(('dp', 'seq')), may hold values from -0.078125 to 0.078125
- attn_gain: bfloat16 [2048], P(('dp', 'seq')), may hold values from 0.25 to 1.75
- ffn_gain: bfloat16 [2048], P(('dp', 'seq')), may hold values from 0.25 to 1.75
- head_gains: bfloat16 [128], P(('dp', 'seq')), may hold values from 0.25 to 1.75
- out_grad: bfloat16 [16, 1024, 2048], P('dp', 'seq'), may hold values from -6 to 6
Outputs:
- mixed: bfloat16 [16, 1024, 2048], P('dp', 'seq')
- tokens_grad: float32 [16, 1024, 2048], P('dp', 'seq')
- w_qkv_grad: float32 [2048, 1920], P(('dp', 'seq'))
- w_out_grad: float32 [1280, 2048], P(('dp', 'seq'))
- w_gate_up_grad: float32 [2048, 12288], P(('dp', 'seq'))
- w_down_grad: float32 [6144, 2048], P(('dp', 'seq'))
- attn_gain_grad: float32 [2048], P(('dp', 'seq'))
- ffn_gain_grad: float32 [2048], P(('dp', 'seq'))
- head_gains_grad: float32 [128], P(('dp', 'seq'))
Inputs may be any that keep to these rules, and one draw needn't show every extreme that they name: Each row's 4 lengths are positive and sum to 1024; in every row one document, at a place drawn per row, begins within the row's first 256 positions and ends within its last 256; in one row, drawn from the seed, every other document has length 1.
All inputs are finite; a program needn't handle non-finite values.
Results may differ from a plain program's by a relative error of at most 0.018.
Values may be sent and summed in bfloat16 or wider, within the bound.
A program may use at most 384 MiB of HBM per device.

v0:
```python
import math

import jax
import jax.numpy as jnp
from jax import lax
from jax.sharding import PartitionSpec as P

QUERY_HEADS = 20
KEY_VALUE_HEADS = 5
HEAD_SIZE = 64
FF = 6144
MICRO = 2


epsilon = 1e-06


def norm_rows(inputs, scales):
    return inputs * lax.rsqrt(jnp.mean(inputs * inputs, axis=-1, keepdims=True) + epsilon) * scales


def rope_tables(positions):
    inverse_freq = 10000.0 ** (-(jnp.arange(HEAD_SIZE // 2, dtype=jnp.float32) * 2.0 / HEAD_SIZE))
    angles = positions.astype(jnp.float32)[:, None] * inverse_freq[None, :]
    return (jnp.cos(angles)[:, None, :], jnp.sin(angles)[:, None, :])


def rotate(head_rows, cosine_table, sine_table):
    first_half = head_rows[..., : HEAD_SIZE // 2]
    second_half = head_rows[..., HEAD_SIZE // 2 :]
    return jnp.concatenate(
        [
            first_half * cosine_table - second_half * sine_table,
            second_half * cosine_table + first_half * sine_table,
        ],
        axis=-1,
    )


def prepare(projected_rows, gain_vec, cosine_table, sine_table):
    packed_row_count = projected_rows.shape[0]
    query_rows = projected_rows[:, : QUERY_HEADS * HEAD_SIZE].reshape(
        packed_row_count, QUERY_HEADS, HEAD_SIZE
    )
    key_head_rows = projected_rows[
        :, QUERY_HEADS * HEAD_SIZE : (QUERY_HEADS + KEY_VALUE_HEADS) * HEAD_SIZE
    ].reshape(packed_row_count, KEY_VALUE_HEADS, HEAD_SIZE)
    value_rows = projected_rows[:, (QUERY_HEADS + KEY_VALUE_HEADS) * HEAD_SIZE :].reshape(
        packed_row_count, KEY_VALUE_HEADS, HEAD_SIZE
    )
    query_rows = rotate(norm_rows(query_rows, gain_vec[:HEAD_SIZE]), cosine_table, sine_table)
    key_head_rows = rotate(norm_rows(key_head_rows, gain_vec[HEAD_SIZE:]), cosine_table, sine_table)
    return (query_rows, key_head_rows, value_rows)


def document_ids(row_lengths, positions):
    doc_ends = jnp.cumsum(row_lengths, dtype=jnp.int32)
    return jnp.sum((positions[:, None] >= doc_ends[None, :]).astype(jnp.int32), axis=1)


def soft_weights(scores, visible):
    masked = jnp.where(visible, scores, -1e30)
    row_top = jnp.max(masked, axis=-1, keepdims=True)
    exponent = jnp.exp(masked - row_top)
    return exponent / jnp.sum(exponent, axis=-1, keepdims=True)


def gated(gate_up_in):
    return jax.nn.silu(gate_up_in[:, :FF]) * gate_up_in[:, FF:]


def outer_sum(left, right):
    return lax.dot_general(
        left, right, (((0,), (0,)), ((), ())), preferred_element_type=jnp.float32
    )


def back_product(grad_rows, weight):
    return lax.dot_general(
        grad_rows, weight, (((1,), (1,)), ((), ())), preferred_element_type=jnp.float32
    )


def fetch_attention(w_qkv, w_out, attn_gain, head_gains):
    return (
        lax.all_gather(w_qkv, ("dp", "seq"), axis=0, tiled=True),
        lax.all_gather(w_out, ("dp", "seq"), axis=0, tiled=True),
        lax.all_gather(attn_gain, ("dp", "seq"), axis=0, tiled=True),
        lax.all_gather(head_gains, ("dp", "seq"), axis=0, tiled=True),
    )


def fetch_feed(w_gate_up, w_down, ffn_gain):
    return (
        lax.all_gather(w_gate_up, ("dp", "seq"), axis=0, tiled=True),
        lax.all_gather(w_down, ("dp", "seq"), axis=0, tiled=True),
        lax.all_gather(ffn_gain, ("dp", "seq"), axis=0, tiled=True),
    )


def gather_keys(key_low, value_low):
    return (
        lax.all_gather(key_low, "seq", axis=0, tiled=True),
        lax.all_gather(value_low, "seq", axis=0, tiled=True),
    )


def scatter_keys(term_fn, packed_row_count):
    return lax.psum_scatter(
        term_fn(jnp.int32(0), lax.axis_size("seq") * packed_row_count).astype(jnp.bfloat16),
        "seq",
        scatter_dimension=0,
        tiled=True,
    ).astype(jnp.float32)


def sum_feed(gate_up_grad, down_grad, ffn_gain_grad):
    return (
        lax.psum_scatter(gate_up_grad, ("dp", "seq"), scatter_dimension=0, tiled=True),
        lax.psum_scatter(down_grad, ("dp", "seq"), scatter_dimension=0, tiled=True),
        lax.psum_scatter(ffn_gain_grad, ("dp", "seq"), scatter_dimension=0, tiled=True),
    )


def sum_attention(qkv_grad, out_weight_grad, attn_gain_grad, head_grad):
    return (
        lax.psum_scatter(qkv_grad, ("dp", "seq"), scatter_dimension=0, tiled=True),
        lax.psum_scatter(out_weight_grad, ("dp", "seq"), scatter_dimension=0, tiled=True),
        lax.psum_scatter(attn_gain_grad, ("dp", "seq"), scatter_dimension=0, tiled=True),
        lax.psum_scatter(head_grad, ("dp", "seq"), scatter_dimension=0, tiled=True),
    )


def shards(
    tokens, lengths, w_qkv, w_out, w_gate_up, w_down, attn_gain, ffn_gain, head_gains, out_grad
):
    local_row_count = tokens.shape[1]
    seq_len = local_row_count * lax.axis_size("seq")
    queries_per_group = QUERY_HEADS // KEY_VALUE_HEADS
    scaling = 1.0 / math.sqrt(HEAD_SIZE)
    offset = lax.axis_index("seq") * local_row_count
    positions = jnp.arange(seq_len, dtype=jnp.int32)
    local_pos = offset + jnp.arange(local_row_count, dtype=jnp.int32)
    cosine_table, sine_table = rope_tables(local_pos)

    def run_rows(indices):
        token_count = len(indices)
        x_rows = jnp.concatenate([tokens[m].astype(jnp.float32) for m in indices], axis=0)
        cosine_all = jnp.concatenate([cosine_table] * token_count, axis=0)
        sine_all = jnp.concatenate([sine_table] * token_count, axis=0)
        qkv_full, out_full, attn_gain_full, head_full = fetch_attention(
            w_qkv, w_out, attn_gain, head_gains
        )
        normed, norm_pull = jax.vjp(norm_rows, x_rows, attn_gain_full.astype(jnp.float32))
        normed_low = normed.astype(jnp.bfloat16)
        projected_rows = jnp.dot(normed_low, qkv_full, preferred_element_type=jnp.float32)

        def prep_local(projected_in, gain_vec):
            return prepare(projected_in, gain_vec, cosine_all, sine_all)

        (query_rows, key_head_rows, value_rows), prep_pull = jax.vjp(
            prep_local, projected_rows, head_full.astype(jnp.float32)
        )
        query_rows_lower = query_rows.astype(jnp.bfloat16).reshape(
            token_count * local_row_count, KEY_VALUE_HEADS, queries_per_group, HEAD_SIZE
        )
        keys_low = key_head_rows.astype(jnp.bfloat16)
        values_low = value_rows.astype(jnp.bfloat16)
        kept = []
        head_parts = []
        for slot in range(token_count):
            start_row = slot * local_row_count
            keys_all, values_all = gather_keys(
                keys_low[start_row : start_row + local_row_count],
                values_low[start_row : start_row + local_row_count],
            )
            documents = document_ids(lengths[indices[slot]], positions)
            local_docs = lax.dynamic_slice_in_dim(documents, offset, local_row_count)
            visible = (positions[None, :] <= local_pos[:, None]) & (
                local_docs[:, None] == documents[None, :]
            )
            query_part = query_rows_lower[start_row : start_row + local_row_count]
            scores = (
                jnp.einsum(
                    "qhgd,khd->hgqk", query_part, keys_all, preferred_element_type=jnp.float32
                )
                * scaling
            )
            weights = soft_weights(scores, visible)
            weights_low = weights.astype(jnp.bfloat16)
            head_part = jnp.einsum(
                "hgqk,khd->qhgd", weights_low, values_all, preferred_element_type=jnp.float32
            )
            head_parts.append(
                head_part.reshape(local_row_count, QUERY_HEADS * HEAD_SIZE).astype(jnp.bfloat16)
            )
            kept.append((keys_all, values_all, weights, weights_low, query_part))
        heads_out = jnp.concatenate(head_parts, axis=0)
        middle = x_rows + jnp.dot(heads_out, out_full, preferred_element_type=jnp.float32)
        gate_up_full, down_full, ffn_gain_full = fetch_feed(w_gate_up, w_down, ffn_gain)
        normed2, norm2_pull = jax.vjp(norm_rows, middle, ffn_gain_full.astype(jnp.float32))
        normed2_low = normed2.astype(jnp.bfloat16)
        gate_up = jnp.dot(normed2_low, gate_up_full, preferred_element_type=jnp.float32)
        hidden_f, gate_pull = jax.vjp(gated, gate_up)
        hidden = hidden_f.astype(jnp.bfloat16)
        result = middle + jnp.dot(hidden, down_full, preferred_element_type=jnp.float32)
        result_low = result.astype(jnp.bfloat16)
        mixed_parts = [
            result_low[slot * local_row_count : (slot + 1) * local_row_count]
            for slot in range(token_count)
        ]
        barriered = lax.optimization_barrier((w_gate_up, w_down, ffn_gain, result))
        gate_up_back, down_back, unused_gain = fetch_feed(barriered[0], barriered[1], barriered[2])
        cotangent_low = jnp.concatenate([out_grad[m] for m in indices], axis=0)
        cotangent = cotangent_low.astype(jnp.float32)
        down_grad = outer_sum(hidden, cotangent_low)
        dhidden = back_product(cotangent_low, down_back)
        (dgate_up,) = gate_pull(dhidden)
        dgate_low = dgate_up.astype(jnp.bfloat16)
        gate_up_grad = outer_sum(normed2_low, dgate_low)
        dnormed2 = back_product(dgate_low, gate_up_back)
        dmiddle_norm, ffn_gain_grad = norm2_pull(dnormed2)
        dmiddle = cotangent + dmiddle_norm
        feed_sums = sum_feed(gate_up_grad, down_grad, ffn_gain_grad)
        barriered = lax.optimization_barrier((w_qkv, w_out, attn_gain, head_gains, dmiddle))
        qkv_back, out_back, unused_attn, unused_head = fetch_attention(
            barriered[0], barriered[1], barriered[2], barriered[3]
        )
        dattend = dmiddle.astype(jnp.bfloat16)
        out_weight_grad = outer_sum(heads_out, dattend)
        dheads = (
            back_product(dattend, out_back)
            .astype(jnp.bfloat16)
            .reshape(token_count * local_row_count, KEY_VALUE_HEADS, queries_per_group, HEAD_SIZE)
        )
        dquery_parts = []
        key_gradient_parts = []
        value_gradient_parts = []
        for slot in range(token_count):
            start_row = slot * local_row_count
            keys_all, values_all, weights, weights_low, query_part = kept[slot]
            dhead_part = dheads[start_row : start_row + local_row_count]
            dweights = jnp.einsum(
                "qhgd,khd->hgqk", dhead_part, values_all, preferred_element_type=jnp.float32
            )
            dscores = (
                weights * (dweights - jnp.sum(weights * dweights, axis=-1, keepdims=True))
            ).astype(jnp.bfloat16)
            dquery_part = jnp.einsum(
                "hgqk,khd->qhgd", dscores, keys_all, preferred_element_type=jnp.float32
            )
            dquery_parts.append(
                dquery_part.reshape(local_row_count, QUERY_HEADS, HEAD_SIZE) * scaling
            )

            def key_terms(
                start,
                packed_row_count,
                dscores=dscores,
                weights_low=weights_low,
                query_part=query_part,
                dhead_part=dhead_part,
            ):
                key_gradient_piece = (
                    jnp.einsum(
                        "hgqk,qhgd->khd", dscores, query_part, preferred_element_type=jnp.float32
                    )
                    * scaling
                )
                value_gradient_piece = jnp.einsum(
                    "hgqk,qhgd->khd", weights_low, dhead_part, preferred_element_type=jnp.float32
                )
                return jnp.concatenate(
                    [
                        key_gradient_piece.reshape(packed_row_count, KEY_VALUE_HEADS * HEAD_SIZE),
                        value_gradient_piece.reshape(packed_row_count, KEY_VALUE_HEADS * HEAD_SIZE),
                    ],
                    axis=1,
                )

            key_gradient_rows = scatter_keys(key_terms, local_row_count)
            key_gradient_parts.append(
                key_gradient_rows[:, : KEY_VALUE_HEADS * HEAD_SIZE].reshape(
                    local_row_count, KEY_VALUE_HEADS, HEAD_SIZE
                )
            )
            value_gradient_parts.append(
                key_gradient_rows[:, KEY_VALUE_HEADS * HEAD_SIZE :].reshape(
                    local_row_count, KEY_VALUE_HEADS, HEAD_SIZE
                )
            )
        dqueries = jnp.concatenate(dquery_parts, axis=0)
        dkeys = jnp.concatenate(key_gradient_parts, axis=0)
        dvalues = jnp.concatenate(value_gradient_parts, axis=0)
        dprojected, head_grad = prep_pull((dqueries, dkeys, dvalues))
        dprojected_low = dprojected.astype(jnp.bfloat16)
        qkv_grad = outer_sum(normed_low, dprojected_low)
        dnormed = back_product(dprojected_low, qkv_back)
        dx_norm, attn_gain_grad = norm_pull(dnormed)
        grad_all = dmiddle + dx_norm
        grad_parts = [
            grad_all[slot * local_row_count : (slot + 1) * local_row_count]
            for slot in range(token_count)
        ]
        attn_sums = sum_attention(qkv_grad, out_weight_grad, attn_gain_grad, head_grad)
        return (mixed_parts, grad_parts, feed_sums, attn_sums)

    mixed_rows, grad_rows, feed_totals, attn_totals = run_rows(list(range(MICRO)))
    mixed = jnp.stack(mixed_rows, axis=0)
    tokens_grad = jnp.stack(grad_rows, axis=0)
    return (
        mixed,
        tokens_grad,
        attn_totals[0],
        attn_totals[1],
        feed_totals[0],
        feed_totals[1],
        attn_totals[2],
        feed_totals[2],
        attn_totals[3],
    )


def solution(mesh):
    in_specs = (
        P("dp", "seq", None),
        P("dp", None),
        P(("dp", "seq"), None),
        P(("dp", "seq"), None),
        P(("dp", "seq"), None),
        P(("dp", "seq"), None),
        P(("dp", "seq")),
        P(("dp", "seq")),
        P(("dp", "seq")),
        P("dp", "seq", None),
    )
    out_specs = (
        P("dp", "seq", None),
        P("dp", "seq", None),
        P(("dp", "seq"), None),
        P(("dp", "seq"), None),
        P(("dp", "seq"), None),
        P(("dp", "seq"), None),
        P(("dp", "seq")),
        P(("dp", "seq")),
        P(("dp", "seq")),
    )
    return jax.shard_map(shards, mesh=mesh, in_specs=in_specs, out_specs=out_specs, check_vma=False)
```

profile of v0, /device:TPU:0, one launch (start us, length us, event | category | flops | bytes accessed | tf_op | source)
XLA Modules:
  0.0 3048.1 jit_solution(2623391133215304929)
XLA Ops:
  12.6 42.6 %all-reduce.18 = (bf16[2048]{0:T(1024)(128)(2,1)S(1)}, bf16[128]{0:T(256)(128)(2,1)S(1)}, bf16[2048]{0:T(1024)(128)(2,1)S(1)}) all-reduce(bf16[2048]{0:T(1024)(128)(2,1)S(1)} %dynamic-update-slice, bf16[128]{0:T(256)(128)(2,1)S(1)} %dynamic-update-slice.1, ...), channel_id=1, replica_groups=mesh['dp'=8,'seq'=4] {'dp','seq'}, use_global_device_ids=true, to_apply=%add.11 | all-reduce | flops 4224 | bytes 16896
  60.5 28.8 all-gather.9.cloned.1.call-done
  111.1 22.6 all_gather.49
  133.7 24.8 all_gather.47
  158.5 17.0 all_gather.51
  175.5 23.4 all_gather.50
  249.8 199.7 %all-gather.13.cloned.1.call-done = bf16[2048,12288]{1,0:T(8,128)(2,1)} async-done(((bf16[64,12288]{1,0:T(8,128)(2,1)}), bf16[2048,12288]{1,0:T(8,128)(2,1)}) %all-gather.13.cloned.1.call-update) | async-done | bytes 50331664 | tf_op jit(solution)/shard_map/all_gather | solution.py:95
  449.5 37.5 %fusion.119 = f32[512,12288]{1,0:T(8,128)} fusion(bf16[2048,12288]{1,0:T(8,128)(2,1)} %all-gather.13.cloned.1.call-done, f32[512,2048]{1,0:T(8,128)} %get-tuple-element.76, f32[2048]{0:T(1024)S(1)} %convert_element_type.115, f32[512]{0:T(512)S(1)} %fusion.107), kind=kOutput, calls=%fused_computation.197 | convolution fusion | flops 25772949504 | bytes 79702016 | tf_op jit(solution)/shard_map/dot_general | solution.py:203
  499.6 105.5 %all-gather.15.cloned.1.call-done = bf16[6144,2048]{1,0:T(8,128)(2,1)} async-done(((bf16[192,2048]{1,0:T(8,128)(2,1)}), bf16[6144,2048]{1,0:T(8,128)(2,1)}) %all-gather.15.cloned.1.call-update) | async-done | bytes 25165840 | tf_op jit(solution)/shard_map/all_gather | solution.py:96
  605.1 21.3 convolution_add_fusion
  628.8 150.7 %all-gather.17.cloned.1.call-done = bf16[6144,2048]{1,0:T(8,128)(2,1)} async-done(((bf16[192,2048]{1,0:T(8,128)(2,1)}), bf16[6144,2048]{1,0:T(8,128)(2,1)}) %all-gather.17.cloned.1.call-update) | async-done | bytes 25165840 | tf_op jit(solution)/shard_map/all_gather | solution.py:96
  779.4 29.7 fusion.52
  809.1 246.8 %all-gather.19.cloned.1.call-done = bf16[2048,12288]{1,0:T(8,128)(2,1)} async-done(((bf16[64,12288]{1,0:T(8,128)(2,1)}), bf16[2048,12288]{1,0:T(8,128)(2,1)}) %all-gather.19.cloned.1.call-update) | async-done | bytes 50331664 | tf_op jit(solution)/shard_map/all_gather | solution.py:95
  1055.9 37.9 %multiply_reduce_fusion = (f32[2048]{0:T(1024)}, f32[512]{0:T(512)S(1)}, f32[512,2048]{1,0:T(8,128)}) fusion(f32[512,2048]{1,0:T(8,128)} %get-tuple-element.76, f32[512]{0:T(512)S(1)} %fusion.107, f32[2048]{0:T(1024)S(1)} %convert_element_type.115, bf16[2048,12288]{1,0:T(8,128)(2,1)} %all-gather.19.cloned.1.call-done, f32[512,6144]{1,0:T(8,128)} %get-tuple-element.32, ...), kind=kOutput, calls=%fused_computation.57 | convolution fusion | flops 25788676096 | bytes 83906560 | tf_op jit(solution)/shard_map/dot_general | solution.py:79
  1100.6 63.4 %all-gather.21.cloned.1.call-done = bf16[1280,2048]{1,0:T(8,128)(2,1)} async-done(((bf16[40,2048]{1,0:T(8,128)(2,1)}), bf16[1280,2048]{1,0:T(8,128)(2,1)}) %all-gather.21.cloned.1.call-update) | async-done | bytes 5242896 | tf_op jit(solution)/shard_map/all_gather | solution.py:87
  1213.0 14.3 fusion.2
  1227.3 14.1 fusion.4
  1259.5 22.6 fusion.96
  1322.9 48.9 %fusion.42 = f32[2048,12288]{1,0:T(8,128)} fusion(f32[512,6144]{1,0:T(8,128)} %get-tuple-element.32, f32[512,6144]{1,0:T(8,128)} %get-tuple-element.31, f32[512,2048]{1,0:T(8,128)} %get-tuple-element.76, f32[2048]{0:T(1024)S(1)} %copy-done.20, f32[512]{0:T(512)S(1)} %copy-done.27), kind=kOutput, calls=%fused_computation.83 | convolution fusion | flops 25785532416 | bytes 130033664 | tf_op jit(solution)/shard_map/dot_general | solution.py:73
  1387.9 40.2 %all-reduce.17 = (f32[2048]{0:T(1024)S(1)}, f32[2048]{0:T(1024)S(1)}, f32[128]{0:T(128)S(1)}) all-reduce(f32[2048]{0:T(1024)S(1)} %get-tuple-element.19, f32[2048]{0:T(1024)S(1)} %copy-done.62, f32[128]{0:T(128)S(1)} %pad_add_fusion.2), channel_id=8, replica_groups=mesh['dp'=8,'seq'=4] {'dp','seq'}, use_global_device_ids=true, to_apply=%region_25.26.clone | all-reduce | flops 4224 | bytes 33792
  1438.9 364.4 %reduce-scatter.17.cloned.1.call-done = f32[192,2048]{1,0:T(8,128)} async-done(((f32[6144,2048]{1,0:T(8,128)}), f32[192,2048]{1,0:T(8,128)}) %reduce-scatter.17.cloned.1.call-update) | async-done | bytes 1572880 | tf_op jit(solution)/shard_map/reduce_scatter | solution.py:120
  1803.3 231.0 %reduce-scatter.13.cloned.1.call-done = f32[40,2048]{1,0:T(8,128)} async-done(((f32[1280,2048]{1,0:T(8,128)}), f32[40,2048]{1,0:T(8,128)}) %reduce-scatter.13.cloned.1.call-update) | async-done | bytes 327696 | tf_op jit(solution)/shard_map/reduce_scatter | solution.py:128
  2034.2 174.5 %reduce-scatter.11.cloned.1.call-done = f32[64,1920]{1,0:T(8,128)} async-done(((f32[2048,1920]{1,0:T(8,128)}), f32[64,1920]{1,0:T(8,128)}) %reduce-scatter.11.cloned.1.call-update) | async-done | bytes 491536 | tf_op jit(solution)/shard_map/reduce_scatter | solution.py:127
  2208.8 832.6 %reduce-scatter.15.cloned.1.call-done = f32[64,12288]{1,0:T(8,128)} async-done(((f32[2048,12288]{1,0:T(8,128)}), f32[64,12288]{1,0:T(8,128)}) %reduce-scatter.15.cloned.1.call-update) | async-done | bytes 3145744 | tf_op jit(solution)/shard_map/reduce_scatter | solution.py:119
  (255 shorter events, 238.9 us)
Async XLA Ops:
  7.2 82.2 %all-gather.9.cloned.1.call-start = ((), (), s32[]{:S(2)}) async-start(), calls=%async_computation.6 | async-start | bytes 8110080 | tf_op jit(solution)/shard_map/all_gather | solution.py:86
  7.9 233.3 %all-gather.11.cloned.1.call-start = ((), (), s32[]{:S(2)}) async-start(), calls=%async_computation.7 | async-start | bytes 5406720 | tf_op jit(solution)/shard_map/all_gather | solution.py:87
  8.7 440.9 %all-gather.13.cloned.1.call-start = ((), (), s32[]{:S(2)}) async-start(), calls=%async_computation.8 | async-start | bytes 51904512 | tf_op jit(solution)/shard_map/all_gather | solution.py:95
  9.4 595.7 %all-gather.15.cloned.1.call-start = ((), (), s32[]{:S(2)}) async-start(), calls=%async_computation.9 | async-start | bytes 25952256 | tf_op jit(solution)/shard_map/all_gather | solution.py:96
  10.0 769.4 %all-gather.17.cloned.1.call-start = ((), (), s32[]{:S(2)}) async-start(), calls=%async_computation.10 | async-start | bytes 25952256 | tf_op jit(solution)/shard_map/all_gather | solution.py:96
  56.6 1037.3 %copy-start.19 = (f32[2048]{0:T(1024)}, f32[2048]{0:T(1024)S(1)}, u32[]{:S(2)}) copy-start(f32[2048]{0:T(1024)S(1)} %convert_element_type.115) | copy-start | bytes 24580
  111.1 100.3 %copy-start.17 = (bf16[256,20,64]{0,2,1:T(8,128)(2,1)}, bf16[256,20,64]{0,2,1:T(8,128)(2,1)S(1)}, u32[]{:S(2)}) copy-start(bf16[256,20,64]{0,2,1:T(8,128)(2,1)S(1)} %get-tuple-element.49) | copy-start | bytes 1966084
  111.1 100.3 %copy-start.15 = (bf16[256,20,64]{0,2,1:T(8,128)(2,1)}, bf16[256,20,64]{0,2,1:T(8,128)(2,1)S(1)}, u32[]{:S(2)}) copy-start(bf16[256,20,64]{0,2,1:T(8,128)(2,1)S(1)} %get-tuple-element.50) | copy-start | bytes 1966084
  133.7 77.7 %copy-start.21 = (bf16[1024,5,64]{0,2,1:T(8,128)(2,1)}, bf16[1024,5,64]{0,2,1:T(8,128)(2,1)S(1)}, u32[]{:S(2)}) copy-start(bf16[1024,5,64]{0,2,1:T(8,128)(2,1)S(1)} %all_gather.49) | copy-start | bytes 1966084
  249.8 237.2 %copy-start.60 = (f32[512]{0:T(512)}, f32[512]{0:T(512)S(1)}, u32[]{:S(2)}) copy-start(f32[512]{0:T(512)S(1)} %get-tuple-element.75) | copy-start | bytes 6148
  249.8 844.0 %copy-start.26 = (f32[512]{0:T(512)}, f32[512]{0:T(512)S(1)}, u32[]{:S(2)}) copy-start(f32[512]{0:T(512)S(1)} %fusion.107) | copy-start | bytes 6148
  626.4 429.5 %all-gather.19.cloned.1.call-start = ((), (), s32[]{:S(2)}) async-start(), calls=%async_computation.11 | async-start | bytes 51904512 | tf_op jit(solution)/shard_map/all_gather | solution.py:95
  627.0 537.0 %all-gather.21.cloned.1.call-start = ((), (), s32[]{:S(2)}) async-start(), calls=%async_computation.12 | async-start | bytes 5406720 | tf_op jit(solution)/shard_map/all_gather | solution.py:87
  628.7 465.1 %copy-start.11 = (bf16[256,2048]{1,0:T(8,128)(2,1)}, bf16[256,2048]{1,0:T(8,128)(2,1)S(1)}, u32[]{:S(2)}) copy-start(bf16[256,2048]{1,0:T(8,128)(2,1)S(1)} %get-tuple-element.39) | copy-start | bytes 3145732
  628.7 465.1 %copy-start.13 = (bf16[256,2048]{1,0:T(8,128)(2,1)}, bf16[256,2048]{1,0:T(8,128)(2,1)S(1)}, u32[]{:S(2)}) copy-start(bf16[256,2048]{1,0:T(8,128)(2,1)S(1)} %get-tuple-element.40) | copy-start | bytes 3145732
  1100.3 70.7 %copy-start.37 = (bf16[1024,5,64]{0,2,1:T(8,128)(2,1)S(1)}, bf16[1024,5,64]{0,2,1:T(8,128)(2,1)}, u32[]{:S(2)}) copy-start(bf16[1024,5,64]{0,2,1:T(8,128)(2,1)} %all_gather.47) | copy-start | bytes 1966084
  1100.3 70.7 %copy-start.55 = (f32[5,4,256]{2,1,0:T(4,128)S(1)}, f32[5,4,256]{2,1,0:T(4,128)}, u32[]{:S(2)}) copy-start(f32[5,4,256]{2,1,0:T(4,128)} %get-tuple-element.73) | copy-start | bytes 61444
  1100.3 209.2 %reduce-scatter.7.cloned.1.call-start = ((), (), s32[]{:S(2)}) async-start(), calls=%async_computation.13 | async-start | bytes 1638400 | tf_op jit(solution)/shard_map/reduce_scatter | solution.py:109
  1212.4 98.9 %reduce-scatter.9.cloned.1.call-start = ((), (), s32[]{:S(2)}) async-start(), calls=%async_computation.14 | async-start | bytes 1638400 | tf_op jit(solution)/shard_map/reduce_scatter | solution.py:109
  1258.9 116.3 %all-gather.23.cloned.1.call-start = ((), (), s32[]{:S(2)}) async-start(), calls=%async_computation.15 | async-start | bytes 8110080 | tf_op jit(solution)/shard_map/all_gather | solution.py:86
  1259.5 543.8 %reduce-scatter.17.cloned.1.call-start = ((), (), s32[]{:S(2)}) async-start(), calls=%async_computation.19 | async-start | bytes 51904512 | tf_op jit(solution)/shard_map/reduce_scatter | solution.py:120
  1282.2 752.0 %reduce-scatter.13.cloned.1.call-start = ((), (), s32[]{:S(2)}) async-start(), calls=%async_computation.17 | async-start | bytes 10813440 | tf_op jit(solution)/shard_map/reduce_scatter | solution.py:128
  1291.2 917.6 %reduce-scatter.11.cloned.1.call-start = ((), (), s32[]{:S(2)}) async-start(), calls=%async_computation.16 | async-start | bytes 16220160 | tf_op jit(solution)/shard_map/reduce_scatter | solution.py:127
  1322.3 1719.1 %reduce-scatter.15.cloned.1.call-start = ((), (), s32[]{:S(2)}) async-start(), calls=%async_computation.18 | async-start | bytes 103809024 | tf_op jit(solution)/shard_map/reduce_scatter | solution.py:119
  (57 other events, 841.2 us)
Sparse Core Ops, SparseCore 0:
  10.8 78.4 all-gather.8
  92.2 73.8 all-gather.10
  168.9 280.5 all-gather.12
  452.2 152.8 all-gather.14
  626.5 152.8 all-gather.16
  782.2 273.7 all-gather.18
  1100.4 63.5 all-gather.20
  1212.6 30.0 reduce-scatter.6
  1259.0 30.0 reduce-scatter.8
  1291.8 74.2 all-gather.22
  1373.0 430.1 reduce-scatter.16
  1806.0 228.1 reduce-scatter.12
  2040.8 167.9 reduce-scatter.10
  2215.6 825.7 reduce-scatter.14
where the time goes:
time: 3060 us; the launch traced here: 3050 us
  waiting for transfers between devices  2400 us (78%)
  matrix products  354 us (12%)
  blocking collectives  170 us (6%)
  other arithmetic  68.6 us (2%)
  local copies, waits for them, and re-layouts  37 us (1%)
    reduce_scatter x1, waiting for transfers between devices, sum_feed(): lax.psum_scatter(gate_up_grad, ('dp', 'seq'), scatter_dimension=0, tiled=...  833 us
    all_gather x2, waiting for transfers between devices, fetch_feed(): lax.all_gather(w_gate_up, ('dp', 'seq'), axis=0, tiled=True)  446 us
    reduce_scatter x1, waiting for transfers between devices, sum_feed(): lax.psum_scatter(down_grad, ('dp', 'seq'), scatter_dimension=0, tiled=True)  364 us
    all_gather x2, waiting for transfers between devices, fetch_feed(): lax.all_gather(w_down, ('dp', 'seq'), axis=0, tiled=True)  256 us
    reduce_scatter x1, waiting for transfers between devices, sum_attention(): lax.psum_scatter(out_weight_grad, ('dp', 'seq'), scatter_dimension=0, til...  231 us
    reduce_scatter x1, waiting for transfers between devices, sum_attention(): lax.psum_scatter(qkv_grad, ('dp', 'seq'), scatter_dimension=0, tiled=True)  175 us
    dot_general x4, matrix products, outer_sum(): lax.dot_general(left, right, (((0,), (0,)), ((), ())), preferred_element_...  88.1 us
    dot_general x4, matrix products, back_product(): lax.dot_general(grad_rows, weight, (((1,), (1,)), ((), ())), preferred_el...  86.9 us
  transfers between devices with their start and end apart: 14, of which 10 were waited for; matrix products, arithmetic and copies ran while one was open for 11% of the time, Pallas kernels for 0%

commit v1 on v0

v1 whole, which is shorter than its diff:
```python
import math

import jax
import jax.numpy as jnp
from jax import lax
from jax.sharding import PartitionSpec as P

QUERY_HEADS = 20
KEY_VALUE_HEADS = 5
HEAD_SIZE = 64
GROUP = QUERY_HEADS // KEY_VALUE_HEADS
QW = QUERY_HEADS * HEAD_SIZE
KW = KEY_VALUE_HEADS * HEAD_SIZE
BOTH = ("dp", "seq")

epsilon = 1e-06
F32 = jnp.float32
BF16 = jnp.bfloat16


def norm_rows(inputs, scales):
    return inputs * lax.rsqrt(jnp.mean(inputs * inputs, axis=-1, keepdims=True) + epsilon) * scales


def rope_tables(positions):
    inverse_freq = 10000.0 ** (-(jnp.arange(HEAD_SIZE // 2, dtype=F32) * 2.0 / HEAD_SIZE))
    angles = positions.astype(F32)[:, None] * inverse_freq[None, :]
    return (jnp.cos(angles)[:, None, :], jnp.sin(angles)[:, None, :])


def rotate(head_rows, cosine_table, sine_table):
    first_half = head_rows[..., : HEAD_SIZE // 2]
    second_half = head_rows[..., HEAD_SIZE // 2 :]
    return jnp.concatenate(
        [
            first_half * cosine_table - second_half * sine_table,
            second_half * cosine_table + first_half * sine_table,
        ],
        axis=-1,
    )


def prepare(projected_rows, gain_vec, cosine_table, sine_table):
    count = projected_rows.shape[0]
    query_rows = projected_rows[:, :QW].reshape(count, QUERY_HEADS, HEAD_SIZE)
    key_rows = projected_rows[:, QW : QW + KW].reshape(count, KEY_VALUE_HEADS, HEAD_SIZE)
    value_rows = projected_rows[:, QW + KW :].reshape(count, KEY_VALUE_HEADS, HEAD_SIZE)
    query_rows = rotate(norm_rows(query_rows, gain_vec[:HEAD_SIZE]), cosine_table, sine_table)
    key_rows = rotate(norm_rows(key_rows, gain_vec[HEAD_SIZE:]), cosine_table, sine_table)
    return (query_rows, key_rows, value_rows)


def document_ids(row_lengths, positions):
    doc_ends = jnp.cumsum(row_lengths, axis=-1, dtype=jnp.int32)
    return jnp.sum((positions[None, :, None] >= doc_ends[:, None, :]).astype(jnp.int32), axis=2)


def soft_weights(scores, visible):
    masked = jnp.where(visible, scores, -1e30)
    row_top = jnp.max(masked, axis=-1, keepdims=True)
    exponent = jnp.exp(masked - row_top)
    return exponent / jnp.sum(exponent, axis=-1, keepdims=True)


def mm(a, b):
    return jnp.dot(a, b, preferred_element_type=F32)


def outer_sum(left, right):
    return lax.dot_general(left, right, (((0,), (0,)), ((), ())), preferred_element_type=F32)


def back_product(rows, weight):
    return lax.dot_general(rows, weight, (((1,), (1,)), ((), ())), preferred_element_type=F32)


def gather(x, axes):
    return lax.all_gather(x, axes, axis=0, tiled=True)


def scatter(x, axes):
    return lax.psum_scatter(x, axes, scatter_dimension=0, tiled=True)


def shards(
    tokens, lengths, w_qkv, w_out, w_gate_up, w_down, attn_gain, ffn_gain, head_gains, out_grad
):
    n_dp, n_seq = lax.axis_size("dp"), lax.axis_size("seq")
    rows, length, width = tokens.shape
    count = rows * length
    seq_len = length * n_seq
    ff = w_gate_up.shape[1] // 2
    part = ff // n_dp
    wr = w_gate_up.shape[0]
    scaling = 1.0 / math.sqrt(HEAD_SIZE)
    offset = lax.axis_index("seq") * length
    positions = jnp.arange(seq_len, dtype=jnp.int32)
    local_pos = offset + jnp.arange(length, dtype=jnp.int32)
    cosine_table, sine_table = rope_tables(local_pos)
    cosine_all = jnp.concatenate([cosine_table] * rows, axis=0)
    sine_all = jnp.concatenate([sine_table] * rows, axis=0)

    heads_column = jnp.pad(head_gains, (0, wr - head_gains.shape[0]))
    extra = jnp.stack([attn_gain, ffn_gain, heads_column], axis=1)
    extra = jnp.pad(extra, ((0, 0), (0, 125)))
    qkv_ext = gather(jnp.concatenate([w_qkv, extra], axis=1), BOTH)
    qkv_w = w_qkv.shape[1]
    qkv_full = qkv_ext[:, :qkv_w]
    attn_gain_full = qkv_ext[:, qkv_w].astype(F32)
    ffn_gain_full = qkv_ext[:, qkv_w + 1].astype(F32)
    head_full = (
        qkv_ext[:, qkv_w + 2]
        .reshape(n_dp * n_seq, wr)[:, : head_gains.shape[0]]
        .reshape(-1)
        .astype(F32)
    )
    out_full = gather(w_out, BOTH)

    spread = lax.all_to_all(w_gate_up.reshape(wr, 2, n_dp, part), "dp", 2, 0, tiled=False)
    spread = spread.reshape(n_dp * wr, 2 * part)
    gate_up_w = gather(spread, "seq").reshape(n_seq, n_dp, wr, 2 * part)
    gate_up_w = gate_up_w.transpose(1, 0, 2, 3).reshape(width, 2 * part)
    down_w = gather(w_down, "seq")

    cotangent_low = out_grad.reshape(count, width)
    cotangent_all = gather(cotangent_low, "dp")

    x_rows = tokens.reshape(count, width).astype(F32)
    normed, norm_pull = jax.vjp(norm_rows, x_rows, attn_gain_full)
    normed_low = normed.astype(BF16)
    projected_rows = mm(normed_low, qkv_full)

    def prep_local(projected_in, gain_vec):
        return prepare(projected_in, gain_vec, cosine_all, sine_all)

    (query_rows, key_rows, value_rows), prep_pull = jax.vjp(prep_local, projected_rows, head_full)
    queries = query_rows.astype(BF16).reshape(rows, length, KEY_VALUE_HEADS, GROUP, HEAD_SIZE)
    kv_low = jnp.concatenate(
        [key_rows.astype(BF16).reshape(count, KW), value_rows.astype(BF16).reshape(count, KW)],
        axis=1,
    )
    kv_all = gather(kv_low, "seq").reshape(n_seq, rows, length, 2, KEY_VALUE_HEADS, HEAD_SIZE)
    kv_all = kv_all.transpose(1, 3, 0, 2, 4, 5).reshape(
        rows, 2, seq_len, KEY_VALUE_HEADS, HEAD_SIZE
    )
    keys_all, values_all = kv_all[:, 0], kv_all[:, 1]
    documents = document_ids(lengths, positions)
    local_docs = lax.dynamic_slice_in_dim(documents, offset, length, axis=1)
    visible = (positions[None, None, :] <= local_pos[None, :, None]) & (
        local_docs[:, :, None] == documents[:, None, :]
    )
    visible = visible[:, None, None]
    scores = (
        jnp.einsum("rqhgd,rkhd->rhgqk", queries, keys_all, preferred_element_type=F32) * scaling
    )
    weights = soft_weights(scores, visible)
    weights_low = weights.astype(BF16)
    heads_out = (
        jnp.einsum("rhgqk,rkhd->rqhgd", weights_low, values_all, preferred_element_type=F32)
        .astype(BF16)
        .reshape(count, QW)
    )
    middle = x_rows + mm(heads_out, out_full)
    normed2, norm2_pull = jax.vjp(norm_rows, middle, ffn_gain_full)
    normed2_all = gather(normed2.astype(BF16), "dp")

    gate_up = mm(normed2_all, gate_up_w).astype(BF16)
    gate, up = gate_up[:, :part].astype(F32), gate_up[:, part:].astype(F32)
    sig = jax.nn.sigmoid(gate)
    hidden = (gate * sig * up).astype(BF16)
    mixed = middle + scatter(mm(hidden, down_w).astype(BF16), "dp").astype(F32)

    down_grad = scatter(outer_sum(hidden, cotangent_all).astype(BF16), "seq")
    dhidden = back_product(cotangent_all, down_w)
    dgate = dhidden * up * sig * (1.0 + gate * (1.0 - sig))
    dup = dhidden * gate * sig
    dgate_up = jnp.concatenate([dgate.astype(BF16), dup.astype(BF16)], axis=1)
    dnormed2 = scatter(back_product(dgate_up, gate_up_w).astype(BF16), "dp").astype(F32)
    gate_up_grad = outer_sum(normed2_all, dgate_up).astype(BF16)
    gate_up_grad = gate_up_grad.reshape(n_dp, n_seq, wr, 2 * part).transpose(1, 0, 2, 3)
    gate_up_grad = scatter(gate_up_grad.reshape(width, 2 * part), "seq")
    gate_up_grad = lax.all_to_all(
        gate_up_grad.reshape(n_dp, wr, 2, part), "dp", 0, 2, tiled=False
    ).reshape(wr, 2 * ff)

    dmiddle_norm, ffn_gain_grad = norm2_pull(dnormed2)
    dmiddle = cotangent_low.astype(F32) + dmiddle_norm
    dattend = dmiddle.astype(BF16)
    out_weight_grad = scatter(outer_sum(heads_out, dattend).astype(BF16), BOTH)
    dheads = (
        back_product(dattend, out_full)
        .astype(BF16)
        .reshape(rows, length, KEY_VALUE_HEADS, GROUP, HEAD_SIZE)
    )
    dweights = jnp.einsum("rqhgd,rkhd->rhgqk", dheads, values_all, preferred_element_type=F32)
    dscores = (
        weights * (dweights - jnp.sum(weights * dweights, axis=-1, keepdims=True))
    ).astype(BF16)
    dqueries = (
        jnp.einsum("rhgqk,rkhd->rqhgd", dscores, keys_all, preferred_element_type=F32).reshape(
            count, QUERY_HEADS, HEAD_SIZE
        )
        * scaling
    )
    dkeys = (
        jnp.einsum("rhgqk,rqhgd->rkhd", dscores, queries, preferred_element_type=F32) * scaling
    )
    dvalues = jnp.einsum("rhgqk,rqhgd->rkhd", weights_low, dheads, preferred_element_type=F32)
    dkv = jnp.concatenate(
        [dkeys.reshape(rows, n_seq, length, KW), dvalues.reshape(rows, n_seq, length, KW)], axis=3
    ).astype(BF16)
    dkv = scatter(dkv.transpose(1, 0, 2, 3).reshape(n_seq * count, 2 * KW), "seq").astype(F32)
    dprojected, head_grad = prep_pull(
        (
            dqueries,
            dkv[:, :KW].reshape(count, KEY_VALUE_HEADS, HEAD_SIZE),
            dkv[:, KW:].reshape(count, KEY_VALUE_HEADS, HEAD_SIZE),
        )
    )
    dprojected_low = dprojected.astype(BF16)
    qkv_grad = outer_sum(normed_low, dprojected_low).astype(BF16)
    qkv_grad = scatter(scatter(qkv_grad, "dp"), "seq")
    dnormed = back_product(dprojected_low, qkv_full)
    dx_norm, attn_gain_grad = norm_pull(dnormed)
    tokens_grad = dmiddle + dx_norm

    n_all = n_dp * n_seq
    small = jnp.concatenate(
        [
            attn_gain_grad.reshape(n_all, -1),
            ffn_gain_grad.reshape(n_all, -1),
            head_grad.reshape(n_all, -1),
        ],
        axis=1,
    )
    small = jnp.sum(lax.all_to_all(small, BOTH, 0, 0, tiled=False), axis=0)
    attn_gain_out = small[:wr]
    ffn_gain_out = small[wr : 2 * wr]
    head_out = small[2 * wr :]
    return (
        mixed.astype(BF16).reshape(rows, length, width),
        tokens_grad.reshape(rows, length, width),
        qkv_grad.astype(F32),
        out_weight_grad.astype(F32),
        gate_up_grad.astype(F32),
        down_grad.astype(F32),
        attn_gain_out,
        ffn_gain_out,
        head_out,
    )


def solution(mesh):
    in_specs = (
        P("dp", "seq", None),
        P("dp", None),
        P(("dp", "seq"), None),
        P(("dp", "seq"), None),
        P(("dp", "seq"), None),
        P(("dp", "seq"), None),
        P(("dp", "seq")),
        P(("dp", "seq")),
        P(("dp", "seq")),
        P("dp", "seq", None),
    )
    out_specs = (
        P("dp", "seq", None),
        P("dp", "seq", None),
        P(("dp", "seq"), None),
        P(("dp", "seq"), None),
        P(("dp", "seq"), None),
        P(("dp", "seq"), None),
        P(("dp", "seq")),
        P(("dp", "seq")),
        P(("dp", "seq")),
    )
    return jax.shard_map(shards, mesh=mesh, in_specs=in_specs, out_specs=out_specs, check_vma=False)
```

time: 3060 us -> 1520 us (0.50)
  waiting for transfers between devices: 2400 us -> 961 us
  blocking collectives: 170 us -> 0 us
  local copies, waits for them, and re-layouts: 37 us -> 114 us
    reduce_scatter x6 -> x8, waiting for transfers between devices: 1600 us -> 523 us  [scatter(): return lax.psum_scatter(x, axes, scatter_dimension=0, tiled=True)]
    all_gather x8 -> x7, waiting for transfers between devices: 795 us -> 416 us  [gather(): return lax.all_gather(x, axes, axis=0, tiled=True)]
    all_gather x4 -> x0, blocking collectives: 87.7 us -> none  [the longest x2 48.2 us: gather_keys(): lax.all_gather(value_low, 'seq', axis=0, tiled=True)]
    unnamed x2 -> x0, blocking collectives: 82.8 us -> none
    reshape x0 -> x15, local copies, waits for them, and re-layouts: none -> 47.3 us  [the longest x2 7.46 us: shards(): dkeys.reshape(rows, n_seq, length, KW)]
    dot_general x18 -> x13, matrix products: 243 us -> 233 us  [the longest x4 79.4 us: back_product(): lax.dot_general(rows, weight, (((1,), (1,)), ((), ())), preferred_element...]
  transfers between devices with their start and end apart: 14 -> 18, of which waited for: 10 -> 16; matrix products, arithmetic and copies ran while one was open for 11% -> 20% of each run, Pallas kernels for 0% -> 0%
where the time goes in v1:
time: 1520 us; the launch traced here: 1510 us
  waiting for transfers between devices  961 us (63%)
  matrix products  326 us (21%)
  local copies, waits for them, and re-layouts  114 us (8%)
  other arithmetic  85.5 us (6%)
    reduce_scatter x8, waiting for transfers between devices, scatter(): return lax.psum_scatter(x, axes, scatter_dimension=0, tiled=True)  523 us
    all_gather x7, waiting for transfers between devices, gather(): return lax.all_gather(x, axes, axis=0, tiled=True)  416 us
    dot_general x4, matrix products, back_product(): lax.dot_general(rows, weight, (((1,), (1,)), ((), ())), preferred_element...  79.4 us
    dot_general x4, matrix products, outer_sum(): lax.dot_general(left, right, (((0,), (0,)), ((), ())), preferred_element_...  73.4 us
    dot_general x4, matrix products, mm(): return jnp.dot(a, b, preferred_element_type=F32)  73 us
    convert_element_type x1, other arithmetic, shards(): dscores = (weights * (dweights - jnp.sum(weights * dweights, axis=-1, kee...  33.8 us
  transfers between devices with their start and end apart: 18, of which 16 were waited for; matrix products, arithmetic and copies ran while one was open for 20% of the time, Pallas kernels for 0%

profile of v1, /device:TPU:0, one launch (start us, length us, event | category | flops | bytes accessed | tf_op | source)
XLA Modules:
  0.0 1514.4 jit_solution(8385965707197783664)
XLA Ops:
  13.5 78.1 %all-gather.8.cloned.1.call-done = bf16[2048,2048]{1,0:T(8,128)(2,1)} async-done(((bf16[64,2048]{1,0:T(8,128)(2,1)}), bf16[2048,2048]{1,0:T(8,128)(2,1)}) %all-gather.8.cloned.1.call-update) | async-done | bytes 8388624 | tf_op jit(solution)/shard_map/all_gather | solution.py:78
  119.2 19.2 %all-to-all-done = bf16[1,64,2,8,768]{4,2,1,0,3:T(2,128)(2,1)S(1)} async-done(((bf16[1,64,2,8,768]{4,2,1,0,3:T(2,128)(2,1)}), bf16[1,64,2,8,768]{4,2,1,0,3:T(2,128)(2,1)S(1)}, u32[]{:S(2)}, u32[]{:S(2)}) %all-to-all-start) | async-done | bytes 1572896 | tf_op jit(solution)/shard_map/all_to_all | solution.py:119
  177.1 19.7 %fusion.74 = (f32[2,5,4,256]{3,2,1,0:T(4,128)S(1)}, f32[2,5,4,256,1024]{3,4,2,1,0:T(8,128)}) fusion(pred[2,256,1024]{1,2,0:T(8,128)(4,1)S(1)} %copy-done.26, bf16[2,256,5,4,64]{1,4,3,2,0:T(8,128)(2,1)} %copy_dynamic-update-slice_fusion, bf16[2,2,1024,5,64]{2,4,3,0,1:T(8,128)(2,1)} %reshape.347), kind=kOutput, calls=%fused_computation.155 | convolution fusion | flops 1384121344 | bytes 45129728 | tf_op jit(solution)/shard_map/sub | solution.py:61
  196.8 16.2 %fusion.48 = bf16[2,256,5,4,64]{1,4,3,2,0:T(8,128)(2,1)} fusion(bf16[2,2,1024,5,64]{2,4,3,0,1:T(8,128)(2,1)S(1)} %copy-done.10, f32[2,5,4,256,1024]{3,4,2,1,0:T(8,128)} %get-tuple-element.40, f32[2,5,4,256]{3,2,1,0:T(4,128)S(1)} %get-tuple-element.39), kind=kOutput, calls=%fused_computation.87 | convolution fusion | flops 1363804160 | bytes 44605440 | tf_op jit(solution)/shard_map/rhgqk,rkhd->rqhgd/dot_general | solution.py:159
  241.9 105.6 %all-gather.16.cloned.1.call-done = bf16[2048,1536]{1,0:T(8,128)(2,1)} async-done(((bf16[512,1536]{1,0:T(8,128)(2,1)}), bf16[2048,1536]{1,0:T(8,128)(2,1)}) %all-gather.16.cloned.1.call-update) | async-done | bytes 6291472 | tf_op jit(solution)/shard_map/all_gather | solution.py:78
  353.6 84.3 %all-gather.14.cloned.1.call-done = bf16[4096,2048]{1,0:T(8,128)(2,1)} async-done(((bf16[512,2048]{1,0:T(8,128)(2,1)}), bf16[4096,2048]{1,0:T(8,128)(2,1)}) %all-gather.14.cloned.1.call-update) | async-done | bytes 16777232 | tf_op jit(solution)/shard_map/all_gather | solution.py:78
  437.9 32.8 %convolution_convert_fusion.2 = bf16[4096,1536]{0,1:T(8,128)(2,1)} fusion(bf16[4096,2048]{1,0:T(8,128)(2,1)} %all-gather.14.cloned.1.call-done, bf16[2048,1536]{1,0:T(8,128)(2,1)} %bitcast.193), kind=kOutput, calls=%fused_computation.21 | convolution fusion | flops 25776095232 | bytes 35651584 | tf_op jit(solution)/shard_map/dot_general | solution.py:66
  470.6 32.2 %all-gather.18.cloned.1.call-done = bf16[768,2048]{1,0:T(8,128)(2,1)} async-done(((bf16[192,2048]{1,0:T(8,128)(2,1)}), bf16[768,2048]{1,0:T(8,128)(2,1)}) %all-gather.18.cloned.1.call-update) | async-done | bytes 3145744 | tf_op jit(solution)/shard_map/all_gather | solution.py:78
  502.8 90.4 %all-gather.20.cloned.1.call-done = bf16[4096,2048]{1,0:T(8,128)(2,1)} async-done(((bf16[512,2048]{1,0:T(8,128)(2,1)}), bf16[4096,2048]{1,0:T(8,128)(2,1)}) %all-gather.20.cloned.1.call-update) | async-done | bytes 16777232 | tf_op jit(solution)/shard_map/all_gather | solution.py:78
  593.3 29.1 %fusion.11 = (bf16[4096,768]{0,1:T(8,128)(2,1)}, bf16[4096,768]{0,1:T(8,128)(2,1)}) fusion(bf16[4096,1536]{0,1:T(8,128)(2,1)} %convolution_convert_fusion.2, bf16[4096,2048]{1,0:T(8,128)(2,1)} %all-gather.20.cloned.1.call-done, bf16[768,2048]{1,0:T(8,128)(2,1)} %all-gather.18.cloned.1.call-done), kind=kOutput, calls=%fused_computation.25 | convolution fusion | flops 12932087808 | bytes 45088768 | tf_op jit(solution)/shard_map/dot_general | solution.py:74
  622.4 32.9 %convolution_convert_fusion = bf16[4096,2048]{1,0:T(8,128)(2,1)} fusion(bf16[2048,1536]{1,0:T(8,128)(2,1)} %bitcast.194, bf16[4096,768]{0,1:T(8,128)(2,1)} %get-tuple-element.20, bf16[4096,768]{0,1:T(8,128)(2,1)} %get-tuple-element.19), kind=kOutput, calls=%fused_computation.19 | convolution fusion | flops 25803358208 | bytes 35651584 | tf_op jit(solution)/shard_map/dot_general | solution.py:74
  657.1 27.0 %convolution_convert_fusion.1 = bf16[4096,2048]{1,0:T(8,128)(2,1)} fusion(bf16[768,2048]{1,0:T(8,128)(2,1)S(1)} %copy-done.53, bf16[4096,1536]{0,1:T(8,128)(2,1)} %convolution_convert_fusion.2), kind=kOutput, calls=%fused_computation.20 | convolution fusion | flops 12918456320 | bytes 32505856 | tf_op jit(solution)/shard_map/dot_general | solution.py:66
  684.2 87.2 %reduce-scatter.11.cloned.1.call-done = bf16[512,2048]{1,0:T(8,128)(2,1)} async-done(((bf16[4096,2048]{1,0:T(8,128)(2,1)}), bf16[512,2048]{1,0:T(8,128)(2,1)}) %reduce-scatter.11.cloned.1.call-update) | async-done | bytes 2097168 | tf_op jit(solution)/shard_map/reduce_scatter | solution.py:82
  776.1 114.8 %reduce-scatter.9.cloned.1.call-done = bf16[512,2048]{1,0:T(8,128)(2,1)} async-done(((bf16[4096,2048]{1,0:T(8,128)(2,1)}), bf16[512,2048]{1,0:T(8,128)(2,1)}) %reduce-scatter.9.cloned.1.call-update) | async-done | bytes 2097168 | tf_op jit(solution)/shard_map/reduce_scatter | solution.py:82
  912.4 17.2 %fusion.52 = bf16[2,1024,5,64]{1,3,2,0:T(8,128)(2,1)} fusion(bf16[2,256,5,4,64]{1,4,3,2,0:T(8,128)(2,1)} %copy.144, f32[2,5,4,256,1024]{3,4,2,1,0:T(8,128)} %get-tuple-element.40, f32[2,5,4,256]{3,2,1,0:T(4,128)S(1)} %copy-done.38), kind=kOutput, calls=%fused_computation.89 | convolution fusion | flops 1363804160 | bytes 44605440 | tf_op jit(solution)/shard_map/rhgqk,rqhgd->rkhd/dot_general | solution.py:208
  929.6 26.7 %fusion.1 = (f32[2,5,4,256]{3,2,1,0:T(4,128)S(1)}, f32[2,5,1024,256,4]{3,2,4,1,0:T(8,128)}) fusion(f32[2,5,4,256,1024]{3,4,2,1,0:T(8,128)} %get-tuple-element.40, f32[2,5,4,256]{3,2,1,0:T(4,128)S(1)} %copy-done.38, bf16[2,256,5,4,64]{1,4,3,2,0:T(8,128)(2,1)} %copy.144, bf16[2,2,1024,5,64]{2,4,3,0,1:T(8,128)(2,1)S(1)} %copy-done.11), kind=kOutput, calls=%fused_computation.3 | convolution fusion | flops 1373624320 | bytes 86589440 | tf_op jit(solution)/shard_map/rqhgd,rkhd->rhgqk/dot_general | solution.py:195
  963.6 33.8 %fusion.3 = bf16[2,5,4,256,1024]{3,4,2,1,0:T(8,128)(2,1)} fusion(f32[2,5,1024,256,4]{3,2,4,1,0:T(8,128)} %get-tuple-element.44, f32[2,5,4,256]{3,2,1,0:T(4,128)S(1)} %get-tuple-element.43, f32[2,5,4,256,1024]{3,4,2,1,0:T(8,128)} %get-tuple-element.40, f32[2,5,4,256]{3,2,1,0:T(4,128)S(1)} %copy-done.38), kind=kLoop, calls=%fused_computation.5 | loop fusion | flops 41943040 | bytes 104939520 | tf_op jit(solution)/shard_map/convert_element_type | solution.py:198
  1021.1 34.0 %fusion.23 = bf16[2048,1536]{1,0:T(8,128)(2,1)} fusion(bf16[4096,2048]{1,0:T(8,128)(2,1)} %all-gather.14.cloned.1.call-done, bf16[4096,768]{0,1:T(8,128)(2,1)} %get-tuple-element.20, bf16[4096,768]{0,1:T(8,128)(2,1)} %get-tuple-element.19), kind=kOutput, calls=%fused_computation.39 | convolution fusion | flops 25798115328 | bytes 35651584 | tf_op jit(solution)/shard_map/dot_general | solution.py:70
  1061.3 23.1 %convolution_convert_fusion.5 = bf16[768,2048]{1,0:T(8,128)(2,1)} fusion(bf16[4096,2048]{1,0:T(8,128)(2,1)} %all-gather.20.cloned.1.call-done, bf16[4096,1536]{0,1:T(8,128)(2,1)} %convolution_convert_fusion.2), kind=kOutput, calls=%fused_computation.72 | convolution fusion | flops 12911640576 | bytes 32505856 | tf_op jit(solution)/shard_map/dot_general | solution.py:70
  1137.2 48.9 %reduce-scatter.21.cloned.1.call-done = bf16[512,1536]{1,0:T(8,128)(2,1)} async-done(((bf16[2048,1536]{1,0:T(8,128)(2,1)}), bf16[512,1536]{1,0:T(8,128)(2,1)}) %reduce-scatter.21.cloned.1.call-update) | async-done | bytes 1572880 | tf_op jit(solution)/shard_map/reduce_scatter | solution.py:82
  1194.4 55.2 %reduce-scatter.23.cloned.1.call-done = bf16[192,2048]{1,0:T(8,128)(2,1)} async-done(((bf16[768,2048]{1,0:T(8,128)(2,1)}), bf16[192,2048]{1,0:T(8,128)(2,1)}) %reduce-scatter.23.cloned.1.call-update) | async-done | bytes 786448 | tf_op jit(solution)/shard_map/reduce_scatter | solution.py:82
  1262.0 60.5 %reduce-scatter.15.cloned.1.call-done = bf16[256,1920]{1,0:T(8,128)(2,1)} async-done(((bf16[2048,1920]{1,0:T(8,128)(2,1)}), bf16[256,1920]{1,0:T(8,128)(2,1)}) %reduce-scatter.15.cloned.1.call-update) | async-done | bytes 983056 | tf_op jit(solution)/shard_map/reduce_scatter | solution.py:82
  1347.9 130.9 %reduce-scatter.19.cloned.1.call-done = bf16[40,2048]{1,0:T(8,128)(2,1)} async-done(((bf16[1280,2048]{1,0:T(8,128)(2,1)}), bf16[40,2048]{1,0:T(8,128)(2,1)}) %reduce-scatter.19.cloned.1.call-update) | async-done | bytes 163856 | tf_op jit(solution)/shard_map/reduce_scatter | solution.py:82
  1480.5 25.4 %reduce-scatter.17.cloned.1.call-done = bf16[64,1920]{1,0:T(8,128)(2,1)} async-done(((bf16[256,1920]{1,0:T(8,128)(2,1)}), bf16[64,1920]{1,0:T(8,128)(2,1)}) %reduce-scatter.17.cloned.1.call-update) | async-done | bytes 245776 | tf_op jit(solution)/shard_map/reduce_scatter | solution.py:82
  (255 shorter events, 274.3 us)
Async XLA Ops:
  7.2 84.5 %all-gather.8.cloned.1.call-start = ((), (), s32[]{:S(2)}) async-start(), calls=%async_computation.11 | async-start | bytes 8650752 | tf_op jit(solution)/shard_map/all_gather | solution.py:78
  10.5 153.4 %all-gather.10.cloned.1.call-start = ((), (), s32[]{:S(2)}) async-start(), calls=%async_computation.12 | async-start | bytes 3276800 | tf_op jit(solution)/shard_map/all_gather | solution.py:78
  13.2 88.5 %copy-start.44 = (f32[512]{0:T(512)}, f32[512]{0:T(512)S(1)}, u32[]{:S(2)}) copy-start(f32[512]{0:T(512)S(1)} %rsqrt.40) | copy-start | bytes 6148
  13.5 134.9 %copy-start.15 = (f32[512,32]{0,1:T(8,128)}, f32[512,32]{0,1:T(8,128)S(1)}, u32[]{:S(2)}) copy-start(f32[512,32]{0,1:T(8,128)S(1)} %maximum_bitcast_fusion) | copy-start | bytes 196612
  13.5 134.9 %copy-start.17 = (f32[512,32]{0,1:T(8,128)}, f32[512,32]{0,1:T(8,128)S(1)}, u32[]{:S(2)}) copy-start(f32[512,32]{0,1:T(8,128)S(1)} %maximum_bitcast_fusion.1) | copy-start | bytes 196612
  93.4 143.9 %copy-start.33 = (f32[2048]{0:T(1024)}, f32[2048]{0:T(1024)S(1)}, u32[]{:S(2)}) copy-start(f32[2048]{0:T(1024)S(1)} %get-tuple-element.9) | copy-start | bytes 24580
  110.4 120.8 %all-gather.12.cloned.1.call-start = ((), (), s32[]{:S(2)}) async-start(), calls=%async_computation.13 | async-start | bytes 5406720 | tf_op jit(solution)/shard_map/all_gather | solution.py:78
  113.8 24.6 %all-to-all-start = ((bf16[1,64,2,8,768]{4,2,1,0,3:T(2,128)(2,1)}), bf16[1,64,2,8,768]{4,2,1,0,3:T(2,128)(2,1)S(1)}, u32[]{:S(2)}, u32[]{:S(2)}) async-start(bf16[1,64,2,8,768]{4,2,1,0,3:T(2,128)(2,1)} %copy.141), calls=%async_computation | async-start | bytes 3145728 | tf_op jit(solution)/shard_map/all_to_all | solution.py:119
  117.4 230.0 %all-gather.16.cloned.1.call-start = ((), (), s32[]{:S(2)}) async-start(), calls=%async_computation.15 | async-start | bytes 7864320 | tf_op jit(solution)/shard_map/all_gather | solution.py:78
  139.8 298.0 %all-gather.14.cloned.1.call-start = ((), (), s32[]{:S(2)}) async-start(), calls=%async_computation.14 | async-start | bytes 18874368 | tf_op jit(solution)/shard_map/all_gather | solution.py:78
  240.5 262.3 %all-gather.18.cloned.1.call-start = ((), (), s32[]{:S(2)}) async-start(), calls=%async_computation.16 | async-start | bytes 3932160 | tf_op jit(solution)/shard_map/all_gather | solution.py:78
  241.1 352.2 %all-gather.20.cloned.1.call-start = ((), (), s32[]{:S(2)}) async-start(), calls=%async_computation.18 | async-start | bytes 18874368 | tf_op jit(solution)/shard_map/all_gather | solution.py:78
  241.8 529.5 %reduce-scatter.11.cloned.1.call-start = ((), (), s32[]{:S(2)}) async-start(), calls=%async_computation.19 | async-start | bytes 18874368 | tf_op jit(solution)/shard_map/reduce_scatter | solution.py:82
  655.2 235.7 %reduce-scatter.9.cloned.1.call-start = ((), (), s32[]{:S(2)}) async-start(), calls=%async_computation.17 | async-start | bytes 18874368 | tf_op jit(solution)/shard_map/reduce_scatter | solution.py:82
  684.1 92.0 %copy-start.49 = (f32[512]{0:T(512)S(1)}, f32[512]{0:T(512)}, u32[]{:S(2)}) copy-start(f32[512]{0:T(512)} %copy-done.48) | copy-start | bytes 6148
  684.1 206.8 %copy-start.9 = (bf16[2,256,2048]{2,1,0:T(8,128)(2,1)S(1)}, bf16[2,256,2048]{2,1,0:T(8,128)(2,1)}, u32[]{:S(2)}) copy-start(bf16[2,256,2048]{2,1,0:T(8,128)(2,1)} %param.19) | copy-start | bytes 6291460
  684.1 427.1 %reduce-scatter.13.cloned.1.call-start = ((), (), s32[]{:S(2)}) async-start(), calls=%async_computation.20 | async-start | bytes 3276800 | tf_op jit(solution)/shard_map/reduce_scatter | solution.py:82
  1021.0 165.0 %reduce-scatter.21.cloned.1.call-start = ((), (), s32[]{:S(2)}) async-start(), calls=%async_computation.24 | async-start | bytes 7864320 | tf_op jit(solution)/shard_map/reduce_scatter | solution.py:82
  1061.3 188.4 %reduce-scatter.23.cloned.1.call-start = ((), (), s32[]{:S(2)}) async-start(), calls=%async_computation.25 | async-start | bytes 3932160 | tf_op jit(solution)/shard_map/reduce_scatter | solution.py:82
  1084.4 238.1 %reduce-scatter.15.cloned.1.call-start = ((), (), s32[]{:S(2)}) async-start(), calls=%async_computation.21 | async-start | bytes 8847360 | tf_op jit(solution)/shard_map/reduce_scatter | solution.py:82
  1129.2 349.6 %reduce-scatter.19.cloned.1.call-start = ((), (), s32[]{:S(2)}) async-start(), calls=%async_computation.23 | async-start | bytes 5406720 | tf_op jit(solution)/shard_map/reduce_scatter | solution.py:82
  1190.7 61.4 %all-to-all-start.1 = ((bf16[8,64,2,1,768]{4,2,1,3,0:T(2,128)(2,1)}), bf16[8,64,2,1,768]{4,2,1,3,0:T(2,128)(2,1)S(1)}, u32[]{:S(2)}, u32[]{:S(2)}) async-start(bf16[8,64,2,1,768]{4,2,1,3,0:T(2,128)(2,1)} %bitcast.45), calls=%async_computation.8 | async-start | bytes 3145728 | tf_op jit(solution)/shard_map/all_to_all | solution.py:182
  1194.3 311.5 %reduce-scatter.17.cloned.1.call-start = ((), (), s32[]{:S(2)}) async-start(), calls=%async_computation.22 | async-start | bytes 1228800 | tf_op jit(solution)/shard_map/reduce_scatter | solution.py:82
  1334.6 12.2 all-to-all-start.2
  (48 other events, 782.6 us)
Sparse Core Ops, SparseCore 0:
  11.5 80.0 all-gather.7
  110.5 53.3 all-gather.9
  166.8 64.3 all-gather.11
  233.2 114.2 all-gather.15
  349.7 88.0 all-gather.13
  439.3 63.4 all-gather.17
  504.7 88.4 all-gather.19
  655.4 115.9 reduce-scatter.10
  774.9 115.9 reduce-scatter.8
  1021.2 52.1 reduce-scatter.12
  1075.6 110.3 reduce-scatter.20
  1188.8 60.7 reduce-scatter.22
  1253.1 69.4 reduce-scatter.14
  1324.8 154.0 reduce-scatter.18
  1481.1 24.7 reduce-scatter.16

commit v2 on v1

v2 whole, which is shorter than its diff:
```python
import functools

import jax
import jax.numpy as jnp
from jax import lax
from jax.experimental import pallas as pl
from jax.experimental.pallas import tpu as pltpu
from jax.sharding import PartitionSpec as P

QUERY_HEADS = 20
KEY_VALUE_HEADS = 5
HEAD_SIZE = 64
GROUP = QUERY_HEADS // KEY_VALUE_HEADS
QW = QUERY_HEADS * HEAD_SIZE
KW = KEY_VALUE_HEADS * HEAD_SIZE
BOTH = ("dp", "seq")

epsilon = 1e-06
F32 = jnp.float32
BF16 = jnp.bfloat16
MESH = pl.DeviceIdType.MESH


def norm_rows(inputs, scales):
    return inputs * lax.rsqrt(jnp.mean(inputs * inputs, axis=-1, keepdims=True) + epsilon) * scales


def rope_tables(positions):
    inverse_freq = 10000.0 ** (-(jnp.arange(HEAD_SIZE // 2, dtype=F32) * 2.0 / HEAD_SIZE))
    angles = inverse_freq[:, None] * positions.astype(F32)[None, :]
    return (jnp.cos(angles)[None], jnp.sin(angles)[None])


def turn(heads, gain, cosine, sine):
    inverse = lax.rsqrt(jnp.mean(heads * heads, axis=1, keepdims=True) + epsilon)
    heads = heads * inverse * gain[None, :, None]
    first, second = heads[:, : HEAD_SIZE // 2], heads[:, HEAD_SIZE // 2 :]
    return jnp.concatenate([first * cosine - second * sine, second * cosine + first * sine], axis=1)


def prepare(projected, gains, cosine, sine):
    tokens = projected.shape[1]
    queries = projected[:QW].reshape(QUERY_HEADS, HEAD_SIZE, tokens)
    pairs = projected[QW:].reshape(KEY_VALUE_HEADS, 2, HEAD_SIZE, tokens)
    queries = turn(queries, gains[:HEAD_SIZE], cosine, sine) * (HEAD_SIZE**-0.5)
    keys = turn(pairs[:, 0], gains[HEAD_SIZE:], cosine, sine)
    pairs = jnp.stack([keys, pairs[:, 1]], axis=1)
    return queries.reshape(QW, tokens), pairs.reshape(2 * KW, tokens)


def dot(a, b):
    return jnp.dot(a, b, preferred_element_type=F32)


def seen(back, me, start, length):
    key = lax.broadcasted_iota(jnp.int32, (length, length), 0)
    found = key + (me - back) * length >= start
    if back == 0:
        found &= key <= lax.broadcasted_iota(jnp.int32, (length, length), 1)
    return found


def attend_kernel(blocks, me_ref, start_ref, q_ref, *refs):
    kv_refs, (o_ref, lse_ref, o_acc, l_acc) = refs[:blocks], refs[blocks:]
    me = me_ref[0]
    length = q_ref.shape[1]
    start = start_ref[0:1, :]
    for back in range(blocks):

        def block(back=back):
            keys = kv_refs[back][:HEAD_SIZE, :].T
            values = kv_refs[back][HEAD_SIZE:, :]
            visible = seen(back, me, start, length)
            for g in range(GROUP):
                rows = slice(g * HEAD_SIZE, (g + 1) * HEAD_SIZE)
                p = jnp.where(visible, jnp.exp(dot(keys, q_ref[rows, :])), 0.0)
                total = jnp.sum(p, axis=0, keepdims=True)
                out = dot(values, p.astype(BF16))
                if back == 0:
                    l_acc[g : g + 1, :] = total
                    o_acc[rows, :] = out
                else:
                    l_acc[g : g + 1, :] += total
                    o_acc[rows, :] += out

        if back == 0:
            block()
        else:
            pl.when(me >= back)(block)
    for g in range(GROUP):
        rows = slice(g * HEAD_SIZE, (g + 1) * HEAD_SIZE)
        o_ref[rows, :] = (o_acc[rows, :] / l_acc[g : g + 1, :]).astype(BF16)
        lse_ref[g : g + 1, :] = jnp.log(l_acc[g : g + 1, :])


def attend_back_kernel(blocks, me_ref, start_ref, q_ref, do_ref, o_ref, lse_ref, *refs):
    kv_refs, dq_ref = refs[:blocks], refs[blocks]
    dkv_refs, (dq_acc, dk_acc, dv_acc) = refs[blocks + 1 : 2 * blocks + 1], refs[2 * blocks + 1 :]
    me = me_ref[0]
    length = q_ref.shape[1]
    start = start_ref[0:1, :]
    for back in range(blocks):

        def block(back=back):
            keys_t = kv_refs[back][:HEAD_SIZE, :]
            keys = keys_t.T
            values = kv_refs[back][HEAD_SIZE:, :].T
            visible = seen(back, me, start, length)
            for g in range(GROUP):
                rows = slice(g * HEAD_SIZE, (g + 1) * HEAD_SIZE)
                q, do = q_ref[rows, :], do_ref[rows, :]
                p = jnp.exp(dot(keys, q) - lse_ref[g : g + 1, :])
                p = jnp.where(visible, p, 0.0)
                inner = jnp.sum(
                    do.astype(F32) * o_ref[rows, :].astype(F32), axis=0, keepdims=True
                )
                ds = (p * (dot(values, do) - inner)).astype(BF16)
                dv = dot(p.astype(BF16), do.T)
                dk = dot(ds, q.T)
                dq = dot(keys_t, ds)
                if g == 0:
                    dk_acc[...] = dk
                    dv_acc[...] = dv
                else:
                    dk_acc[...] += dk
                    dv_acc[...] += dv
                if back == 0:
                    dq_acc[rows, :] = dq
                else:
                    dq_acc[rows, :] += dq
            dkv_refs[back][:HEAD_SIZE, :] = dk_acc[...].T.astype(BF16)
            dkv_refs[back][HEAD_SIZE:, :] = dv_acc[...].T.astype(BF16)

        if back == 0:
            block()
        else:
            pl.when(me >= back)(block)

            @pl.when(me < back)
            def _(back=back):
                dkv_refs[back][...] = jnp.zeros_like(dkv_refs[back])

    dq_ref[...] = dq_acc[...]


def attend(me, start, queries, pairs, rows):
    blocks, length = len(pairs), queries.shape[1] // rows
    spec = lambda height: pl.BlockSpec((height, length), lambda r, h, m: (h, r))
    return pl.pallas_call(
        functools.partial(attend_kernel, blocks),
        grid_spec=pltpu.PrefetchScalarGridSpec(
            num_scalar_prefetch=1,
            grid=(rows, KEY_VALUE_HEADS),
            in_specs=[
                pl.BlockSpec((8, length), lambda r, h, m: (0, r)),
                spec(GROUP * HEAD_SIZE),
                *[spec(2 * HEAD_SIZE)] * blocks,
            ],
            out_specs=[spec(GROUP * HEAD_SIZE), spec(8)],
            scratch_shapes=[
                pltpu.VMEM((GROUP * HEAD_SIZE, length), F32),
                pltpu.VMEM((8, length), F32),
            ],
        ),
        out_shape=[
            jax.ShapeDtypeStruct(queries.shape, BF16),
            jax.ShapeDtypeStruct((8 * KEY_VALUE_HEADS, queries.shape[1]), F32),
        ],
        compiler_params=pltpu.CompilerParams(vmem_limit_bytes=48 * 2**20),
        name="attend",
    )(me, start, queries, *pairs)


def attend_back(me, start, queries, pairs, dheads, heads, lse, rows):
    blocks, length = len(pairs), queries.shape[1] // rows
    spec = lambda height: pl.BlockSpec((height, length), lambda r, h, m: (h, r))
    wide, pair = spec(GROUP * HEAD_SIZE), spec(2 * HEAD_SIZE)
    return pl.pallas_call(
        functools.partial(attend_back_kernel, blocks),
        grid_spec=pltpu.PrefetchScalarGridSpec(
            num_scalar_prefetch=1,
            grid=(rows, KEY_VALUE_HEADS),
            in_specs=[
                pl.BlockSpec((8, length), lambda r, h, m: (0, r)),
                *[wide] * 3,
                spec(8),
                *[pair] * blocks,
            ],
            out_specs=[wide, *[pair] * blocks],
            scratch_shapes=[
                pltpu.VMEM((GROUP * HEAD_SIZE, length), F32),
                pltpu.VMEM((length, HEAD_SIZE), F32),
                pltpu.VMEM((length, HEAD_SIZE), F32),
            ],
        ),
        out_shape=[
            jax.ShapeDtypeStruct(queries.shape, F32),
            *[jax.ShapeDtypeStruct(pairs[0].shape, BF16)] * blocks,
        ],
        compiler_params=pltpu.CompilerParams(vmem_limit_bytes=48 * 2**20),
        name="attend_back",
    )(me, start, queries, dheads, heads, lse, *pairs)


def places():
    d, s = lax.axis_index("dp"), lax.axis_index("seq")
    core, column, line = d % 2, (d // 2) % 2, d // 4
    return d, s, d + 1 - 2 * core, d + 2 - 4 * column, d + 4 - 8 * line, line


def greet(peers, line=None):
    barrier = pltpu.get_barrier_semaphore()

    def signal(peer):
        pl.semaphore_signal(barrier, inc=1, device_id=peer, device_id_type=MESH)

    for peer in peers:
        signal(peer)
    if line is None:
        pl.semaphore_wait(barrier, len(peers))
        return
    d, s = line
    pl.when(s < 3)(lambda: signal((d, s + 1)))
    pl.when(s > 0)(lambda: signal((d, s - 1)))
    pl.semaphore_wait(barrier, len(peers) + 1 - s // 3 + (s + 2) // 3)


def remote(src, dst, sent, got, peer):
    return pltpu.make_async_remote_copy(
        src_ref=src,
        dst_ref=dst,
        send_sem=sent,
        recv_sem=got,
        device_id=peer,
        device_id_type=MESH,
    )


def weights_kernel(n, *refs):
    x_refs, out_refs = refs[:n], refs[n : 2 * n]
    own_sem, recv, send_z, send_x, send_y, send_d, send_c = refs[2 * n :]
    d, s, d_c, d_x, d_y, line = places()
    d_d = d_x + 4 - 8 * line
    greet([(d_c, s), (d_x, s), (d_y, s)], (d, s))

    def copies(slot, sent, got, peer, own=False):
        return [
            remote(
                x_refs[i] if own else out_refs[i].at[slot],
                out_refs[i].at[slot],
                sent(i),
                got(i),
                peer,
            )
            for i in range(n)
        ]

    def start(group):
        for one in group:
            one.start()

    def sent(group):
        for one in group:
            one.wait_send()

    def each(visit):
        visit(s, 0)
        for far in (1, 2, 3):
            pl.when(s >= far)(lambda far=far: visit(s - far, 1))
            pl.when(s + far <= 3)(lambda far=far: visit(s + far, -1))

    def got(k, b):
        return lambda i: recv.at[i, k, b]

    def arrived(k, b):
        for one in copies(d * 4 + b, lambda i: send_x.at[i, b], got(k, b), (d_x, s)):
            one.wait_recv()

    own = [
        pltpu.make_async_copy(x_refs[i], out_refs[i].at[d * 4 + s], own_sem.at[i])
        for i in range(n)
    ]
    start(own)

    def up(b, own=False):
        return copies(d * 4 + b, lambda i: send_z.at[i, 0, b], got(0, b), (d, s + 1), own)

    def down(b, own=False):
        return copies(d * 4 + b, lambda i: send_z.at[i, 1, b], got(0, b), (d, s - 1), own)

    def spread(b, own=False):
        return (
            copies(d * 4 + b, lambda i: send_x.at[i, b], got(2, b), (d_x, s), own)
            + copies(d * 4 + b, lambda i: send_y.at[i, b], got(4, b), (d_y, s), own)
            + copies(d * 4 + b, lambda i: send_c.at[i, 0, b], got(1, b), (d_c, s), own)
        )

    def column_block(b, direction):
        own = direction == 0
        if direction:
            arrived(0, b)
        if direction >= 0:
            pl.when(s < 3)(lambda: start(up(b, own)))
        if direction <= 0:
            pl.when(s > 0)(lambda: start(down(b, own)))
        start(spread(b, own))

    each(column_block)

    def over_y(b):
        return copies(d_x * 4 + b, lambda i: send_d.at[i, b], got(6, b), (d_y, s))

    def over_x(b):
        return copies(d_y * 4 + b, lambda i: send_d.at[i, b], got(6, b), (d_x, s))

    def to_core(index, holder, b):
        return copies(
            holder * 4 + b, lambda i: send_c.at[i, index, b], got(2 * index + 1, b), (d_c, s)
        )

    def side_blocks(b, direction):
        arrived(2, b)
        pl.when(b % 2 == 0)(lambda: start(over_y(b)))
        start(to_core(1, d_x, b))
        arrived(4, b)
        pl.when(b % 2 == 1)(lambda: start(over_x(b)))
        start(to_core(2, d_y, b))

    each(side_blocks)

    def far_block(b, direction):
        arrived(6, b)
        start(to_core(3, d_d, b))

    each(far_block)

    def finish(b, direction):
        for k in (1, 3, 5, 7):
            arrived(k, b)
        if direction >= 0:
            pl.when(s < 3)(lambda: sent(up(b)))
        if direction <= 0:
            pl.when(s > 0)(lambda: sent(down(b)))
        sent(spread(b))
        sent(over_y(b))
        sent(to_core(1, d_x, b))
        sent(to_core(2, d_y, b))
        sent(to_core(3, d_d, b))

    each(finish)
    for one in own:
        one.wait()


def gather_weights(arrays, n_dp, n_seq):
    if (n_dp, n_seq) != (8, 4):
        return [lax.all_gather(x, BOTH, axis=0, tiled=False) for x in arrays]
    n = len(arrays)
    dma = pltpu.SemaphoreType.DMA
    return pl.pallas_call(
        functools.partial(weights_kernel, n),
        out_shape=[jax.ShapeDtypeStruct((n_dp * n_seq, *x.shape), x.dtype) for x in arrays],
        in_specs=[pl.BlockSpec(memory_space=pl.ANY)] * n,
        out_specs=[pl.BlockSpec(memory_space=pl.ANY)] * n,
        scratch_shapes=[
            dma((n,)),
            dma((n, 8, 4)),
            dma((n, 2, 4)),
            dma((n, 4)),
            dma((n, 4)),
            dma((n, 4)),
            dma((n, 4, 4)),
        ],
        compiler_params=pltpu.CompilerParams(collective_id=1, has_side_effects=True),
        name="gather_weights",
    )(*arrays)


def sum_weights_kernel(g_ref, out_ref, kept, rcv_c, rcv_d, rcv_x, rcv_y, rcv_z, *sems):
    load, sent_c, got_c, sent_p, got_p, sent_z, got_z = sems
    d, s, d_c, d_x, d_y, line = places()
    d_d = d_x + 4 - 8 * line
    holders = (d, d_x, d_y, d_d)
    greet([(d_c, s), (d_x, s), (d_y, s)], (d, s))
    swapped = d_c - d
    loads, crossing = [], []
    for i in (3, 1, 2, 0):
        one = remote(
            g_ref.at[pl.ds((holders[i] + swapped) * 4, 4)],
            rcv_c.at[i],
            sent_c.at[i],
            got_c.at[i],
            (d_c, s),
        )
        one.start()
        crossing.append(one)
        one = pltpu.make_async_copy(
            g_ref.at[pl.ds(holders[i] * 4, 4)], kept.at[i], load.at[i]
        )
        one.start()
        loads.append(one)

    def plus(ref, *others):
        total = ref[...].astype(F32)
        for other in others:
            total += other[...].astype(F32)
        ref[...] = total.astype(BF16)

    def merge(turn, i):
        loads[turn].wait()
        crossing[turn].wait_recv()
        plus(kept.at[i], rcv_c.at[i])

    low, high = pl.ds(0, 2), pl.ds(2, 2)

    def pushed(src, dst, n, peer):
        one = remote(src, dst, sent_p.at[n], got_p.at[n], (peer, s))
        one.start()
        return one

    merge(0, 3)
    far_x = pushed(kept.at[3, low], rcv_d.at[low], 0, d_x)
    far_y = pushed(kept.at[3, high], rcv_d.at[high], 1, d_y)
    merge(1, 1)
    x_low = pushed(kept.at[1, low], rcv_x.at[low], 2, d_x)
    merge(2, 2)
    y_high = pushed(kept.at[2, high], rcv_y.at[high], 3, d_y)
    merge(3, 0)
    far_x.wait_recv()
    plus(kept.at[2, low], rcv_d.at[low])
    y_low = pushed(kept.at[2, low], rcv_y.at[low], 4, d_y)
    far_y.wait_recv()
    plus(kept.at[1, high], rcv_d.at[high])
    x_high = pushed(kept.at[1, high], rcv_x.at[high], 5, d_x)
    x_low.wait_recv()
    y_low.wait_recv()
    plus(kept.at[0, low], rcv_x.at[low], rcv_y.at[low])
    x_high.wait_recv()
    y_high.wait_recv()
    plus(kept.at[0, high], rcv_x.at[high], rcv_y.at[high])

    def up(b):
        return remote(
            kept.at[0, b], rcv_z.at[0, b], sent_z.at[0, b], got_z.at[0, b], (d, s + 1)
        )

    def down(b):
        return remote(
            kept.at[0, b], rcv_z.at[1, b], sent_z.at[1, b], got_z.at[1, b], (d, s - 1)
        )

    def send_up(b):
        @pl.when(s > 0)
        def _():
            up(b).wait_recv()
            plus(kept.at[0, b], rcv_z.at[0, b])

        up(b).start()

    def send_down(b):
        @pl.when(s < 3)
        def _():
            down(b).wait_recv()
            plus(kept.at[0, b], rcv_z.at[1, b])

        down(b).start()

    for b in (3, 2, 1):
        pl.when(s < b)(functools.partial(send_up, b))
        pl.when(s > 3 - b)(functools.partial(send_down, 3 - b))
    out_ref[...] = kept[0, s].astype(F32)

    @pl.when(s > 0)
    def _():
        up(s).wait_recv()
        out_ref[...] += rcv_z[0, s].astype(F32)

    @pl.when(s < 3)
    def _():
        down(s).wait_recv()
        out_ref[...] += rcv_z[1, s].astype(F32)

    for b in (3, 2, 1):
        pl.when(s < b)(lambda b=b: up(b).wait_send())
        pl.when(s > 3 - b)(lambda b=b: down(3 - b).wait_send())
    for one in crossing + [far_x, far_y, x_low, y_high, y_low, x_high]:
        one.wait_send()


def sum_weights(g, n_dp, n_seq, number):
    if (n_dp, n_seq) != (8, 4):
        flat = g.reshape(-1, g.shape[2])
        return scatter(scatter(flat, "dp"), "seq").astype(F32)
    _, rows, columns = g.shape
    dma = pltpu.SemaphoreType.DMA
    buffer = lambda *lead: pltpu.VMEM((*lead, rows, columns), BF16)
    return pl.pallas_call(
        sum_weights_kernel,
        out_shape=jax.ShapeDtypeStruct((rows, columns), F32),
        in_specs=[pl.BlockSpec(memory_space=pl.ANY)],
        out_specs=pl.BlockSpec(memory_space=pltpu.VMEM),
        scratch_shapes=[
            buffer(4, 4),
            buffer(4, 4),
            buffer(4),
            buffer(4),
            buffer(4),
            buffer(2, 4),
            dma((4,)),
            dma((4,)),
            dma((4,)),
            dma((6,)),
            dma((6,)),
            dma((2, 4)),
            dma((2, 4)),
        ],
        compiler_params=pltpu.CompilerParams(
            collective_id=number, has_side_effects=True, vmem_limit_bytes=40 * 2**20
        ),
        name="sum_weights",
    )(g)


def plane_kernel(x_ref, out_ref, own_sem, sent, got):
    d, s, d_c, d_x, d_y, line = places()
    greet([(d_c, s), (d_x, s), (d_y, s)])
    half = x_ref.shape[0] // 2
    halves = (pl.ds(0, half), pl.ds(half, half))

    def piece(k, h, peer, first=False):
        source = {1: 0, 2: 0, 4: 0, 3: 2, 5: 4, 7: 6}
        back = source[k] if k in source else (4 if h == 0 else 2)
        src = x_ref.at[halves[h]] if back == 0 else out_ref.at[back, halves[h]]
        return remote(src, out_ref.at[k, halves[h]], sent.at[k, h], got.at[k, h], (peer, s))

    own = pltpu.make_async_copy(x_ref, out_ref.at[0], own_sem)
    own.start()
    to = {1: d_c, 2: d_x, 4: d_y, 3: d_c, 5: d_c, 7: d_c}
    for h in (0, 1):
        for k in (2, 4, 1):
            piece(k, h, to[k]).start()
    piece(4, 0, d_y).wait_recv()
    piece(6, 0, d_x).start()
    piece(5, 0, d_c).start()
    piece(2, 0, d_x).wait_recv()
    piece(3, 0, d_c).start()
    piece(2, 1, d_x).wait_recv()
    piece(6, 1, d_y).start()
    piece(3, 1, d_c).start()
    piece(4, 1, d_y).wait_recv()
    piece(5, 1, d_c).start()
    piece(6, 0, d_x).wait_recv()
    piece(7, 0, d_c).start()
    piece(6, 1, d_y).wait_recv()
    piece(7, 1, d_c).start()
    for k in (1, 3, 5, 7):
        for h in (0, 1):
            piece(k, h, d_c).wait_recv()
    for k in range(1, 8):
        for h in (0, 1):
            piece(k, h, d_c).wait_send()
    own.wait()


def plane_gather_now(x, n_dp, n_seq):
    if (n_dp, n_seq) != (8, 4):
        return lax.all_gather(x, "dp", axis=0, tiled=True)
    dma = pltpu.SemaphoreType.DMA
    return pl.pallas_call(
        plane_kernel,
        out_shape=jax.ShapeDtypeStruct((n_dp, *x.shape), x.dtype),
        in_specs=[pl.BlockSpec(memory_space=pl.ANY)],
        out_specs=pl.BlockSpec(memory_space=pl.ANY),
        scratch_shapes=[dma, dma((8, 2)), dma((8, 2))],
        compiler_params=pltpu.CompilerParams(collective_id=4, has_side_effects=True),
        name="plane_gather",
    )(x).reshape(n_dp * x.shape[0], x.shape[1])


def plane_sum_kernel(
    g_ref, w_ref, x_ref, out_ref, grad_ref, w_v, g_v, kept, leaving, rcv_c, rcv_d, rcv_x, rcv_y,
    acc, w_sem, g_sem, sent_c, got_c, sent_p, got_p, out_sem,
):
    d, s, d_c, d_x, d_y, line = places()
    rows, deep = g_v.shape[1], g_v.shape[2]
    width = w_v.shape[0]
    order = (7, 6, 3, 2, 5, 4, 1, 0)
    w_load = pltpu.make_async_copy(w_ref, w_v, w_sem)
    w_load.start()

    def g_load(turn):
        return pltpu.make_async_copy(
            g_ref.at[pl.ds(order[turn] * rows, rows)], g_v.at[turn % 2], g_sem.at[turn % 2]
        )

    g_load(0).start()
    greet([(d_c, s), (d_x, s), (d_y, s)])
    w_load.wait()
    chunk = 512

    def product(turn, dst):
        if turn + 1 < 8:
            g_load(turn + 1).start()
        g_load(turn).wait()

        @pl.loop(0, width // chunk)
        def _(c):
            span = pl.ds(pl.multiple_of(c * chunk, chunk), chunk)
            dst[:, span] = back_product(g_v[turn % 2], w_v[span, :]).astype(BF16)

    def plus(ref, *others):
        total = ref[...].astype(F32)
        for other in others:
            total += other[...].astype(F32)
        ref[...] = total.astype(BF16)

    def crossing(i):
        return remote(leaving.at[i], rcv_c.at[i], sent_c.at[i], got_c.at[i], (d_c, s))

    def pair(turn, i):
        product(turn, leaving.at[i])
        crossing(i).start()
        product(turn + 1, kept.at[i])

    def merge(i):
        crossing(i).wait_recv()
        plus(kept.at[i], rcv_c.at[i])

    low, high = pl.ds(0, rows // 2), pl.ds(rows // 2, rows // 2)

    def pushed(src, dst, n, peer):
        one = remote(src, dst, sent_p.at[n], got_p.at[n], (peer, s))
        one.start()
        return one

    pair(0, 3)
    pair(2, 1)
    merge(3)
    far_x = pushed(kept.at[3, low], rcv_d.at[low], 0, d_x)
    far_y = pushed(kept.at[3, high], rcv_d.at[high], 1, d_y)
    pair(4, 2)
    merge(1)
    x_low = pushed(kept.at[1, low], rcv_x.at[low], 2, d_x)
    pair(6, 0)
    merge(2)
    y_high = pushed(kept.at[2, high], rcv_y.at[high], 3, d_y)
    merge(0)

    tokens = g_ref.shape[0]
    depth, tall = 1024, 512

    def grad_body(x_tile, g_tile, grad_tile):
        k = pl.program_id(1)
        term = outer_sum(x_tile[...], g_tile[...])

        @pl.when(k == 0)
        def _():
            acc[...] = term

        @pl.when(k > 0)
        def _():
            acc[...] += term

        @pl.when(k == tokens // depth - 1)
        def _():
            grad_tile[...] = acc[...].astype(BF16)

    def grad_tiles(first, count):
        pltpu.emit_pipeline(
            grad_body,
            grid=(count, tokens // depth),
            in_specs=[
                pl.BlockSpec((depth, tall), lambda i, k: (k, first + i)),
                pl.BlockSpec((depth, deep), lambda i, k: (k, 0)),
            ],
            out_specs=[pl.BlockSpec((tall, deep), lambda i, k: (first + i, 0))],
        )(x_ref, g_ref, grad_ref)

    grad_tiles(0, 1)
    far_x.wait_recv()
    plus(kept.at[2, low], rcv_d.at[low])
    y_low = pushed(kept.at[2, low], rcv_y.at[low], 4, d_y)
    far_y.wait_recv()
    plus(kept.at[1, high], rcv_d.at[high])
    x_high = pushed(kept.at[1, high], rcv_x.at[high], 5, d_x)
    grad_tiles(1, width // tall - 1)
    x_low.wait_recv()
    y_low.wait_recv()
    x_high.wait_recv()
    y_high.wait_recv()
    plus(kept.at[0], rcv_x, rcv_y)
    out = pltpu.make_async_copy(kept.at[0], out_ref, out_sem)
    out.start()
    for one in [far_x, far_y, x_low, y_high, y_low, x_high] + [crossing(i) for i in range(4)]:
        one.wait_send()
    out.wait()


def plane_sum(g, w, x, rows):
    dma = pltpu.SemaphoreType.DMA
    width, deep = w.shape
    buffer = lambda *lead: pltpu.VMEM((*lead, width), BF16)
    return pl.pallas_call(
        plane_sum_kernel,
        out_shape=[
            jax.ShapeDtypeStruct((rows, width), BF16),
            jax.ShapeDtypeStruct((width, deep), BF16),
        ],
        in_specs=[pl.BlockSpec(memory_space=pl.ANY)] * 3,
        out_specs=[pl.BlockSpec(memory_space=pl.ANY)] * 2,
        scratch_shapes=[
            pltpu.VMEM((width, deep), BF16),
            pltpu.VMEM((2, rows, deep), BF16),
            buffer(4, rows),
            buffer(4, rows),
            buffer(4, rows),
            buffer(rows),
            buffer(rows),
            buffer(rows),
            pltpu.VMEM((512, deep), F32),
            dma,
            dma((2,)),
            dma((4,)),
            dma((4,)),
            dma((6,)),
            dma((6,)),
            dma,
        ],
        compiler_params=pltpu.CompilerParams(
            collective_id=5, has_side_effects=True, vmem_limit_bytes=62 * 2**20
        ),
        name="plane_sum",
    )(g, w, x)


def swap(x, mask, size):
    return lax.ppermute(x, "dp", [(i, i ^ mask) for i in range(size)])


def plane_gather(x, n_dp):
    if n_dp != 8:
        return lax.all_gather(x, "dp", axis=0, tiled=True)
    half = x.shape[0] // 2
    b1, b2, b4 = swap(x, 1, 8), swap(x, 2, 8), swap(x, 4, 8)
    b6 = jnp.concatenate([swap(b4[:half], 2, 8), swap(b2[half:], 4, 8)], axis=0)
    b3, b5, b7 = swap(b2, 1, 8), swap(b4, 1, 8), swap(b6, 1, 8)
    return jnp.concatenate([x, b1, b2, b3, b4, b5, b6, b7], axis=0)


def add(a, b):
    return (a.astype(F32) + b.astype(F32)).astype(BF16)


def plane_scatter(make, rows, n_dp):
    if n_dp != 8:
        return lax.psum_scatter(make(0, n_dp), "dp", scatter_dimension=0, tiled=True).astype(F32)
    half = rows // 2
    kept = {}
    for c in (6, 2, 4, 0):
        part = make(c, c + 2)
        kept[c] = add(part[:rows], swap(part[rows:], 1, 8))
    from_x = swap(kept[6][:half], 2, 8)
    from_y = swap(kept[6][half:], 4, 8)
    x_first = swap(kept[2][:half], 2, 8)
    y_last = swap(kept[4][half:], 4, 8)
    x_last = swap(add(kept[2][half:], from_y), 2, 8)
    y_first = swap(add(kept[4][:half], from_x), 4, 8)
    first = kept[0][:half].astype(F32) + x_first.astype(F32) + y_first.astype(F32)
    last = kept[0][half:].astype(F32) + x_last.astype(F32) + y_last.astype(F32)
    return jnp.concatenate([first, last], axis=0)


def sigmoid(v):
    return 1.0 / (1.0 + jnp.exp(-v))


def gate_up_kernel(x_ref, w_ref, gu_ref, hidden_ref):
    part = hidden_ref.shape[1]
    step = 256 if part % 256 == 0 else 128
    for c in range(0, part, step):
        gate = dot(x_ref[...], w_ref[:, c : c + step])
        up = dot(x_ref[...], w_ref[:, part + c : part + c + step])
        gu_ref[:, c : c + step] = gate.astype(BF16)
        gu_ref[:, part + c : part + c + step] = up.astype(BF16)
        hidden_ref[:, c : c + step] = (gate * sigmoid(gate) * up).astype(BF16)


def gate_up_product(x, w):
    tokens, width = x.shape
    wide = w.shape[1]
    block = 512
    return pl.pallas_call(
        gate_up_kernel,
        grid=(tokens // block,),
        in_specs=[
            pl.BlockSpec((block, width), lambda i: (i, 0)),
            pl.BlockSpec((width, wide), lambda i: (0, 0)),
        ],
        out_specs=[
            pl.BlockSpec((block, wide), lambda i: (i, 0)),
            pl.BlockSpec((block, wide // 2), lambda i: (i, 0)),
        ],
        out_shape=[
            jax.ShapeDtypeStruct((tokens, wide), BF16),
            jax.ShapeDtypeStruct((tokens, wide // 2), BF16),
        ],
        compiler_params=pltpu.CompilerParams(vmem_limit_bytes=56 * 2**20),
        cost_estimate=pl.CostEstimate(
            flops=2 * tokens * width * wide,
            bytes_accessed=2 * (tokens * width + width * wide + tokens * wide * 3 // 2),
            transcendentals=tokens * wide // 2,
        ),
        name="gate_up",
    )(x, w)


def gate_up_back_kernel(g_ref, w_ref, gu_ref, out_ref):
    part = w_ref.shape[0]
    step = 256 if part % 256 == 0 else 128
    for c in range(0, part, step):
        dhidden = back_product(g_ref[...], w_ref[c : c + step, :])
        gate = gu_ref[:, c : c + step].astype(F32)
        up = gu_ref[:, part + c : part + c + step].astype(F32)
        sig = sigmoid(gate)
        rest = dhidden * sig
        out_ref[:, c : c + step] = (rest * up * (1.0 + gate * (1.0 - sig))).astype(BF16)
        out_ref[:, part + c : part + c + step] = (rest * gate).astype(BF16)


def gate_up_back(g, w, gu):
    tokens, width = g.shape
    wide = gu.shape[1]
    block = 512
    return pl.pallas_call(
        gate_up_back_kernel,
        grid=(tokens // block,),
        in_specs=[
            pl.BlockSpec((block, width), lambda i: (i, 0)),
            pl.BlockSpec(w.shape, lambda i: (0, 0)),
            pl.BlockSpec((block, wide), lambda i: (i, 0)),
        ],
        out_specs=pl.BlockSpec((block, wide), lambda i: (i, 0)),
        out_shape=jax.ShapeDtypeStruct((tokens, wide), BF16),
        compiler_params=pltpu.CompilerParams(vmem_limit_bytes=56 * 2**20),
        cost_estimate=pl.CostEstimate(
            flops=tokens * width * wide,
            bytes_accessed=2 * (tokens * width + width * wide // 2 + tokens * wide * 2),
            transcendentals=tokens * wide // 2,
        ),
        name="gate_up_back",
    )(g, w, gu)


def shift(x, by, size):
    pairs = [(i, i + by) for i in range(size) if 0 <= i + by < size]
    return lax.ppermute(x, "seq", pairs)


def mm(a, b):
    return jnp.dot(a, b, preferred_element_type=F32)


def outer_sum(left, right):
    return lax.dot_general(left, right, (((0,), (0,)), ((), ())), preferred_element_type=F32)


def back_product(rows, weight):
    return lax.dot_general(rows, weight, (((1,), (1,)), ((), ())), preferred_element_type=F32)


def gather(x, axes):
    return lax.all_gather(x, axes, axis=0, tiled=True)


def scatter(x, axes):
    return lax.psum_scatter(x, axes, scatter_dimension=0, tiled=True)


def shards(
    tokens, lengths, w_qkv, w_out, w_gate_up, w_down, attn_gain, ffn_gain, head_gains, out_grad
):
    n_dp, n_seq = lax.axis_size("dp"), lax.axis_size("seq")
    rows, length, width = tokens.shape
    count = rows * length
    ff = w_gate_up.shape[1] // 2
    part = ff // n_dp
    wr = w_gate_up.shape[0]
    me = lax.axis_index("seq")
    offset = me * length
    me = me.reshape(1).astype(jnp.int32)
    local_pos = offset + jnp.arange(length, dtype=jnp.int32)
    cosine, sine = rope_tables(jnp.concatenate([local_pos] * rows))
    ends = jnp.cumsum(lengths, axis=1, dtype=jnp.int32)
    start = jnp.sum(
        jnp.where(local_pos[None, :, None] >= ends[:, None, :], lengths[:, None, :], 0), axis=2
    ).reshape(1, count)
    start = jnp.broadcast_to(start, (8, count))

    out_rows = w_out.shape[0]
    gains = jnp.concatenate([attn_gain, ffn_gain, head_gains])
    gains = jnp.pad(gains, (0, width - gains.shape[0]))[None]
    fill = -(out_rows + 1) % 16
    own_rest = jnp.concatenate([w_out, gains, jnp.zeros((fill, width), BF16)], axis=0)
    qkv_w = w_qkv.shape[1]
    paired = w_qkv[:, QW:].reshape(wr, 2, KEY_VALUE_HEADS, HEAD_SIZE).transpose(0, 2, 1, 3)
    own_qkv = jnp.concatenate([w_qkv[:, :QW], paired.reshape(wr, 2 * KW)], axis=1)
    all_qkv, all_rest = gather_weights([own_qkv, own_rest], n_dp, n_seq)
    qkv_full = all_qkv.reshape(width, qkv_w)
    out_full = all_rest[:, :out_rows].reshape(QW, width)
    gains = all_rest[:, out_rows]
    attn_gain_full = gains[:, :wr].reshape(-1).astype(F32)
    ffn_gain_full = gains[:, wr : 2 * wr].reshape(-1).astype(F32)
    head_full = gains[:, 2 * wr : 2 * wr + head_gains.shape[0]].reshape(-1).astype(F32)

    down_w = gather(w_down, "seq")
    w_gate_up, qkv_full = lax.optimization_barrier((w_gate_up, qkv_full))
    spread = lax.all_to_all(w_gate_up.reshape(wr, 2, n_dp, part), "dp", 2, 0, tiled=False)
    spread = spread.reshape(n_dp * wr, 2 * part)
    cotangent_low = out_grad.reshape(count, width)
    cotangent_low, qkv_full = lax.optimization_barrier((cotangent_low, qkv_full))
    cotangent_all = plane_gather(cotangent_low, n_dp)

    x_rows = tokens.reshape(count, width).astype(F32)
    normed, norm_pull = jax.vjp(norm_rows, x_rows, attn_gain_full)
    normed_low = normed.astype(BF16)
    projected = lax.dot_general(
        qkv_full, normed_low, (((0,), (1,)), ((), ())), preferred_element_type=F32
    )

    def prep_local(projected_in, gain_vec):
        return prepare(projected_in, gain_vec, cosine, sine)

    (queries, pairs), prep_pull = jax.vjp(prep_local, projected, head_full)
    queries = queries.astype(BF16)
    pairs = [pairs.astype(BF16)]
    for _ in range(n_seq - 1):
        pairs.append(shift(pairs[-1], 1, n_seq))
    spread, pairs[-1] = lax.optimization_barrier((spread, pairs[-1]))
    gate_up_w = gather(spread, "seq").reshape(n_seq, n_dp, wr, 2 * part)
    gate_up_w = gate_up_w.transpose(1, 0, 2, 3).reshape(width, 2 * part)
    heads_out, lse = attend(me, start, queries, pairs, rows)
    middle = x_rows + outer_sum(heads_out, out_full)
    normed2, norm2_pull = jax.vjp(norm_rows, middle, ffn_gain_full)
    normed2_all = plane_gather_now(normed2.astype(BF16), n_dp, n_seq)
    gate_up, hidden = gate_up_product(normed2_all, gate_up_w)
    down_grad = outer_sum(hidden, cotangent_all).astype(BF16)
    gate_up, down_grad = lax.optimization_barrier((gate_up, down_grad))
    down_grad = scatter(down_grad, "seq")
    dgate_up = gate_up_back(cotangent_all, down_w, gate_up)
    if (n_dp, n_seq) == (8, 4):
        dnormed2, gate_up_grad = plane_sum(dgate_up, gate_up_w, normed2_all, count)
    else:
        dnormed2 = scatter(back_product(dgate_up, gate_up_w).astype(BF16), "dp")
        gate_up_grad = outer_sum(normed2_all, dgate_up).astype(BF16)
    dnormed2 = dnormed2.astype(F32)
    gate_up_grad = gate_up_grad.reshape(n_dp, n_seq, wr, 2 * part).transpose(1, 0, 2, 3)
    gate_up_grad = gate_up_grad.reshape(width, 2 * part)
    gate_up_grad, dnormed2 = lax.optimization_barrier((gate_up_grad, dnormed2))
    gate_up_grad = scatter(gate_up_grad, "seq")
    gate_up_grad = lax.all_to_all(
        gate_up_grad.reshape(n_dp, wr, 2, part), "dp", 0, 2, tiled=False
    ).reshape(wr, 2 * ff)
    hidden, dnormed2 = lax.optimization_barrier((hidden, dnormed2))

    def mixed_part(first, last):
        return mm(hidden[first * count : last * count], down_w).astype(BF16)

    mixed = middle + plane_scatter(mixed_part, count, n_dp)

    dmiddle_norm, ffn_gain_grad = norm2_pull(dnormed2)
    dmiddle = cotangent_low.astype(F32) + dmiddle_norm
    dattend = dmiddle.astype(BF16)
    out_weight_grad = mm(heads_out, dattend).astype(BF16).reshape(n_dp * n_seq, out_rows, width)
    out_weight_grad = jnp.pad(out_weight_grad, ((0, 0), (0, -out_rows % 16), (0, 0)))
    out_weight_grad = sum_weights(out_weight_grad, n_dp, n_seq, 6)[:out_rows]
    dheads = back_product(out_full, dattend).astype(BF16)
    dqueries, *dpairs = attend_back(me, start, queries, pairs, dheads, heads_out, lse, rows)
    dpair = dpairs[-1]
    for back in range(n_seq - 2, -1, -1):
        dpair = dpairs[back].astype(F32) + shift(dpair, -1, n_seq).astype(F32)
        if back:
            dpair = dpair.astype(BF16)
    dprojected, head_grad = prep_pull((dqueries, dpair))
    dprojected_low = dprojected.astype(BF16)
    qkv_grad = lax.dot_general(
        normed_low, dprojected_low, (((0,), (1,)), ((), ())), preferred_element_type=F32
    ).astype(BF16)
    qkv_grad = sum_weights(qkv_grad.reshape(n_dp * n_seq, wr, qkv_w), n_dp, n_seq, 7)
    unpaired = qkv_grad[:, QW:].reshape(wr, KEY_VALUE_HEADS, 2, HEAD_SIZE).transpose(0, 2, 1, 3)
    qkv_grad = jnp.concatenate([qkv_grad[:, :QW], unpaired.reshape(wr, 2 * KW)], axis=1)
    dnormed = lax.dot_general(
        dprojected_low, qkv_full, (((0,), (1,)), ((), ())), preferred_element_type=F32
    )
    dx_norm, attn_gain_grad = norm_pull(dnormed)
    tokens_grad = dmiddle + dx_norm

    n_all = n_dp * n_seq
    small = jnp.concatenate(
        [
            attn_gain_grad.reshape(n_all, -1),
            ffn_gain_grad.reshape(n_all, -1),
            head_grad.reshape(n_all, -1),
        ],
        axis=1,
    )
    small = jnp.sum(lax.all_to_all(small, BOTH, 0, 0, tiled=False), axis=0)
    attn_gain_out = small[:wr]
    ffn_gain_out = small[wr : 2 * wr]
    head_out = small[2 * wr :]
    return (
        mixed.astype(BF16).reshape(rows, length, width),
        tokens_grad.reshape(rows, length, width),
        qkv_grad,
        out_weight_grad,
        gate_up_grad.astype(F32),
        down_grad.astype(F32),
        attn_gain_out,
        ffn_gain_out,
        head_out,
    )


def solution(mesh):
    in_specs = (
        P("dp", "seq", None),
        P("dp", None),
        P(("dp", "seq"), None),
        P(("dp", "seq"), None),
        P(("dp", "seq"), None),
        P(("dp", "seq"), None),
        P(("dp", "seq")),
        P(("dp", "seq")),
        P(("dp", "seq")),
        P("dp", "seq", None),
    )
    out_specs = (
        P("dp", "seq", None),
        P("dp", "seq", None),
        P(("dp", "seq"), None),
        P(("dp", "seq"), None),
        P(("dp", "seq"), None),
        P(("dp", "seq"), None),
        P(("dp", "seq")),
        P(("dp", "seq")),
        P(("dp", "seq")),
    )
    return jax.shard_map(shards, mesh=mesh, in_specs=in_specs, out_specs=out_specs, check_vma=False)
```

time: 1520 us -> 945 us (0.62)
  waiting for transfers between devices: 961 us -> 205 us
  Pallas kernels: 0 us -> 451 us
  matrix products: 326 us -> 80.8 us
  other arithmetic: 85.5 us -> 52.7 us
  starting transfers between devices: 12.5 us -> 39.3 us
  local copies, waits for them, and re-layouts: 114 us -> 91.7 us
    reduce_scatter x8 -> x2, waiting for transfers between devices: 523 us -> 0.01 us  [scatter(): return lax.psum_scatter(x, axes, scatter_dimension=0, tiled=True)]
    pallas_call x0 -> x9, Pallas kernels: none -> 451 us  [the longest x2 132 us: sum_weights(): pl.pallas_call(sum_weights_kernel, out_shape=jax.ShapeDtypeStruct((rows,...]
    all_gather x7 -> x2, waiting for transfers between devices: 416 us -> 0.01 us  [gather(): return lax.all_gather(x, axes, axis=0, tiled=True)]
    ppermute x0 -> x24, waiting for transfers between devices: none -> 204 us  [the longest x6 117 us: shift(): return lax.ppermute(x, 'seq', pairs)]
    dot_general x4 -> x1, matrix products: 79.4 us -> 4.05 us  [back_product(): lax.dot_general(rows, weight, (((1,), (1,)), ((), ())), preferred_element...]
    dot_general x5 -> x3, matrix products: 80.8 us -> 27.8 us  [the longest x1 10.5 us: shards(): lax.dot_general(normed_low, dprojected_low, (((0,), (1,)), ((), ())), pre...]
    dot_general x4 -> x2, matrix products: 73.4 us -> 23.2 us  [outer_sum(): lax.dot_general(left, right, (((0,), (0,)), ((), ())), preferred_element_...]
    dot_general x4 -> x5, matrix products: 73 us -> 25.7 us  [mm(): return jnp.dot(a, b, preferred_element_type=F32)]
  transfers between devices with their start and end apart: 18 -> 31, of which waited for: 16 -> 11; matrix products, arithmetic and copies ran while one was open for 20% -> 19% of each run, Pallas kernels for 0% -> 28%
where the time goes in v2:
time: 945 us; the launch traced here: 935 us
  Pallas kernels  451 us (48%)
  waiting for transfers between devices  205 us (22%)
  local copies, waits for them, and re-layouts  91.7 us (10%)
  matrix products  80.8 us (9%)
  other arithmetic  52.7 us (6%)
  starting transfers between devices  39.3 us (4%)
  between operations  15.3 us (2%)
    pallas_call x2, Pallas kernels, sum_weights(): pl.pallas_call(sum_weights_kernel, out_shape=jax.ShapeDtypeStruct((rows,...  132 us
    ppermute x6, waiting for transfers between devices, shift(): return lax.ppermute(x, 'seq', pairs)  117 us
    pallas_call x1, Pallas kernels, plane_sum(): pl.pallas_call(plane_sum_kernel, out_shape=[jax.ShapeDtypeStruct((rows, w...  92.2 us
    ppermute x18, waiting for transfers between devices, swap(): return lax.ppermute(x, 'dp', [(i, i ^ mask) for i in range(size)])  87.2 us
    pallas_call x1, Pallas kernels, plane_gather_now(): pl.pallas_call(plane_kernel, out_shape=jax.ShapeDtypeStruct((n_dp, *x.sha...  75.3 us
    pallas_call x1, Pallas kernels, gather_weights(): pl.pallas_call(functools.partial(weights_kernel, n), out_shape=[jax.Shape...  68.9 us
    unnamed x140, local copies, waits for them, and re-layouts  36.9 us
    pallas_call x1, Pallas kernels, gate_up_product(): pl.pallas_call(gate_up_kernel, grid=(tokens // block,), in_specs=[pl.Bloc...  32.9 us
  transfers between devices with their start and end apart: 31, of which 11 were waited for; matrix products, arithmetic and copies ran while one was open for 19% of the time, Pallas kernels for 28%

profile of v2, /device:TPU:0, one launch (start us, length us, event | category | flops | bytes accessed | tf_op | source)
XLA Modules:
  0.0 935.2 jit_solution(12568352224366681482)
XLA Ops:
  12.9 68.9 %gather_weights.1 = (bf16[32,64,1920]{2,1,0:T(8,128)(2,1)}, bf16[32,48,2048]{2,1,0:T(8,128)(2,1)}) custom-call(bf16[64,1920]{1,0:T(8,128)(2,1)} %pad_maximum_fusion.3.refs_0_, bf16[48,2048]{1,0:T(8,128)(2,1)} %maximum_maximum_fusion.refs_1_), custom_call_target="tpu_custom_call" | custom-call | tf_op jit(solution)/shard_map/gather_weights/pallas_call | solution.py:360
  85.2 7.5 fusion.32
  103.5 7.7 collective-permute-done.refs_1_
  115.7 14.0 %collective-permute-done.1.refs_2_ = bf16[640,512]{1,0:T(8,128)(2,1)S(1)} collective-permute-done((bf16[640,512]{1,0:T(8,128)(2,1)S(1)}, bf16[640,512]{1,0:T(8,128)(2,1)S(1)}, u32[]{:S(2)}, u32[]{:S(2)}) %collective-permute-start.1) | collective-permute-done | bytes 655392 | tf_op jit(solution)/shard_map/ppermute | solution.py:856
  136.9 10.3 %collective-permute-done.2.refs_3_ = bf16[640,512]{1,0:T(8,128)(2,1)S(1)} collective-permute-done((bf16[640,512]{1,0:T(8,128)(2,1)S(1)}, bf16[640,512]{1,0:T(8,128)(2,1)S(1)}, u32[]{:S(2)}, u32[]{:S(2)}) %collective-permute-start.2) | collective-permute-done | bytes 655392 | tf_op jit(solution)/shard_map/ppermute | solution.py:856
  166.8 11.1 %attend.1 = (bf16[1280,512]{1,0:T(8,128)(2,1)S(1)}, f32[40,512]{1,0:T(8,128)S(1)}) custom-call(s32[1]{0:T(128)} %bitcast.1.me_ref, s32[8,512]{1,0:T(8,128)S(1)} %broadcast_in_dim.58.start_ref, bf16[1280,512]{1,0:T(8,128)(2,1)S(1)} %bitcast.110, bf16[640,512]{1,0:T(8,128)(2,1)S(1)} %bitcast.114, bf16[640,512]{1,0:T(8,128)(2,1)S(1)} %collective-permute-done.refs_1_, ...), custom_call_target="tpu_custom_call" | custom-call | tf_op jit(solution)/shard_map/attend/pallas_call | solution.py:149
  177.9 15.6 %collective-permute-done.6 = bf16[512,2048]{1,0:T(8,128)(2,1)} collective-permute-done((bf16[512,2048]{1,0:T(8,128)(2,1)}, bf16[512,2048]{1,0:T(8,128)(2,1)}, u32[]{:S(2)}, u32[]{:S(2)}) %collective-permute-start.6) | collective-permute-done | bytes 2097184 | tf_op jit(solution)/shard_map/ppermute | solution.py:737
  202.8 15.0 %collective-permute-done.8 = bf16[256,2048]{1,0:T(8,128)(2,1)S(1)} collective-permute-done((bf16[256,2048]{1,0:T(8,128)(2,1)S(1)}, bf16[256,2048]{1,0:T(8,128)(2,1)S(1)}, u32[]{:S(2)}, u32[]{:S(2)}) %collective-permute-start.8) | collective-permute-done | bytes 1048608 | tf_op jit(solution)/shard_map/ppermute | solution.py:737
  223.8 75.3 %plane_gather.1 = bf16[8,512,2048]{2,1,0:T(8,128)(2,1)} custom-call(bf16[512,2048]{1,0:T(8,128)(2,1)} %multiply_convert_fusion.x_ref), custom_call_target="tpu_custom_call" | custom-call | tf_op jit(solution)/shard_map/plane_gather/pallas_call | solution.py:569
  326.6 32.9 %gate_up.1 = (bf16[4096,1536]{1,0:T(8,128)(2,1)}, bf16[4096,768]{1,0:T(8,128)(2,1)}) custom-call(bf16[4096,2048]{1,0:T(8,128)(2,1)} %bitcast.116, bf16[2048,1536]{1,0:T(8,128)(2,1)} %bitcast.123), custom_call_target="tpu_custom_call" | custom-call | flops 25769803776 | bytes 41943040 | tf_op jit(solution)/shard_map/gate_up/pallas_call | solution.py:792
  359.5 20.0 %convolution_convert_fusion.6 = bf16[768,2048]{1,0:T(8,128)(2,1)} fusion(bf16[4096,768]{1,0:T(8,128)(2,1)} %get-tuple-element.49, bf16[4096,2048]{1,0:T(8,128)(2,1)} %constant_dynamic-update-slice_fusion.g_ref), kind=kOutput, calls=%fused_computation.33 | convolution fusion | flops 12886474752 | bytes 26214400 | tf_op jit(solution)/shard_map/dot_general | solution.py:864
  379.5 23.6 %gate_up_back.1.g_ref = bf16[4096,1536]{1,0:T(8,128)(2,1)} custom-call(bf16[4096,2048]{1,0:T(8,128)(2,1)} %constant_dynamic-update-slice_fusion.g_ref, bf16[768,2048]{1,0:T(8,128)(2,1)} %all-gather.5.cloned.1.call-done.w_ref, bf16[4096,1536]{1,0:T(8,128)(2,1)} %get-tuple-element.45.gu_ref), custom_call_target="tpu_custom_call" | custom-call | flops 12884901888 | bytes 45088768 | tf_op jit(solution)/shard_map/gate_up_back/pallas_call | solution.py:834
  403.1 92.2 %plane_sum.1 = (bf16[512,2048]{1,0:T(8,128)(2,1)}, bf16[2048,1536]{1,0:T(8,128)(2,1)}) custom-call(bf16[4096,1536]{1,0:T(8,128)(2,1)} %gate_up_back.1.g_ref, bf16[2048,1536]{1,0:T(8,128)(2,1)} %bitcast.124, bf16[4096,2048]{1,0:T(8,128)(2,1)} %bitcast.117), custom_call_target="tpu_custom_call" | custom-call | tf_op jit(solution)/shard_map/plane_sum/pallas_call | solution.py:703
  539.0 18.2 %collective-permute-done.16 = bf16[256,2048]{1,0:T(8,128)(2,1)S(1)} collective-permute-done((bf16[256,2048]{1,0:T(8,128)(2,1)S(1)}, bf16[256,2048]{1,0:T(8,128)(2,1)S(1)}, u32[]{:S(2)}, u32[]{:S(2)}) %collective-permute-start.16) | collective-permute-done | bytes 1048608 | tf_op jit(solution)/shard_map/ppermute | solution.py:737
  566.4 14.0 %collective-permute-done.20 = bf16[256,2048]{1,0:T(8,128)(2,1)S(1)} collective-permute-done((bf16[256,2048]{1,0:T(8,128)(2,1)}, bf16[256,2048]{1,0:T(8,128)(2,1)S(1)}, u32[]{:S(2)}, u32[]{:S(2)}) %collective-permute-start.20) | collective-permute-done | bytes 1048608 | tf_op jit(solution)/shard_map/ppermute | solution.py:737
  580.4 21.5 %collective-permute-done.17 = bf16[256,2048]{1,0:T(8,128)(2,1)} collective-permute-done((bf16[256,2048]{1,0:T(8,128)(2,1)}, bf16[256,2048]{1,0:T(8,128)(2,1)}, u32[]{:S(2)}, u32[]{:S(2)}) %collective-permute-start.17) | collective-permute-done | bytes 1048608 | tf_op jit(solution)/shard_map/ppermute | solution.py:737
  614.4 14.5 %attend_back.1 = (f32[1280,512]{1,0:T(8,128)}, bf16[640,512]{1,0:T(8,128)(2,1)S(1)}, bf16[640,512]{1,0:T(8,128)(2,1)S(1)}, bf16[640,512]{1,0:T(8,128)(2,1)S(1)}, bf16[640,512]{1,0:T(8,128)(2,1)S(1)}) custom-call(s32[1]{0:T(128)} %bitcast.1.me_ref, s32[8,512]{1,0:T(8,128)S(1)} %copy-done.11, bf16[1280,512]{1,0:T(8,128)(2,1)} %bitcast.111, ...), custom_call_target="tpu_custom_call" | custom-call | tf_op jit(solution)/shard_map/attend_back/pallas_call | solution.py:178
  632.3 64.1 %collective-permute-done.21 = bf16[640,512]{1,0:T(8,128)(2,1)S(1)} collective-permute-done((bf16[640,512]{1,0:T(8,128)(2,1)S(1)}, bf16[640,512]{1,0:T(8,128)(2,1)S(1)}, u32[]{:S(2)}, u32[]{:S(2)}) %collective-permute-start.21) | collective-permute-done | bytes 655392 | tf_op jit(solution)/shard_map/ppermute | solution.py:856
  703.9 21.1 %collective-permute-done.22 = bf16[640,512]{1,0:T(8,128)(2,1)S(1)} collective-permute-done((bf16[640,512]{1,0:T(8,128)(2,1)S(1)}, bf16[640,512]{1,0:T(8,128)(2,1)S(1)}, u32[]{:S(2)}, u32[]{:S(2)}) %collective-permute-start.22) | collective-permute-done | bytes 655392 | tf_op jit(solution)/shard_map/ppermute | solution.py:856
  731.6 57.4 %sum_weights.3 = f32[48,2048]{1,0:T(8,128)S(1)} custom-call(bf16[32,48,2048]{2,1,0:T(8,128)(2,1)S(1)} %pad.47.g_ref), custom_call_target="tpu_custom_call" | custom-call | tf_op jit(solution)/shard_map/sum_weights/pallas_call | solution.py:497
  795.1 9.9 %fusion.6 = (f32[2048]{0:T(1024)S(1)}, f32[512]{0:T(512)S(1)}, f32[512,2048]{1,0:T(8,128)}) fusion(bf16[2,256,2048]{2,1,0:T(8,128)(2,1)S(1)} %copy-done.21, f32[512]{0:T(512)S(1)} %copy-done.52, f32[2048]{0:T(1024)S(1)} %copy-done.48, bf16[2048,1920]{1,0:T(8,128)(2,1)} %bitcast.165, f32[1280,512]{1,0:T(8,128)S(1)} %bitcast.150, f32[640,512]{1,0:T(8,128)S(1)} %bitcast.154), kind=kOutput, calls=%fused_computation.16 | convolution fusion | flops 4035835392 | bytes 18108416 | tf_op jit(solution)/shard_map/dot_general | solution.py:991
  809.0 10.5 %convolution_convert_fusion.1 = bf16[2048,1920]{1,0:T(8,128)(2,1)} fusion(bf16[512,2048]{1,0:T(8,128)(2,1)} %copy-done.32, f32[1280,512]{1,0:T(8,128)} %bitcast.151, f32[640,512]{1,0:T(8,128)} %bitcast.155), kind=kOutput, calls=%fused_computation.1 | convolution fusion | flops 4032430080 | bytes 13893632 | tf_op jit(solution)/shard_map/dot_general | solution.py:985
  831.7 75.0 %sum_weights.2 = f32[64,1920]{1,0:T(8,128)S(1)} custom-call(bf16[32,64,1920]{2,1,0:T(8,128)(2,1)S(1)} %bitcast.112), custom_call_target="tpu_custom_call" | custom-call | tf_op jit(solution)/shard_map/sum_weights/pallas_call | solution.py:497
  908.1 6.5 fusion.1
  (313 shorter events, 213.2 us)
Async XLA Ops:
  99.2 34.9 %all-to-all-start = ((bf16[1,64,2,8,768]{4,2,1,0,3:T(2,128)(2,1)}), bf16[1,64,2,8,768]{4,2,1,0,3:T(2,128)(2,1)}, u32[]{:S(2)}, u32[]{:S(2)}) async-start(bf16[1,64,2,8,768]{4,2,1,0,3:T(2,128)(2,1)} %copy.77), calls=%async_computation | async-start | bytes 3145728 | tf_op jit(solution)/shard_map/all_to_all | solution.py:917
  103.5 216.9 %all-gather.3.cloned.1.call-start = ((), (), s32[]{:S(2)}) async-start(), calls=%async_computation.5 | async-start | bytes 7864320 | tf_op jit(solution)/shard_map/all_gather | solution.py:872
  147.3 232.2 %all-gather.5.cloned.1.call-start = ((), (), s32[]{:S(2)}) async-start(), calls=%async_computation.6 | async-start | bytes 3932160 | tf_op jit(solution)/shard_map/all_gather | solution.py:872
  147.3 46.1 %collective-permute-start.6 = (bf16[512,2048]{1,0:T(8,128)(2,1)}, bf16[512,2048]{1,0:T(8,128)(2,1)}, u32[]{:S(2)}, u32[]{:S(2)}) collective-permute-start(bf16[512,2048]{1,0:T(8,128)(2,1)} %bitcast.131), channel_id=1, source_target_pairs={{0,16},{4,20},{8,24},{12,28},{16,0},{20,4},{24,8},{28,12},{1,17},{... | collective-permute-start | bytes 6291464 | tf_op jit(solution)/shard_map/ppermute | solution.py:737
  149.2 48.0 %collective-permute-start.4 = (bf16[512,2048]{1,0:T(8,128)(2,1)}, bf16[512,2048]{1,0:T(8,128)(2,1)}, u32[]{:S(2)}, u32[]{:S(2)}) collective-permute-start(bf16[512,2048]{1,0:T(8,128)(2,1)} %bitcast.132), channel_id=1, source_target_pairs={{0,8},{4,12},{8,0},{12,4},{16,24},{20,28},{24,16},{28,20},{1,9},{5... | collective-permute-start | bytes 6291464 | tf_op jit(solution)/shard_map/ppermute | solution.py:737
  149.9 149.2 %collective-permute-start.3 = (bf16[512,2048]{1,0:T(8,128)(2,1)}, bf16[512,2048]{1,0:T(8,128)(2,1)}, u32[]{:S(2)}, u32[]{:S(2)}) collective-permute-start(bf16[512,2048]{1,0:T(8,128)(2,1)} %bitcast.133), channel_id=1, source_target_pairs={{0,4},{4,0},{8,12},{12,8},{16,20},{20,16},{24,28},{28,24},{1,5},{5... | collective-permute-start | bytes 6291464 | tf_op jit(solution)/shard_map/ppermute | solution.py:737
  150.0 669.5 %reduce-scatter.3.cloned.1.call-start = ((), (), s32[]{:S(2)}) async-start(), calls=%async_computation.7 | async-start | bytes 7864320 | tf_op jit(solution)/shard_map/reduce_scatter | solution.py:876
  194.8 23.0 %collective-permute-start.8 = (bf16[256,2048]{1,0:T(8,128)(2,1)S(1)}, bf16[256,2048]{1,0:T(8,128)(2,1)S(1)}, u32[]{:S(2)}, u32[]{:S(2)}) collective-permute-start(bf16[256,2048]{1,0:T(8,128)(2,1)S(1)} %slice.202), channel_id=1, source_target_pairs={{0,8},{4,12},{8,0},{12,4},{16,24},{20,28},{24,16},{28,20},{1,9},{5... | collective-permute-start | bytes 3145736 | tf_op jit(solution)/shard_map/ppermute | solution.py:737
  198.6 22.0 %collective-permute-start.9 = (bf16[256,2048]{1,0:T(8,128)(2,1)S(1)}, bf16[256,2048]{1,0:T(8,128)(2,1)S(1)}, u32[]{:S(2)}, u32[]{:S(2)}) collective-permute-start(bf16[256,2048]{1,0:T(8,128)(2,1)S(1)} %slice.203), channel_id=1, source_target_pairs={{0,16},{4,20},{8,24},{12,28},{16,0},{20,4},{24,8},{28,12},{1,17},{... | collective-permute-start | bytes 3145736 | tf_op jit(solution)/shard_map/ppermute | solution.py:737
  198.9 106.6 %collective-permute-start.5 = (bf16[512,2048]{1,0:T(8,128)(2,1)}, bf16[512,2048]{1,0:T(8,128)(2,1)}, u32[]{:S(2)}, u32[]{:S(2)}) collective-permute-start(bf16[512,2048]{1,0:T(8,128)(2,1)} %collective-permute-done.4), channel_id=1, source_target_pairs={{0,4},{4,0},{8,12},{12,8},{16,20},{20,16},{24,28},{28,24},{1,5},{5... | collective-permute-start | bytes 6291464 | tf_op jit(solution)/shard_map/ppermute | solution.py:737
  202.2 109.7 %collective-permute-start.7 = (bf16[512,2048]{1,0:T(8,128)(2,1)}, bf16[512,2048]{1,0:T(8,128)(2,1)}, u32[]{:S(2)}, u32[]{:S(2)}) collective-permute-start(bf16[512,2048]{1,0:T(8,128)(2,1)} %collective-permute-done.6), channel_id=1, source_target_pairs={{0,4},{4,0},{8,12},{12,8},{16,20},{20,16},{24,28},{28,24},{1,5},{5... | collective-permute-start | bytes 6291464 | tf_op jit(solution)/shard_map/ppermute | solution.py:737
  222.1 95.2 %collective-permute-start.10 = (bf16[512,2048]{1,0:T(8,128)(2,1)}, bf16[512,2048]{1,0:T(8,128)(2,1)}, u32[]{:S(2)}, u32[]{:S(2)}) collective-permute-start(bf16[512,2048]{1,0:T(8,128)(2,1)} %pad_maximum_fusion), channel_id=1, source_target_pairs={{0,4},{4,0},{8,12},{12,8},{16,20},{20,16},{24,28},{28,24},{1,5},{5... | collective-permute-start | bytes 6291464 | tf_op jit(solution)/shard_map/ppermute | solution.py:737
  504.2 411.5 %reduce-scatter.5.cloned.1.call-start = ((), (), s32[]{:S(2)}) async-start(), calls=%async_computation.8 | async-start | bytes 3932160 | tf_op jit(solution)/shard_map/reduce_scatter | solution.py:876
  529.9 33.4 %collective-permute-start.11 = (bf16[512,2048]{1,0:T(8,128)(2,1)}, bf16[512,2048]{1,0:T(8,128)(2,1)}, u32[]{:S(2)}, u32[]{:S(2)}) collective-permute-start(bf16[512,2048]{1,0:T(8,128)(2,1)} %slice.205), channel_id=1, source_target_pairs={{0,4},{4,0},{8,12},{12,8},{16,20},{20,16},{24,28},{28,24},{1,5},{5... | collective-permute-start | bytes 6291464 | tf_op jit(solution)/shard_map/ppermute | solution.py:737
  531.1 26.0 %collective-permute-start.16 = (bf16[256,2048]{1,0:T(8,128)(2,1)S(1)}, bf16[256,2048]{1,0:T(8,128)(2,1)S(1)}, u32[]{:S(2)}, u32[]{:S(2)}) collective-permute-start(bf16[256,2048]{1,0:T(8,128)(2,1)S(1)} %get-tuple-element.75), channel_id=1, source_target_pairs={{0,8},{4,12},{8,0},{12,4},{16,24},{20,28},{24,16},{28,20},{1,9},{5... | collective-permute-start | bytes 3145736 | tf_op jit(solution)/shard_map/ppermute | solution.py:737
  531.9 27.4 %collective-permute-start.18 = (bf16[256,2048]{1,0:T(8,128)(2,1)S(1)}, bf16[256,2048]{1,0:T(8,128)(2,1)S(1)}, u32[]{:S(2)}, u32[]{:S(2)}) collective-permute-start(bf16[256,2048]{1,0:T(8,128)(2,1)S(1)} %get-tuple-element.76), channel_id=1, source_target_pairs={{0,16},{4,20},{8,24},{12,28},{16,0},{20,4},{24,8},{28,12},{1,17},{... | collective-permute-start | bytes 3145736 | tf_op jit(solution)/shard_map/ppermute | solution.py:737
  535.2 45.2 %collective-permute-start.20 = (bf16[256,2048]{1,0:T(8,128)(2,1)}, bf16[256,2048]{1,0:T(8,128)(2,1)S(1)}, u32[]{:S(2)}, u32[]{:S(2)}) collective-permute-start(bf16[256,2048]{1,0:T(8,128)(2,1)} %slice.219), channel_id=1, source_target_pairs={{0,16},{4,20},{8,24},{12,28},{16,0},{20,4},{24,8},{28,12},{1,17},{... | collective-permute-start | bytes 3145736 | tf_op jit(solution)/shard_map/ppermute | solution.py:737
  537.7 42.8 %collective-permute-start.13 = (bf16[256,2048]{1,0:T(8,128)(2,1)}, bf16[256,2048]{1,0:T(8,128)(2,1)S(1)}, u32[]{:S(2)}, u32[]{:S(2)}) collective-permute-start(bf16[256,2048]{1,0:T(8,128)(2,1)} %slice.209), channel_id=1, source_target_pairs={{0,8},{4,12},{8,0},{12,4},{16,24},{20,28},{24,16},{28,20},{1,9},{5... | collective-permute-start | bytes 3145736 | tf_op jit(solution)/shard_map/ppermute | solution.py:737
  558.5 43.4 %collective-permute-start.17 = (bf16[256,2048]{1,0:T(8,128)(2,1)}, bf16[256,2048]{1,0:T(8,128)(2,1)}, u32[]{:S(2)}, u32[]{:S(2)}) collective-permute-start(bf16[256,2048]{1,0:T(8,128)(2,1)} %add_convert_fusion.6), channel_id=1, source_target_pairs={{0,16},{4,20},{8,24},{12,28},{16,0},{20,4},{24,8},{28,12},{1,17},{... | collective-permute-start | bytes 3145736 | tf_op jit(solution)/shard_map/ppermute | solution.py:737
  560.7 41.2 %collective-permute-start.19 = (bf16[256,2048]{1,0:T(8,128)(2,1)}, bf16[256,2048]{1,0:T(8,128)(2,1)}, u32[]{:S(2)}, u32[]{:S(2)}) collective-permute-start(bf16[256,2048]{1,0:T(8,128)(2,1)} %add_convert_fusion.5), channel_id=1, source_target_pairs={{0,8},{4,12},{8,0},{12,4},{16,24},{20,28},{24,16},{28,20},{1,9},{5... | collective-permute-start | bytes 3145736 | tf_op jit(solution)/shard_map/ppermute | solution.py:737
  628.9 67.5 %collective-permute-start.21 = (bf16[640,512]{1,0:T(8,128)(2,1)S(1)}, bf16[640,512]{1,0:T(8,128)(2,1)S(1)}, u32[]{:S(2)}, u32[]{:S(2)}) collective-permute-start(bf16[640,512]{1,0:T(8,128)(2,1)S(1)} %get-tuple-element.55), channel_id=1, source_target_pairs={{1,0},{2,1},{3,2},{5,4},{6,5},{7,6},{9,8},{10,9},{11,10},{13,12},{... | collective-permute-start | bytes 1966088 | tf_op jit(solution)/shard_map/ppermute | solution.py:856
  696.6 28.4 %collective-permute-start.22 = (bf16[640,512]{1,0:T(8,128)(2,1)S(1)}, bf16[640,512]{1,0:T(8,128)(2,1)S(1)}, u32[]{:S(2)}, u32[]{:S(2)}) collective-permute-start(bf16[640,512]{1,0:T(8,128)(2,1)S(1)} %add_convert_fusion.8), channel_id=1, source_target_pairs={{1,0},{2,1},{3,2},{5,4},{6,5},{7,6},{9,8},{10,9},{11,10},{13,12},{... | collective-permute-start | bytes 1966088 | tf_op jit(solution)/shard_map/ppermute | solution.py:856
  725.1 65.4 %collective-permute-start.23 = (bf16[640,512]{1,0:T(8,128)(2,1)S(1)}, bf16[640,512]{1,0:T(8,128)(2,1)S(1)}, u32[]{:S(2)}, u32[]{:S(2)}) collective-permute-start(bf16[640,512]{1,0:T(8,128)(2,1)S(1)} %add_convert_fusion.7), channel_id=1, source_target_pairs={{1,0},{2,1},{3,2},{5,4},{6,5},{7,6},{9,8},{10,9},{11,10},{13,12},{... | collective-permute-start | bytes 1966088 | tf_op jit(solution)/shard_map/ppermute | solution.py:856
  824.1 94.1 %all-to-all-start.1 = ((bf16[8,64,2,1,768]{4,2,1,3,0:T(2,128)(2,1)}), bf16[8,64,2,1,768]{4,2,1,3,0:T(2,128)(2,1)}, u32[]{:S(2)}, u32[]{:S(2)}) async-start(bf16[8,64,2,1,768]{4,2,1,3,0:T(2,128)(2,1)} %bitcast.139), calls=%async_computation.2 | async-start | bytes 3145728 | tf_op jit(solution)/shard_map/all_to_all | solution.py:960
  (70 other events, 1258.6 us)
Sparse Core Ops, SparseCore 0:
  147.4 115.5 all-gather.2
  264.6 61.7 all-gather.4
  504.3 127.7 reduce-scatter.2
  634.9 74.3 reduce-scatter.4

commit v3 on v1

v3 whole, which is shorter than its diff:
```python
import functools

import jax
import jax.numpy as jnp
from jax import lax
from jax.experimental import pallas as pl
from jax.experimental.pallas import tpu as pltpu
from jax.sharding import PartitionSpec as P

QUERY_HEADS = 20
KEY_VALUE_HEADS = 5
HEAD_SIZE = 64
GROUP = QUERY_HEADS // KEY_VALUE_HEADS
QW = QUERY_HEADS * HEAD_SIZE
KW = KEY_VALUE_HEADS * HEAD_SIZE
BOTH = ("dp", "seq")

epsilon = 1e-06
F32 = jnp.float32
BF16 = jnp.bfloat16
MESH = pl.DeviceIdType.MESH


def norm_rows(inputs, scales):
    return inputs * lax.rsqrt(jnp.mean(inputs * inputs, axis=-1, keepdims=True) + epsilon) * scales


def rope_tables(positions):
    inverse_freq = 10000.0 ** (-(jnp.arange(HEAD_SIZE // 2, dtype=F32) * 2.0 / HEAD_SIZE))
    angles = inverse_freq[:, None] * positions.astype(F32)[None, :]
    return (jnp.cos(angles), jnp.sin(angles))


def head_rows(i):
    return pl.ds(pl.multiple_of(i * HEAD_SIZE, HEAD_SIZE), HEAD_SIZE)


def key_rows(i):
    return head_rows(2 * i), head_rows(2 * i + 1)


def unit(v):
    inverse = lax.rsqrt(jnp.mean(v * v, axis=0, keepdims=True) + epsilon)
    return v * inverse, inverse


def prepare_kernel(p_ref, gain_ref, cos_ref, sin_ref, q_ref, kv_ref):
    cosine, sine = cos_ref[...], sin_ref[...]

    def turned(v, gain):
        v = unit(v)[0] * gain
        first, second = v[: HEAD_SIZE // 2], v[HEAD_SIZE // 2 :]
        return jnp.concatenate(
            [first * cosine - second * sine, second * cosine + first * sine], axis=0
        )

    @pl.loop(0, KEY_VALUE_HEADS)
    def _(i):
        key, value = key_rows(i)
        keys_in = p_ref[head_rows(QUERY_HEADS + 2 * i), :]
        kv_ref[key, :] = turned(keys_in, gain_ref[HEAD_SIZE:, :]).astype(BF16)
        kv_ref[value, :] = p_ref[head_rows(QUERY_HEADS + 2 * i + 1), :].astype(BF16)

    @pl.loop(0, QUERY_HEADS)
    def _(i):
        rows = head_rows(i)
        queries = turned(p_ref[rows, :], gain_ref[:HEAD_SIZE, :]) * HEAD_SIZE**-0.5
        q_ref[rows, :] = queries.astype(BF16)


def prepare(projected, gains, cosine, sine):
    tokens = projected.shape[1]
    return pl.pallas_call(
        prepare_kernel,
        out_shape=[
            jax.ShapeDtypeStruct((QW, tokens), BF16),
            jax.ShapeDtypeStruct((2 * KW, tokens), BF16),
        ],
        compiler_params=pltpu.CompilerParams(vmem_limit_bytes=40 * 2**20),
        name="prepare",
    )(projected, gains, cosine, sine)


def prepare_back_kernel(p_ref, gain_ref, cos_ref, sin_ref, dq_ref, dkv_ref, out_ref, dg_ref, acc):
    cosine, sine = cos_ref[...], sin_ref[...]
    acc[...] = jnp.zeros_like(acc)

    def back(v, gain, dy, lines):
        u, inverse = unit(v)
        first, second = dy[: HEAD_SIZE // 2], dy[HEAD_SIZE // 2 :]
        dz = jnp.concatenate(
            [first * cosine + second * sine, second * cosine - first * sine], axis=0
        )
        acc[lines, :] += dz * u
        du = dz * gain
        return inverse * (du - u * jnp.mean(du * u, axis=0, keepdims=True))

    @pl.loop(0, KEY_VALUE_HEADS)
    def _(i):
        key, value = key_rows(i)
        rows = head_rows(QUERY_HEADS + 2 * i)
        dv = back(p_ref[rows, :], gain_ref[HEAD_SIZE:, :], dkv_ref[key, :], slice(HEAD_SIZE, None))
        out_ref[rows, :] = dv.astype(BF16)
        out_ref[head_rows(QUERY_HEADS + 2 * i + 1), :] = dkv_ref[value, :].astype(BF16)

    @pl.loop(0, QUERY_HEADS)
    def _(i):
        rows = head_rows(i)
        dy = dq_ref[rows, :] * HEAD_SIZE**-0.5
        dv = back(p_ref[rows, :], gain_ref[:HEAD_SIZE, :], dy, slice(0, HEAD_SIZE))
        out_ref[rows, :] = dv.astype(BF16)

    rest = out_ref.shape[0] - QW - 2 * KW
    out_ref[QW + 2 * KW :, :] = jnp.zeros((rest, out_ref.shape[1]), BF16)
    total = jnp.sum(acc[...], axis=1, keepdims=True)
    dg_ref[...] = jnp.broadcast_to(total, dg_ref.shape)


def prepare_back(projected, gains, cosine, sine, dqueries, dpairs):
    tokens = projected.shape[1]
    dprojected, dgains = pl.pallas_call(
        prepare_back_kernel,
        out_shape=[
            jax.ShapeDtypeStruct(projected.shape, BF16),
            jax.ShapeDtypeStruct((2 * HEAD_SIZE, 128), F32),
        ],
        scratch_shapes=[pltpu.VMEM((2 * HEAD_SIZE, tokens), F32)],
        compiler_params=pltpu.CompilerParams(vmem_limit_bytes=40 * 2**20),
        name="prepare_back",
    )(projected, gains, cosine, sine, dqueries, dpairs)
    return dprojected, dgains[:, 0]


def dot(a, b):
    return jnp.dot(a, b, preferred_element_type=F32)


def places():
    d, s = lax.axis_index("dp"), lax.axis_index("seq")
    core, column, line = d % 2, (d // 2) % 2, d // 4
    return d, s, d + 1 - 2 * core, d + 2 - 4 * column, d + 4 - 8 * line, line


def greet(peers, line=None):
    barrier = pltpu.get_barrier_semaphore()

    def signal(peer):
        pl.semaphore_signal(barrier, inc=1, device_id=peer, device_id_type=MESH)

    for peer in peers:
        signal(peer)
    if line is None:
        pl.semaphore_wait(barrier, len(peers))
        return
    d, s = line
    last = lax.axis_size("seq") - 1
    pl.when(s < last)(lambda: signal((d, s + 1)))
    pl.when(s > 0)(lambda: signal((d, s - 1)))
    pl.semaphore_wait(barrier, len(peers) + 1 - s // last + (s + last - 1) // last)


def remote(src, dst, sent, got, peer):
    return pltpu.make_async_remote_copy(
        src_ref=src,
        dst_ref=dst,
        send_sem=sent,
        recv_sem=got,
        device_id=peer,
        device_id_type=MESH,
    )


def plane_stages(x_ref, out_ref, own_sem, sent, got, place, ordered=False):
    d, s, d_c, d_x, d_y, line = place
    flip, d_d = d_c - d, d_x + d_y - d
    slots = list(range(8))
    if ordered:
        slots = [d, d_c, d_x, d_x + flip, d_y, d_y + flip, d_d, d_d + flip]
    half = x_ref.shape[0] // 2
    halves = (pl.ds(0, half), pl.ds(half, half))
    source = {1: 0, 2: 0, 4: 0, 3: 2, 5: 4, 7: 6}

    def piece(k, h, peer):
        back = source[k] if k in source else (4 if h == 0 else 2)
        src = x_ref.at[halves[h]] if back == 0 else out_ref.at[slots[back], halves[h]]
        dst = out_ref.at[slots[back] if ordered else k, halves[h]]
        return remote(src, dst, sent.at[k, h], got.at[k, h], (peer, s))

    own = pltpu.make_async_copy(x_ref, out_ref.at[slots[0]], own_sem)

    def begin():
        own.start()
        for h in (0, 1):
            for k, peer in ((2, d_x), (4, d_y), (1, d_c)):
                piece(k, h, peer).start()

    def first():
        piece(4, 0, d_y).wait_recv()
        piece(6, 0, d_x).start()
        piece(5, 0, d_c).start()
        piece(2, 0, d_x).wait_recv()
        piece(3, 0, d_c).start()

    def second():
        piece(2, 1, d_x).wait_recv()
        piece(6, 1, d_y).start()
        piece(3, 1, d_c).start()
        piece(4, 1, d_y).wait_recv()
        piece(5, 1, d_c).start()

    def end():
        for h in (0, 1):
            piece(6, h, d_x).wait_recv()
            piece(7, h, d_c).start()
        for k in (1, 3, 5, 7):
            for h in (0, 1):
                piece(k, h, d_c).wait_recv()
        for k in range(1, 8):
            for h in (0, 1):
                piece(k, h, d_c).wait_send()
        own.wait()

    return begin, first, second, end


def abreast(block):
    return jnp.concatenate(
        [block[i * HEAD_SIZE : (i + 1) * HEAD_SIZE] for i in range(GROUP)], axis=1
    )


def across(rows):
    return jnp.concatenate([rows[i : i + 1] for i in range(GROUP)], axis=1)


def seen(back, me, start):
    length = start.shape[1]
    key = lax.broadcasted_iota(jnp.int32, (length, length), 0)
    found = key + (me - back) * length >= start
    if back == 0:
        found &= key <= lax.broadcasted_iota(jnp.int32, (length, length), 1)
    bias = jnp.where(found, 0.0, -1e30)
    return jnp.concatenate([bias] * GROUP, axis=1)


def spans(i, length):
    row, head = i // KEY_VALUE_HEADS, i % KEY_VALUE_HEADS
    wide, pair = GROUP * HEAD_SIZE, 2 * HEAD_SIZE
    tokens = pl.ds(pl.multiple_of(row * length, length), length)
    return (
        tokens,
        pl.ds(pl.multiple_of(head * wide, wide), wide),
        pl.ds(pl.multiple_of(head * pair, pair), pair),
        head,
    )


def attend_kernel(n, rows, planes, start_ref, q_ref, kv_ref, *refs):
    x_refs, refs = refs[:planes], refs[planes:]
    o_ref, lse_ref, held, *refs = refs
    out_refs, refs = refs[:planes], refs[planes:]
    o_acc, l_acc, sent, got, *refs = refs
    d, me = lax.axis_index("dp"), lax.axis_index("seq")
    length = q_ref.shape[1] // rows
    if planes:
        place = places()
        d, me, d_c, d_x, d_y, _ = place
        greet([(d_c, me), (d_x, me), (d_y, me)], (d, me))
        each = [
            plane_stages(x_refs[i], out_refs[i], *refs[3 * i : 3 * i + 3], place, i > 0)
            for i in range(planes)
        ]
    else:
        greet([], (d, me))
        each = []

    def climb(step, head):
        lines = pl.ds(head * 2 * HEAD_SIZE, 2 * HEAD_SIZE)
        src = kv_ref.at[lines] if step == 1 else held.at[step - 2, lines]
        dst = held.at[step - 1, lines]
        return remote(src, dst, sent.at[step - 1, head], got.at[step - 1, head], (d, me + 1))

    heads = range(KEY_VALUE_HEADS)

    def climbs(step):
        for head in heads:
            climb(step, head).start()

    def level(back):
        @pl.loop(0, rows * KEY_VALUE_HEADS)
        def _(i):
            tokens, wide, pair, head = spans(i, length)
            block = kv_ref[pair, tokens] if back == 0 else held[back - 1, pair, tokens]
            keys, values = block[:HEAD_SIZE].T, block[HEAD_SIZE:]
            bias = seen(back, me, start_ref[0:1, tokens])
            p = jnp.exp(dot(keys, abreast(q_ref[wide, tokens])) + bias)
            total = jnp.sum(p, axis=0, keepdims=True)
            out = dot(values, p.astype(BF16))
            for g in range(GROUP):
                own = slice(g * length, (g + 1) * length)
                line = slice(g, g + 1)
                part = pl.ds(wide.start + g * HEAD_SIZE, HEAD_SIZE)
                if back == 0:
                    l_acc[head, line, tokens] = total[:, own]
                    o_acc[part, tokens] = out[:, own]
                else:
                    l_acc[head, line, tokens] += total[:, own]
                    o_acc[part, tokens] += out[:, own]

    pl.when(me < n - 1)(lambda: climbs(1))
    for stages in each:
        stages[0]()
    level(0)
    for back in range(1, n):

        def step(back=back):
            for head in heads:
                climb(back, head).wait_recv()
                if back < n - 1:
                    pl.when(me < n - 1)(lambda head=head: climb(back + 1, head).start())
            level(back)

        pl.when(me >= back)(step)
        if back <= 2:
            for stages in each:
                stages[back]()

    @pl.loop(0, rows * KEY_VALUE_HEADS)
    def _(i):
        tokens, wide, pair, head = spans(i, length)
        for g in range(GROUP):
            line = slice(g, g + 1)
            part = pl.ds(wide.start + g * HEAD_SIZE, HEAD_SIZE)
            o_ref[part, tokens] = (o_acc[part, tokens] / l_acc[head, line, tokens]).astype(BF16)
            lse_ref[head, line, tokens] = jnp.log(l_acc[head, line, tokens])

    for back in range(1, n):
        for head in heads:
            pl.when((me >= back - 1) & (me < n - 1))(
                lambda back=back, head=head: climb(back, head).wait_send()
            )
    for stages in each:
        stages[3]()


def attend(start, queries, pairs, rows, n, more):
    vmem, dma = pl.BlockSpec(memory_space=pltpu.VMEM), pltpu.SemaphoreType.DMA
    anywhere = pl.BlockSpec(memory_space=pl.ANY)
    count = queries.shape[1]
    lines = (KEY_VALUE_HEADS, 8, count)
    out_shape = [
        jax.ShapeDtypeStruct(queries.shape, BF16),
        jax.ShapeDtypeStruct(lines, F32),
        jax.ShapeDtypeStruct((n - 1, *pairs.shape), BF16),
    ]
    scratch = [
        pltpu.VMEM(queries.shape, F32),
        pltpu.VMEM(lines, F32),
        dma((n - 1, KEY_VALUE_HEADS)),
        dma((n - 1, KEY_VALUE_HEADS)),
    ]
    for extra in more:
        out_shape.append(jax.ShapeDtypeStruct((8, *extra.shape), BF16))
        scratch += [dma, dma((8, 2)), dma((8, 2))]
    return pl.pallas_call(
        functools.partial(attend_kernel, n, rows, len(more)),
        in_specs=[vmem] * 3 + [anywhere] * len(more),
        out_specs=[vmem] * 3 + [anywhere] * len(more),
        out_shape=out_shape,
        scratch_shapes=scratch,
        compiler_params=pltpu.CompilerParams(
            collective_id=2, has_side_effects=True, vmem_limit_bytes=40 * 2**20
        ),
        name="attend",
    )(start, queries, pairs, *more)


def plus(ref, *others):
    total = ref[...].astype(F32)
    for other in others:
        total += other[...].astype(F32)
    ref[...] = total.astype(BF16)


def attend_back_kernel(n, rows, summed, *refs):
    start_ref, q_ref, do_ref, o_ref, lse_ref, kv_ref, held, *refs = refs
    if summed:
        h_ref, w_ref, *refs = refs
    dq_ref, dkv_ref, *refs = refs
    if summed:
        mixed_ref, *refs = refs
    inner, part, rcv, sent, got, *refs = refs
    d, me = lax.axis_index("dp"), lax.axis_index("seq")
    length = q_ref.shape[1] // rows
    if summed:
        place = places()
        d, me, d_c, d_x, d_y, _ = place
        w_v, h_v, w_sem, h_sem, *refs = refs
        kept, leaving = refs[:2]
        load, product = block_products(h_ref, h_v, h_sem, lambda h, span: dot(h, w_v[:, span]))
        load(0).start()
        w_load = pltpu.make_async_copy(w_ref, w_v, w_sem)
        w_load.start()
        greet([(d_c, me), (d_x, me), (d_y, me)], (d, me))
        crossing, far, near, pass_on, end = plane_sums(*refs, place)

        def pair(turn, i):
            slot = turn // 2 % 2
            if turn >= 4:
                crossing(3 if slot == 0 else 1, slot).wait_send()
            product(turn, leaving.at[slot])
            crossing(i, slot).start()
            product(turn + 1, kept.at[i])

        def stage(i):
            if i == 0:
                w_load.wait()
                pair(0, 3)
                far()
                pair(2, 1)
            elif i == 1:
                near(1)
                pair(4, 2)
                pair(6, 0)
                near(2)
                near(0)
            elif i == 2:
                pass_on()
            else:
                end()
                mixed_ref[...] = kept[0]
                crossing(2, 0).wait_send()
                crossing(0, 1).wait_send()
    else:
        greet([], (d, me))

        def stage(i):
            pass

    def descend(back):
        return remote(
            part.at[back - 1], rcv.at[back - 1], sent.at[back - 1], got.at[back - 1], (d, me - 1)
        )

    def level(back):
        @pl.loop(0, rows * KEY_VALUE_HEADS)
        def _(i):
            tokens, wide, pair, head = spans(i, length)
            block = kv_ref[pair, tokens] if back == 0 else held[back - 1, pair, tokens]
            keys_t = block[:HEAD_SIZE]
            keys, values = keys_t.T, block[HEAD_SIZE:].T
            q, do = abreast(q_ref[wide, tokens]), abreast(do_ref[wide, tokens])
            bias = seen(back, me, start_ref[0:1, tokens])
            p = jnp.exp(dot(keys, q) + (bias - across(lse_ref[head, :, tokens])))
            ds = (p * (dot(values, do) - across(inner[head, :, tokens]))).astype(BF16)
            dv = back_product(p.astype(BF16), do)
            dk = back_product(ds, q)
            dq = dot(keys_t, ds)
            if back == 0:
                dkv_ref[pair, tokens] = jnp.concatenate([dk.T, dv.T], axis=0)
            else:
                part[back - 1, pair, tokens] = jnp.concatenate([dk.T, dv.T], axis=0).astype(BF16)
            for g in range(GROUP):
                own = slice(g * length, (g + 1) * length)
                line = pl.ds(wide.start + g * HEAD_SIZE, HEAD_SIZE)
                dq_ref[line, tokens] += dq[:, own]

    def finish(back):
        def more():
            descend(back + 1).wait_recv()
            if back == 0:
                dkv_ref[...] += rcv[0].astype(F32)
            else:
                plus(part.at[back - 1], rcv.at[back])

        if back < n - 1:
            pl.when(me < n - 1)(more)
        if back > 0:
            descend(back).start()

    stage(0)
    dq_ref[...] = jnp.zeros_like(dq_ref)

    @pl.loop(0, rows * KEY_VALUE_HEADS)
    def _(i):
        tokens, wide, pair, head = spans(i, length)
        for g in range(GROUP):
            line = slice(g, g + 1)
            own = pl.ds(wide.start + g * HEAD_SIZE, HEAD_SIZE)
            product = do_ref[own, tokens].astype(F32) * o_ref[own, tokens].astype(F32)
            inner[head, line, tokens] = jnp.sum(product, axis=0, keepdims=True)

    for back in range(n - 1, -1, -1):

        def run(back=back):
            level(back)
            pl.when(me == n - 1)(lambda: finish(back))

        if back:
            pl.when(me >= back)(run)
        else:
            level(0)
            pl.when(me == n - 1)(lambda: finish(0))
        if back + 1 < n - 1:
            pl.when((me >= back + 1) & (me < n - 1))(lambda back=back: finish(back + 1))
        if n - 1 - back in (1, 2):
            stage(n - 1 - back)
    pl.when(me < n - 1)(lambda: finish(0))
    stage(3)
    for back in range(1, n):
        pl.when(me >= back)(lambda back=back: descend(back).wait_send())


def attend_back(start, queries, dheads, heads, lse, pairs, held, rows, n, more):
    vmem, dma = pl.BlockSpec(memory_space=pltpu.VMEM), pltpu.SemaphoreType.DMA
    anywhere = pl.BlockSpec(memory_space=pl.ANY)
    count = queries.shape[1]
    out_shape = [
        jax.ShapeDtypeStruct(queries.shape, F32),
        jax.ShapeDtypeStruct(pairs.shape, F32),
    ]
    scratch = [
        pltpu.VMEM((KEY_VALUE_HEADS, 8, count), F32),
        pltpu.VMEM((n - 1, *pairs.shape), BF16),
        pltpu.VMEM((n - 1, *pairs.shape), BF16),
        dma((n - 1,)),
        dma((n - 1,)),
    ]
    if more:
        (tokens, deep), (_, width) = more[0].shape, more[1].shape
        block = tokens // 8
        out_shape.append(jax.ShapeDtypeStruct((block, width), BF16))
        scratch += [
            pltpu.VMEM((deep, width), BF16),
            pltpu.VMEM((2, block, deep), BF16),
            dma,
            dma((2,)),
            *sums_scratch(block, width),
        ]
    return pl.pallas_call(
        functools.partial(attend_back_kernel, n, rows, bool(more)),
        in_specs=[vmem] * 7 + [anywhere] * len(more),
        out_specs=[vmem] * len(out_shape),
        out_shape=out_shape,
        scratch_shapes=scratch,
        compiler_params=pltpu.CompilerParams(
            collective_id=3, has_side_effects=True, vmem_limit_bytes=62 * 2**20
        ),
        name="attend_back",
    )(start, queries, dheads, heads, lse, pairs, held, *more)


def weights_kernel(n, *refs):
    x_refs, (w_ref, *out_refs), refs = refs[:n], refs[n : 2 * n + 1], refs[2 * n + 1 :]
    spread_ref, own_sem, recv, send_z, send_x, send_y, send_d, send_c, own_w, sent_w, got_w = refs
    d, s, d_c, d_x, d_y, line = places()
    d_d = d_x + 4 - 8 * line
    flip = d_c - d
    plane = (d, d_c, d_x, d_x + flip, d_y, d_y + flip, d_d, d_d + flip)
    greet([(other, s) for other in plane[1:]], (d, s))
    part = spread_ref.shape[2] // 2

    def columns(k, half):
        begin = half * 8 * part + plane[k] * part
        src = w_ref.at[:, pl.ds(pl.multiple_of(begin, 128), part)]
        dst = spread_ref.at[d, :, pl.ds(half * part, part)]
        if k == 0:
            return pltpu.make_async_copy(src, dst, own_w.at[half])
        return remote(src, dst, sent_w.at[k, half], got_w.at[k, half], (plane[k], s))

    def copies(slot, sent, got, peer, own=False, many=1):
        return [
            remote(
                x_refs[i] if own else out_refs[i].at[slot if i == 0 else slot % 4],
                out_refs[i].at[slot if i == 0 else slot % 4],
                sent(i),
                got(i),
                peer,
            )
            for i in range(many)
        ]

    def start(group):
        for one in group:
            one.start()

    def sent(group):
        for one in group:
            one.wait_send()

    def each(visit, between=lambda: None):
        visit(s, 0)
        between()
        for far in (1, 2, 3):
            pl.when(s >= far)(lambda far=far: visit(s - far, 1))
            pl.when(s + far <= 3)(lambda far=far: visit(s + far, -1))

    def got(k, b):
        return lambda i: recv.at[i, k, b]

    def arrived(k, b):
        many = 1 if k else n
        for one in copies(d * 4 + b, lambda i: send_x.at[i, b], got(k, b), (d_x, s), many=many):
            one.wait_recv()

    own = [
        pltpu.make_async_copy(x_refs[i], out_refs[i].at[d * 4 + s if i == 0 else s], own_sem.at[i])
        for i in range(n)
    ]
    start(own)

    def up(b, own=False):
        return copies(d * 4 + b, lambda i: send_z.at[i, 0, b], got(0, b), (d, s + 1), own, n)

    def down(b, own=False):
        return copies(d * 4 + b, lambda i: send_z.at[i, 1, b], got(0, b), (d, s - 1), own, n)

    def spread(b, own=False):
        return (
            copies(d * 4 + b, lambda i: send_x.at[i, b], got(2, b), (d_x, s), own)
            + copies(d * 4 + b, lambda i: send_y.at[i, b], got(4, b), (d_y, s), own)
            + copies(d * 4 + b, lambda i: send_c.at[i, 0, b], got(1, b), (d_c, s), own)
        )

    def column_block(b, direction):
        own = direction == 0
        if direction:
            arrived(0, b)
        if direction >= 0:
            pl.when(s < 3)(lambda: start(up(b, own)))
        if direction <= 0:
            pl.when(s > 0)(lambda: start(down(b, own)))
        start(spread(b, own))

    def start_columns():
        for k in range(8):
            for half in (0, 1):
                columns(k, half).start()

    each(column_block, start_columns)

    def over_y(b):
        return copies(d_x * 4 + b, lambda i: send_d.at[i, b], got(6, b), (d_y, s))

    def over_x(b):
        return copies(d_y * 4 + b, lambda i: send_d.at[i, b], got(6, b), (d_x, s))

    def to_core(index, holder, b):
        return copies(
            holder * 4 + b, lambda i: send_c.at[i, index, b], got(2 * index + 1, b), (d_c, s)
        )

    def side_blocks(b, direction):
        arrived(2, b)
        pl.when(b % 2 == 0)(lambda: start(over_y(b)))
        start(to_core(1, d_x, b))
        arrived(4, b)
        pl.when(b % 2 == 1)(lambda: start(over_x(b)))
        start(to_core(2, d_y, b))

    each(side_blocks)

    def far_block(b, direction):
        arrived(6, b)
        start(to_core(3, d_d, b))

    each(far_block)

    def finish(b, direction):
        for k in (1, 3, 5, 7):
            arrived(k, b)
        if direction >= 0:
            pl.when(s < 3)(lambda: sent(up(b)))
        if direction <= 0:
            pl.when(s > 0)(lambda: sent(down(b)))
        sent(spread(b))
        sent(over_y(b))
        sent(to_core(1, d_x, b))
        sent(to_core(2, d_y, b))
        sent(to_core(3, d_d, b))

    each(finish)
    for one in own:
        one.wait()
    for k in range(8):
        for half in (0, 1):
            if k:
                columns(k, half).wait_recv()
                columns(k, half).wait_send()
            else:
                columns(k, half).wait()


def gather_weights(first, others, wide, n_dp, n_seq):
    rows, part = wide.shape[0], wide.shape[1] // (2 * n_dp)
    if (n_dp, n_seq) != (8, 4):
        spread = lax.all_to_all(wide.reshape(rows, 2, n_dp, part), "dp", 2, 0, tiled=False)
        spread = spread.reshape(n_dp, rows, 2 * part)
        return [lax.all_gather(x, BOTH, axis=0, tiled=False) for x in (first, *others)] + [spread]
    arrays = [first, *others]
    n = len(arrays)
    dma = pltpu.SemaphoreType.DMA
    return pl.pallas_call(
        functools.partial(weights_kernel, n),
        out_shape=[
            jax.ShapeDtypeStruct((n_seq if i else n_dp * n_seq, *x.shape), x.dtype)
            for i, x in enumerate(arrays)
        ]
        + [jax.ShapeDtypeStruct((n_dp, rows, 2 * part), wide.dtype)],
        in_specs=[pl.BlockSpec(memory_space=pl.ANY)] * (n + 1),
        out_specs=[pl.BlockSpec(memory_space=pl.ANY)] * (n + 1),
        scratch_shapes=[
            dma((n,)),
            dma((n, 8, 4)),
            dma((n, 2, 4)),
            dma((n, 4)),
            dma((n, 4)),
            dma((n, 4)),
            dma((n, 4, 4)),
            dma((2,)),
            dma((8, 2)),
            dma((8, 2)),
        ],
        compiler_params=pltpu.CompilerParams(collective_id=1, has_side_effects=True),
        name="gather_weights",
    )(*arrays, wide)


def weight_sums(g_ref, out_ref, refs, place):
    kept, rcv_c, rcv_d, rcv_x, rcv_y, rcv_z, load, sent_c, got_c, sent_p, got_p, sent_z, got_z = refs
    d, s, d_c, d_x, d_y, line = place
    holders = (d, d_x, d_y, d_x + d_y - d)
    flip = d_c - d
    low, high = pl.ds(0, 2), pl.ds(2, 2)

    def crossing(i):
        src = g_ref.at[pl.ds((holders[i] + flip) * 4, 4)]
        return remote(src, rcv_c.at[i], sent_c.at[i], got_c.at[i], (d_c, s))

    def loading(i):
        return pltpu.make_async_copy(
            g_ref.at[pl.ds(holders[i] * 4, 4)], kept.at[i], load.at[i]
        )

    def merge(i):
        loading(i).wait()
        crossing(i).wait_recv()
        plus(kept.at[i], rcv_c.at[i])

    def push(i):
        src, dst, peer = (
            (kept.at[3, low], rcv_d.at[low], d_x),
            (kept.at[3, high], rcv_d.at[high], d_y),
            (kept.at[1, low], rcv_x.at[low], d_x),
            (kept.at[2, high], rcv_y.at[high], d_y),
            (kept.at[2, low], rcv_y.at[low], d_y),
            (kept.at[1, high], rcv_x.at[high], d_x),
        )[i]
        return remote(src, dst, sent_p.at[i], got_p.at[i], (peer, s))

    def up(b):
        return remote(
            kept.at[0, b], rcv_z.at[0, b], sent_z.at[0, b], got_z.at[0, b], (d, s + 1)
        )

    def down(b):
        return remote(
            kept.at[0, b], rcv_z.at[1, b], sent_z.at[1, b], got_z.at[1, b], (d, s - 1)
        )

    def begin():
        for i in (3, 1, 2, 0):
            crossing(i).start()
            loading(i).start()

    def far():
        merge(3)
        push(0).start()
        push(1).start()

    def near():
        merge(1)
        push(2).start()
        merge(2)
        push(3).start()
        merge(0)

    def pass_on():
        push(0).wait_recv()
        plus(kept.at[2, low], rcv_d.at[low])
        push(4).start()
        push(1).wait_recv()
        plus(kept.at[1, high], rcv_d.at[high])
        push(5).start()

    def send_up(b):
        @pl.when(s > 0)
        def _():
            up(b).wait_recv()
            plus(kept.at[0, b], rcv_z.at[0, b])

        up(b).start()

    def send_down(b):
        @pl.when(s < 3)
        def _():
            down(b).wait_recv()
            plus(kept.at[0, b], rcv_z.at[1, b])

        down(b).start()

    def along():
        for i in (2, 3, 4, 5):
            push(i).wait_recv()
        plus(kept.at[0], rcv_x, rcv_y)
        for b in (3, 2, 1):
            pl.when(s < b)(functools.partial(send_up, b))
            pl.when(s > 3 - b)(functools.partial(send_down, 3 - b))

    def end():
        out_ref[...] = kept[0, s].astype(F32)

        @pl.when(s > 0)
        def _():
            up(s).wait_recv()
            out_ref[...] += rcv_z[0, s].astype(F32)

        @pl.when(s < 3)
        def _():
            down(s).wait_recv()
            out_ref[...] += rcv_z[1, s].astype(F32)

        for b in (3, 2, 1):
            pl.when(s < b)(lambda: up(b).wait_send())
            pl.when(s > 3 - b)(lambda: down(3 - b).wait_send())
        for i in range(4):
            crossing(i).wait_send()
        for i in range(6):
            push(i).wait_send()

    return begin, far, near, pass_on, along, end


def weight_sums_scratch(rows, columns):
    dma = pltpu.SemaphoreType.DMA
    buffer = lambda *lead: pltpu.VMEM((*lead, rows, columns), BF16)
    return [
        buffer(4, 4),
        buffer(4, 4),
        buffer(4),
        buffer(4),
        buffer(4),
        buffer(2, 4),
        dma((4,)),
        dma((4,)),
        dma((4,)),
        dma((6,)),
        dma((6,)),
        dma((2, 4)),
        dma((2, 4)),
    ]


def normed_back(dy, x, gain):
    inverse = lax.rsqrt(jnp.mean(x * x, axis=1, keepdims=True) + epsilon)
    gy = dy * gain
    x = x * inverse
    return inverse * (gy - x * jnp.mean(gy * x, axis=1, keepdims=True))


def sum_weights_kernel(n, *refs):
    g_refs, refs = refs[:n], refs[n:]
    p_ref, w_ref, x_ref, dm_ref, gain_ref, back_ref, wide_ref, *refs = refs
    out_refs, (dx_ref, wide_out, dg_ref), refs = refs[:n], refs[n : n + 3], refs[n + 3 :]
    p_v, w_v, p_sem, w_sem, *refs = refs
    w_load = pltpu.make_async_copy(w_ref, w_v, w_sem)
    p_load = pltpu.make_async_copy(p_ref, p_v, p_sem)
    w_load.start()
    p_load.start()
    place = places()
    d, s, d_c, d_x, d_y, line = place
    greet([(d_c, s), (d_x, s), (d_y, s)], (d, s))
    each = [
        weight_sums(g_refs[i], out_refs[i], refs[13 * i : 13 * i + 13], place) for i in range(n)
    ]
    block = 128

    def body(x_tile, dm_tile, dx_tile):
        i = pl.program_id(0) + offset
        span = pl.ds(pl.multiple_of(i * block, block), block)
        dy = back_product(p_v[:, span].T, w_v[...])
        dx_tile[...] = dm_tile[...] + normed_back(dy, x_tile[...].astype(F32), gain_ref[...])

    count = x_ref.shape[0] // block
    half = count // 2
    spec = lambda: pl.BlockSpec((block, x_ref.shape[1]), lambda i: (i + offset, 0))
    for i in range(6):
        for stages in each:
            stages[i]()
        if i == 0:
            w_load.wait()
            p_load.wait()
        if i in (1, 2):
            offset = (i - 1) * half
            pltpu.emit_pipeline(
                body, grid=(half,), in_specs=[spec(), spec()], out_specs=[spec()]
            )(x_ref, dm_ref, dx_ref)
        if i == 3:
            part = back_ref.shape[2] // 2
            total = jnp.zeros((dg_ref.shape[0], 1), F32)
            for j in range(16):
                half_j, holder = j // 8, j % 8
                span = slice(j * part, (j + 1) * part)
                grad = back_ref[holder, :, half_j * part : (half_j + 1) * part].astype(F32)
                wide_out[:, span] = grad
                total += jnp.sum(grad * wide_ref[:, span].astype(F32), axis=1, keepdims=True)
            dg_ref[...] = jnp.broadcast_to(total, dg_ref.shape)


def sum_weights(arrays, dprojected, w, x, dmiddle, gain, back, wide):
    dma, anywhere = pltpu.SemaphoreType.DMA, pl.BlockSpec(memory_space=pl.ANY)
    vmem = pl.BlockSpec(memory_space=pltpu.VMEM)
    n = len(arrays)
    scratch = [pltpu.VMEM(dprojected.shape, BF16), pltpu.VMEM(w.shape, BF16), dma, dma]
    for g in arrays:
        scratch += weight_sums_scratch(*g.shape[1:])
    return pl.pallas_call(
        functools.partial(sum_weights_kernel, n),
        out_shape=[jax.ShapeDtypeStruct(g.shape[1:], F32) for g in arrays]
        + [
            jax.ShapeDtypeStruct(dmiddle.shape, F32),
            jax.ShapeDtypeStruct(wide.shape, F32),
            jax.ShapeDtypeStruct((wide.shape[0], 128), F32),
        ],
        in_specs=[anywhere] * (n + 4) + [vmem] * 3,
        out_specs=[vmem] * n + [anywhere, vmem, vmem],
        scratch_shapes=scratch,
        compiler_params=pltpu.CompilerParams(
            collective_id=6, has_side_effects=True, vmem_limit_bytes=60 * 2**20
        ),
        name="sum_weights",
    )(*arrays, dprojected, w, x, dmiddle, gain, back, wide)


def plane_kernel(x_ref, g_ref, w_ref, out_ref, dh_ref, w_v, w_sem, own_sem, sent, got):
    place = places()
    d, s, d_c, d_x, d_y, line = place
    load = pltpu.make_async_copy(w_ref, w_v, w_sem)
    load.start()
    greet([(d_c, s), (d_x, s), (d_y, s)])
    begin, first, second, end = plane_stages(x_ref, out_ref, own_sem, sent, got, place)
    begin()
    load.wait()

    def body(g_tile, dh_tile):
        dh_tile[...] = back_product(g_tile[...], w_v[...]).astype(BF16)

    def some(start, count):
        pltpu.emit_pipeline(
            body,
            grid=(count,),
            in_specs=[pl.BlockSpec((512, w_v.shape[1]), lambda i: (start + i, 0))],
            out_specs=[pl.BlockSpec((512, w_v.shape[0]), lambda i: (start + i, 0))],
        )(g_ref, dh_ref)

    blocks = g_ref.shape[0] // 512
    some(0, blocks)
    first()
    second()
    end()


def plane_gather_now(x, g, w, n_dp, n_seq):
    if (n_dp, n_seq) != (8, 4):
        everyone = lax.all_gather(x, "dp", axis=0, tiled=True)
        return everyone, back_product(g, w).astype(BF16)
    dma, anywhere = pltpu.SemaphoreType.DMA, pl.BlockSpec(memory_space=pl.ANY)
    everyone, dhidden = pl.pallas_call(
        plane_kernel,
        out_shape=[
            jax.ShapeDtypeStruct((n_dp, *x.shape), x.dtype),
            jax.ShapeDtypeStruct((g.shape[0], w.shape[0]), BF16),
        ],
        in_specs=[anywhere] * 3,
        out_specs=[anywhere] * 2,
        scratch_shapes=[pltpu.VMEM(w.shape, BF16), dma, dma, dma((8, 2)), dma((8, 2))],
        compiler_params=pltpu.CompilerParams(
            collective_id=4, has_side_effects=True, vmem_limit_bytes=40 * 2**20
        ),
        name="plane_gather",
    )(x, g, w)
    return everyone.reshape(n_dp * x.shape[0], x.shape[1]), dhidden


def transposed_kernel(x_ref, g_ref, out_ref):
    n_seq, n_dp, rows, _ = out_ref.shape
    total = outer_sum(x_ref[...], g_ref[...])
    for i in range(n_dp * n_seq):
        out_ref[i % n_seq, i // n_seq] = total[i * rows : (i + 1) * rows].astype(BF16)


def transposed_product(x, g, n_dp, n_seq):
    (tokens, width), wide = x.shape, g.shape[1]
    rows, tall = width // (n_dp * n_seq), 512
    return pl.pallas_call(
        transposed_kernel,
        grid=(width // tall,),
        in_specs=[
            pl.BlockSpec((tokens, tall), lambda i: (0, i)),
            pl.BlockSpec((tokens, wide), lambda i: (0, 0)),
        ],
        out_specs=pl.BlockSpec(
            (n_seq, tall // (n_seq * rows), rows, wide), lambda i: (0, i, 0, 0)
        ),
        out_shape=jax.ShapeDtypeStruct((n_seq, n_dp, rows, wide), BF16),
        compiler_params=pltpu.CompilerParams(vmem_limit_bytes=60 * 2**20),
        cost_estimate=pl.CostEstimate(
            flops=2 * tokens * width * wide,
            bytes_accessed=2 * (tokens * width + tokens * wide + width * wide),
            transcendentals=0,
        ),
        name="transposed_product",
    )(x, g)


def plane_sums(kept, leaving, rcv_c, rcv_d, rcv_x, rcv_y, sent_c, got_c, sent_p, got_p, place):
    d, s, d_c, d_x, d_y, line = place
    rows = kept.shape[1]
    low, high = pl.ds(0, rows // 2), pl.ds(rows // 2, rows // 2)

    def crossing(i, slot):
        return remote(leaving.at[slot], rcv_c.at[i], sent_c.at[i], got_c.at[i], (d_c, s))

    def merge(i):
        crossing(i, 0).wait_recv()
        plus(kept.at[i], rcv_c.at[i])

    def push(i):
        src, dst, peer = (
            (kept.at[3, low], rcv_d.at[low], d_x),
            (kept.at[3, high], rcv_d.at[high], d_y),
            (kept.at[1, low], rcv_x.at[low], d_x),
            (kept.at[2, high], rcv_y.at[high], d_y),
            (kept.at[2, low], rcv_y.at[low], d_y),
            (kept.at[1, high], rcv_x.at[high], d_x),
        )[i]
        return remote(src, dst, sent_p.at[i], got_p.at[i], (peer, s))

    def far():
        merge(3)
        push(0).start()
        push(1).start()

    def near(i):
        merge(i)
        if i:
            push(i + 1).start()

    def pass_on():
        push(0).wait_recv()
        plus(kept.at[2, low], rcv_d.at[low])
        push(4).start()
        push(1).wait_recv()
        plus(kept.at[1, high], rcv_d.at[high])
        push(5).start()

    def end():
        for i in (2, 3, 4, 5):
            push(i).wait_recv()
        plus(kept.at[0], rcv_x, rcv_y)
        for i in range(6):
            push(i).wait_send()

    return crossing, far, near, pass_on, end


def sums_scratch(rows, width):
    dma = pltpu.SemaphoreType.DMA
    buffer = lambda *lead: pltpu.VMEM((*lead, rows, width), BF16)
    return [
        buffer(4),
        buffer(2),
        buffer(4),
        buffer(),
        buffer(),
        buffer(),
        dma((4,)),
        dma((4,)),
        dma((6,)),
        dma((6,)),
    ]


ORDER = (7, 6, 3, 2, 5, 4, 1, 0)


def block_products(g_ref, g_v, g_sem, multiply):
    rows = g_v.shape[1]

    def load(turn):
        block = pl.ds(ORDER[turn] * rows, rows)
        return pltpu.make_async_copy(g_ref.at[block], g_v.at[turn % 2], g_sem.at[turn % 2])

    def product(turn, dst):
        if turn + 1 < 8:
            load(turn + 1).start()
        load(turn).wait()
        chunk = 512

        @pl.loop(0, dst.shape[1] // chunk)
        def _(c):
            span = pl.ds(pl.multiple_of(c * chunk, chunk), chunk)
            dst[:, span] = multiply(g_v[turn % 2], span).astype(BF16)

    return load, product


def plane_sum_kernel(g_ref, w_ref, h_ref, t_ref, out_ref, grad_ref, w_v, g_v, h_v, *refs):
    w_sem, g_sem, h_sem, out_sem, *refs = refs
    place = places()
    d, s, d_c, d_x, d_y, line = place
    kept, leaving = refs[:2]
    w_wait = load_rows(w_ref, w_v, w_sem, 8, 4)
    load, product = block_products(
        g_ref, g_v, g_sem, lambda g, span: back_product(g, w_v[span, :])
    )
    load(0).start()
    h_load = pltpu.make_async_copy(h_ref, h_v, h_sem)
    h_load.start()
    greet([(d_c, s), (d_x, s), (d_y, s)])
    crossing, far, near, pass_on, end = plane_sums(*refs, place)
    w_wait()

    def pair(turn, i):
        slot = turn // 2 % 2
        if turn >= 4:
            crossing(3 if slot == 0 else 1, slot).wait_send()
        product(turn, leaving.at[slot])
        crossing(i, slot).start()
        product(turn + 1, kept.at[i])

    pair(0, 3)
    far()
    pair(2, 1)
    pair(4, 2)
    near(1)
    pair(6, 0)
    near(2)
    near(0)
    h_load.wait()

    def grad_body(t_tile, grad_tile):
        grad_tile[...] = outer_sum(h_v[...], t_tile[...]).astype(BF16)

    tokens, deep = h_v.shape
    wide = 256

    def grad_tiles(first, count):
        pltpu.emit_pipeline(
            grad_body,
            grid=(count,),
            in_specs=[pl.BlockSpec((tokens, wide), lambda i: (0, first + i))],
            out_specs=[pl.BlockSpec((deep, wide), lambda i: (0, first + i))],
        )(t_ref, grad_ref)

    grad_tiles(0, 2)
    pass_on()
    grad_tiles(2, t_ref.shape[1] // wide - 2)
    end()
    out = pltpu.make_async_copy(kept.at[0], out_ref, out_sem)
    out.start()
    crossing(2, 0).wait_send()
    crossing(0, 1).wait_send()
    out.wait()


def plane_sum(g, w, h, t, rows):
    dma, anywhere = pltpu.SemaphoreType.DMA, pl.BlockSpec(memory_space=pl.ANY)
    width, deep = w.shape
    return pl.pallas_call(
        plane_sum_kernel,
        out_shape=[
            jax.ShapeDtypeStruct((rows, width), BF16),
            jax.ShapeDtypeStruct((h.shape[1], t.shape[1]), BF16),
        ],
        in_specs=[anywhere] * 4,
        out_specs=[anywhere] * 2,
        scratch_shapes=[
            pltpu.VMEM((width, deep), BF16),
            pltpu.VMEM((2, rows, deep), BF16),
            pltpu.VMEM(h.shape, BF16),
            dma,
            dma((2,)),
            dma,
            dma,
            *sums_scratch(rows, width),
        ],
        compiler_params=pltpu.CompilerParams(
            collective_id=5, has_side_effects=True, vmem_limit_bytes=62 * 2**20
        ),
        name="plane_sum",
    )(g, w, h, t)


def sigmoid(v):
    return 1.0 / (1.0 + jnp.exp(-v))


def load_rows(w_ref, w_v, sem, n_dp, n_seq):
    rows = w_v.shape[0] // (n_dp * n_seq)

    @pl.loop(0, n_dp * n_seq)
    def _(i):
        src = pl.ds(pl.multiple_of(i * rows, rows), rows)
        place = (i % n_dp) * n_seq + i // n_dp
        dst = pl.ds(pl.multiple_of(place * rows, rows), rows)
        pltpu.make_async_copy(w_ref.at[src], w_v.at[dst], sem).start()

    return pltpu.make_async_copy(w_ref, w_v, sem).wait


def gate_up_kernel(n_dp, n_seq, x_ref, dh_ref, w_ref, hidden_ref, dgu_ref, w_v, sem):
    pl.when(pl.program_id(0) == 0)(lambda: load_rows(w_ref, w_v, sem, n_dp, n_seq)())
    part = hidden_ref.shape[1]
    step = 256 if part % 256 == 0 else 128
    for c in range(0, part, step):
        first, second = slice(c, c + step), slice(part + c, part + c + step)
        gate, up = dot(x_ref[...], w_v[:, first]), dot(x_ref[...], w_v[:, second])
        dhidden = dh_ref[:, first].astype(F32)
        sig = sigmoid(gate)
        silu = gate * sig
        hidden_ref[:, first] = (silu * up).astype(BF16)
        dgu_ref[:, first] = (dhidden * up * (sig + silu * (1.0 - sig))).astype(BF16)
        dgu_ref[:, second] = (dhidden * silu).astype(BF16)


def gate_up_product(x, dhidden, w, n_dp, n_seq):
    tokens, width = x.shape
    wide = w.shape[1]
    block = 512
    span = lambda columns: pl.BlockSpec((block, columns), lambda i: (i, 0))
    return pl.pallas_call(
        functools.partial(gate_up_kernel, n_dp, n_seq),
        grid=(tokens // block,),
        in_specs=[span(width), span(wide // 2), pl.BlockSpec(memory_space=pl.ANY)],
        out_specs=[span(wide // 2), span(wide)],
        out_shape=[
            jax.ShapeDtypeStruct((tokens, wide // 2), BF16),
            jax.ShapeDtypeStruct((tokens, wide), BF16),
        ],
        scratch_shapes=[pltpu.VMEM(w.shape, BF16), pltpu.SemaphoreType.DMA],
        compiler_params=pltpu.CompilerParams(vmem_limit_bytes=56 * 2**20),
        cost_estimate=pl.CostEstimate(
            flops=2 * tokens * width * wide,
            bytes_accessed=2 * (tokens * width + width * wide + tokens * wide * 2),
            transcendentals=tokens * wide // 2,
        ),
        name="gate_up",
    )(x, dhidden, w)


def mm(a, b):
    return jnp.dot(a, b, preferred_element_type=F32)


def outer_sum(left, right):
    return lax.dot_general(left, right, (((0,), (0,)), ((), ())), preferred_element_type=F32)


def back_product(rows, weight):
    return lax.dot_general(rows, weight, (((1,), (1,)), ((), ())), preferred_element_type=F32)


def gather(x, axes):
    return lax.all_gather(x, axes, axis=0, tiled=True)


def scatter(x, axes):
    return lax.psum_scatter(x, axes, scatter_dimension=0, tiled=True)


def shards(
    tokens, lengths, w_qkv, w_out, w_gate_up, w_down, attn_gain, ffn_gain, head_gains, out_grad
):
    n_dp, n_seq = lax.axis_size("dp"), lax.axis_size("seq")
    rows, length, width = tokens.shape
    count = rows * length
    ff = w_gate_up.shape[1] // 2
    part = ff // n_dp
    wr = w_gate_up.shape[0]
    offset = lax.axis_index("seq") * length
    local_pos = offset + jnp.arange(length, dtype=jnp.int32)
    cosine, sine = rope_tables(jnp.concatenate([local_pos] * rows))
    ends = jnp.cumsum(lengths, axis=1, dtype=jnp.int32)
    start = jnp.sum(
        jnp.where(local_pos[None, :, None] >= ends[:, None, :], lengths[:, None, :], 0), axis=2
    ).reshape(1, count)
    start = jnp.broadcast_to(start, (8, count))

    full = (n_dp, n_seq) == (8, 4)
    qkv_w = w_qkv.shape[1]
    paired = w_qkv[:, QW:].reshape(wr, 2, KEY_VALUE_HEADS, HEAD_SIZE).transpose(0, 2, 1, 3)
    spare = width - qkv_w
    gains = jnp.concatenate([attn_gain, ffn_gain])
    gains = [jnp.pad(g, (0, spare - g.shape[0]))[None] for g in (gains, head_gains)]
    gains.append(jnp.zeros((wr - 2, spare), BF16))
    own_qkv = jnp.concatenate(
        [w_qkv[:, :QW], paired.reshape(wr, 2 * KW), jnp.concatenate(gains, axis=0)], axis=1
    )
    out_rows = w_out.shape[0]
    own_out = jnp.pad(w_out, ((0, -out_rows % 16), (0, 0)))
    all_qkv, some_out, spread = gather_weights(own_qkv, [own_out], w_gate_up, n_dp, n_seq)
    qkv_full = all_qkv.reshape(width, width)
    attn_gain_full = all_qkv[:, 0, qkv_w : qkv_w + wr].reshape(-1).astype(F32)
    ffn_gain_full = all_qkv[:, 0, qkv_w + wr : qkv_w + 2 * wr].reshape(-1).astype(F32)
    head_full = all_qkv[:, 1, qkv_w : qkv_w + head_gains.shape[0]].reshape(-1).astype(F32)

    w_down, qkv_full = lax.optimization_barrier((w_down, qkv_full))
    down_w = gather(w_down, "seq")
    cotangent_low = out_grad.reshape(count, width)

    x_rows = tokens.reshape(count, width).astype(F32)
    normed_low = norm_rows(x_rows, attn_gain_full).astype(BF16)
    projected = lax.dot_general(
        qkv_full, normed_low, (((0,), (1,)), ((), ())), preferred_element_type=F32
    )

    queries, pairs = prepare(projected, head_full[:, None], cosine, sine)
    more = [cotangent_low, some_out] if full else []
    heads_out, lse, held, *planes = attend(start, queries, pairs, rows, n_seq, more)
    gate_up_w = gather(spread.reshape(n_dp * wr, 2 * part), "seq")
    if full:
        cotangent_all = planes[0].reshape(n_dp * count, width)
        all_out = planes[1].reshape(n_dp * n_seq, -1, width)
    else:
        cotangent_all, all_out = gather(cotangent_low, "dp"), some_out
    out_full = all_out.reshape(-1, width)
    fill = ((0, 0), (0, all_out.shape[1] - out_rows), (0, 0))
    heads_full = jnp.pad(heads_out.reshape(n_dp * n_seq, out_rows, count), fill)
    heads_full = heads_full.reshape(-1, count)
    middle = x_rows + outer_sum(heads_full, out_full)
    normed2, norm2_pull = jax.vjp(norm_rows, middle, ffn_gain_full)
    normed2_all, dhidden = plane_gather_now(
        normed2.astype(BF16), cotangent_all, down_w, n_dp, n_seq
    )
    hidden, dgate_up = gate_up_product(normed2_all, dhidden, gate_up_w, n_dp, n_seq)
    gate_up_grad = transposed_product(normed2_all, dgate_up, n_dp, n_seq)
    gate_up_grad, dgate_up = lax.optimization_barrier((gate_up_grad, dgate_up))
    gate_up_grad = scatter(gate_up_grad.reshape(width, 2 * part), "seq")
    if full:
        dnormed2, down_grad = plane_sum(dgate_up, gate_up_w, hidden, cotangent_all, count)
    else:
        ordered = gate_up_w.reshape(n_seq, n_dp, wr, 2 * part).transpose(1, 0, 2, 3)
        ordered = ordered.reshape(width, 2 * part)
        dnormed2 = scatter(back_product(dgate_up, ordered).astype(BF16), "dp")
        down_grad = outer_sum(hidden, cotangent_all).astype(BF16)
    dnormed2 = dnormed2.astype(F32)

    dmiddle_norm = norm2_pull(dnormed2)[0]
    dmiddle = cotangent_low.astype(F32) + dmiddle_norm
    dattend = dmiddle.astype(BF16)
    dheads = back_product(out_full, dattend).astype(BF16).reshape(n_dp * n_seq, -1, count)
    dheads = dheads[:, :out_rows].reshape(QW, count)
    if full:
        dqueries, dpairs, mixed = attend_back(
            start, queries, dheads, heads_out, lse, pairs, held, rows, n_seq, [hidden, down_w]
        )
    else:
        dqueries, dpairs = attend_back(
            start, queries, dheads, heads_out, lse, pairs, held, rows, n_seq, []
        )
        mixed = scatter(mm(hidden, down_w).astype(BF16), "dp")
    mixed = middle + mixed.astype(F32)
    gate_up_grad, dqueries = lax.optimization_barrier((gate_up_grad, dqueries))
    gate_up_grad = lax.all_to_all(
        gate_up_grad.reshape(n_dp, wr, 2 * part), "dp", 0, 0, tiled=True
    )
    down_grad, dqueries = lax.optimization_barrier((down_grad, dqueries))
    down_grad = scatter(down_grad, "seq")
    dprojected_low, head_grad = prepare_back(
        projected, head_full[:, None], cosine, sine, dqueries, dpairs
    )
    qkv_grad = lax.dot_general(
        normed_low, dprojected_low, (((0,), (1,)), ((), ())), preferred_element_type=F32
    ).astype(BF16)
    few = head_gains.shape[0]
    head_grad = head_grad.astype(BF16).reshape(n_dp * n_seq, 1, few)
    qkv_grad = lax.dynamic_update_slice(
        qkv_grad.reshape(n_dp * n_seq, wr, width), head_grad, (0, 0, qkv_w)
    )
    dattend, qkv_grad = lax.optimization_barrier((dattend, qkv_grad))
    out_grads = mm(heads_full, dattend).astype(BF16).reshape(n_dp * n_seq, -1, width)
    if full:
        qkv_grad, out_weight_grad, tokens_grad, gate_up_grad, ffn_products = sum_weights(
            [qkv_grad, out_grads],
            dprojected_low,
            qkv_full,
            tokens.reshape(count, width),
            dmiddle,
            attn_gain_full[None],
            gate_up_grad,
            w_gate_up,
        )
        ffn_products = ffn_products[:, 0]
    else:
        qkv_grad, out_weight_grad = (
            scatter(scatter(g.reshape(-1, width), "dp"), "seq").astype(F32)
            for g in (qkv_grad, out_grads)
        )
        gate_up_grad = gate_up_grad.reshape(n_dp, wr, 2, part).transpose(1, 2, 0, 3)
        gate_up_grad = gate_up_grad.reshape(wr, 2 * ff).astype(F32)
        ffn_products = jnp.sum(w_gate_up.astype(F32) * gate_up_grad, axis=1)
        dnormed = back_product(dprojected_low.T, qkv_full)
        tokens_grad = dmiddle + normed_back(dnormed, x_rows, attn_gain_full)
    head_out = qkv_grad[0, qkv_w : qkv_w + few]
    unpaired = qkv_grad[:, QW:qkv_w].reshape(wr, KEY_VALUE_HEADS, 2, HEAD_SIZE).transpose(0, 2, 1, 3)
    qkv_grad = jnp.concatenate([qkv_grad[:, :QW], unpaired.reshape(wr, 2 * KW)], axis=1)
    attn_gain_out = jnp.sum(w_qkv.astype(F32) * qkv_grad, axis=1) / attn_gain.astype(F32)
    ffn_gain_out = ffn_products / ffn_gain.astype(F32)
    return (
        mixed.astype(BF16).reshape(rows, length, width),
        tokens_grad.reshape(rows, length, width),
        qkv_grad,
        out_weight_grad[:out_rows],
        gate_up_grad,
        down_grad.astype(F32),
        attn_gain_out,
        ffn_gain_out,
        head_out,
    )


def solution(mesh):
    in_specs = (
        P("dp", "seq", None),
        P("dp", None),
        P(("dp", "seq"), None),
        P(("dp", "seq"), None),
        P(("dp", "seq"), None),
        P(("dp", "seq"), None),
        P(("dp", "seq")),
        P(("dp", "seq")),
        P(("dp", "seq")),
        P("dp", "seq", None),
    )
    out_specs = (
        P("dp", "seq", None),
        P("dp", "seq", None),
        P(("dp", "seq"), None),
        P(("dp", "seq"), None),
        P(("dp", "seq"), None),
        P(("dp", "seq"), None),
        P(("dp", "seq")),
        P(("dp", "seq")),
        P(("dp", "seq")),
    )
    return jax.shard_map(shards, mesh=mesh, in_specs=in_specs, out_specs=out_specs, check_vma=False)
```

time: 1520 us -> 742 us (0.49)
  waiting for transfers between devices: 961 us -> 3.09 us
  Pallas kernels: 0 us -> 613 us
  matrix products: 326 us -> 37 us
  local copies, waits for them, and re-layouts: 114 us -> 36.7 us
  other arithmetic: 85.5 us -> 26.9 us
    pallas_call x0 -> x10, Pallas kernels: none -> 613 us  [the longest x1 113 us: sum_weights(): pl.pallas_call(functools.partial(sum_weights_kernel, n), out_shape=[jax.S...]
    reduce_scatter x8 -> x2, waiting for transfers between devices: 523 us -> 0.02 us  [scatter(): return lax.psum_scatter(x, axes, scatter_dimension=0, tiled=True)]
    all_gather x7 -> x2, waiting for transfers between devices: 416 us -> 0.02 us  [gather(): return lax.all_gather(x, axes, axis=0, tiled=True)]
    dot_general x4 -> x1, matrix products: 79.4 us -> 3.47 us  [back_product(): lax.dot_general(rows, weight, (((1,), (1,)), ((), ())), preferred_element...]
    dot_general x4 -> x1, matrix products: 73 us -> 8.2 us  [mm(): return jnp.dot(a, b, preferred_element_type=F32)]
    dot_general x5 -> x2, matrix products: 80.8 us -> 16.3 us  [the longest x1 8.84 us: shards(): lax.dot_general(normed_low, dprojected_low, (((0,), (1,)), ((), ())), pre...]
    dot_general x4 -> x1, matrix products: 73.4 us -> 9.02 us  [outer_sum(): lax.dot_general(left, right, (((0,), (0,)), ((), ())), preferred_element_...]
    reshape x15 -> x4, local copies, waits for them, and re-layouts: 47.3 us -> 0.69 us  [the longest x2 0.39 us: shards(): qkv_grad[:, QW:qkv_w].reshape(wr, KEY_VALUE_HEADS, 2, HEAD_SIZE)]
  transfers between devices with their start and end apart: 18 -> 5, of which waited for: 16 -> 1; matrix products, arithmetic and copies ran while one was open for 20% -> 10% of each run, Pallas kernels for 0% -> 65%
where the time goes in v3:
time: 742 us; the launch traced here: 736 us
  Pallas kernels  613 us (83%)
  matrix products  37 us (5%)
  local copies, waits for them, and re-layouts  36.7 us (5%)
  other arithmetic  26.9 us (4%)
  between operations  14.8 us (2%)
    pallas_call x1, Pallas kernels, sum_weights(): pl.pallas_call(functools.partial(sum_weights_kernel, n), out_shape=[jax.S...  113 us
    pallas_call x1, Pallas kernels, attend_back(): pl.pallas_call(functools.partial(attend_back_kernel, n, rows, bool(more))...  100 us
    pallas_call x1, Pallas kernels, attend(): pl.pallas_call(functools.partial(attend_kernel, n, rows, len(more)), in_s...  98.5 us
    pallas_call x1, Pallas kernels, plane_sum(): pl.pallas_call(plane_sum_kernel, out_shape=[jax.ShapeDtypeStruct((rows, w...  86.9 us
    pallas_call x1, Pallas kernels, plane_gather_now(): pl.pallas_call(plane_kernel, out_shape=[jax.ShapeDtypeStruct((n_dp, *x.sh...  75.9 us
    pallas_call x1, Pallas kernels, gather_weights(): pl.pallas_call(functools.partial(weights_kernel, n), out_shape=[jax.Shape...  60.9 us
    pallas_call x1, Pallas kernels, gate_up_product(): pl.pallas_call(functools.partial(gate_up_kernel, n_dp, n_seq), grid=(toke...  37.6 us
    pallas_call x1, Pallas kernels, transposed_product(): pl.pallas_call(transposed_kernel, grid=(width // tall,), in_specs=[pl.Blo...  33.8 us
  transfers between devices with their start and end apart: 5, of which 1 were waited for; matrix products, arithmetic and copies ran while one was open for 10% of the time, Pallas kernels for 65%

profile of v3, /device:TPU:0, one launch (start us, length us, event | category | flops | bytes accessed | tf_op | source)
XLA Modules:
  0.0 735.8 jit_solution(3055285263353379752)
XLA Ops:
  12.8 60.9 %gather_weights.1 = (bf16[32,64,2048]{2,1,0:T(8,128)(2,1)}, bf16[4,48,2048]{2,1,0:T(8,128)(2,1)}, bf16[8,64,1536]{2,1,0:T(8,128)(2,1)}) custom-call(bf16[64,2048]{1,0:T(8,128)(2,1)} %maximum_maximum_fusion.refs_0_, bf16[48,2048]{1,0:T(8,128)(2,1)} %pad.13.refs_1_, bf16[64,12288]{1,0:T(8,128)(2,1)} %refs_8_.1), custom_call_target="tpu_custom_call" | custom-call | tf_op jit(solution)/shard_map/gather_weights/pallas_call | solution.py:703
  78.4 7.5 %fusion.4.p_ref = f32[2048,512]{1,0:T(8,128)S(1)} fusion(bf16[2048,2048]{1,0:T(8,128)(2,1)} %bitcast.57, bf16[512,2048]{1,0:T(8,128)(2,1)S(1)} %bitcast.55, f32[2048]{0:T(1024)S(1)} %reshape.206, f32[512]{0:T(512)S(1)} %bitcast.75), kind=kOutput, calls=%fused_computation.15 | convolution fusion | flops 4299161600 | bytes 14690304 | tf_op jit(solution)/shard_map/dot_general | solution.py:1324
  86.0 2.4 prepare.1
  90.4 98.5 %attend.1 = (bf16[1280,512]{1,0:T(8,128)(2,1)S(1)}, f32[5,8,512]{2,1,0:T(8,128)S(1)}, bf16[3,640,512]{2,1,0:T(8,128)(2,1)S(1)}, bf16[8,512,2048]{2,1,0:T(8,128)(2,1)}, bf16[8,4,48,2048]{3,2,1,0:T(8,128)(2,1)S(1)}) custom-call(s32[8,512]{1,0:T(8,128)S(1)} %broadcast_in_dim.46.start_ref.refs_0_, bf16[1280,512]{1,0:T(8,128)(2,1)S(1)} %get-tuple-element.47.q_ref.refs_1_, ...), custom_call_target="tpu_custom_call" | custom-call | tf_op jit(solution)/shard_map/attend/pallas_call | solution.py:365
  189.0 2.6 copy-done.5
  196.3 9.0 %multiply_reduce_fusion.1 = (f32[512]{0:T(512)S(1)}, f32[512,2048]{1,0:T(8,128)}) fusion(bf16[1536,512]{1,0:T(8,128)(2,1)} %bitcast.62, bf16[1536,2048]{1,0:T(8,128)(2,1)} %bitcast.46, bf16[512,2048]{1,0:T(8,128)(2,1)S(1)} %bitcast.56), kind=kOutput, calls=%fused_computation.12 | convolution fusion | flops 3225419264 | bytes 14157824 | tf_op jit(solution)/shard_map/dot_general | solution.py:1267
  205.9 2.6 multiply_convert_fusion.x_ref
  210.5 75.9 %plane_gather.1 = (bf16[8,512,2048]{2,1,0:T(8,128)(2,1)}, bf16[4096,768]{1,0:T(8,128)(2,1)S(1)}) custom-call(bf16[512,2048]{1,0:T(8,128)(2,1)S(1)} %multiply_convert_fusion.x_ref, bf16[4096,2048]{1,0:T(8,128)(2,1)} %bitcast.51, bf16[768,2048]{1,0:T(8,128)(2,1)S(1)} %copy-done.2), custom_call_target="tpu_custom_call" | custom-call | tf_op jit(solution)/shard_map/plane_gather/pallas_call | solution.py:978
  286.4 2.6 copy-done.18
  289.1 37.6 %gate_up.1 = (bf16[4096,768]{1,0:T(8,128)(2,1)}, bf16[4096,1536]{1,0:T(8,128)(2,1)}) custom-call(bf16[4096,2048]{1,0:T(8,128)(2,1)} %bitcast.77, bf16[4096,768]{1,0:T(8,128)(2,1)} %copy-done.18, bf16[2048,1536]{1,0:T(8,128)(2,1)} %all-gather.5.cloned.1.call-done.w_ref), custom_call_target="tpu_custom_call" | custom-call | flops 25769803776 | bytes 48234496 | tf_op jit(solution)/shard_map/gate_up/pallas_call | solution.py:1242
  326.7 33.8 %transposed_product.1 = bf16[4,8,64,1536]{3,2,1,0:T(8,128)(2,1)} custom-call(bf16[4096,2048]{1,0:T(8,128)(2,1)} %bitcast.78, bf16[4096,1536]{1,0:T(8,128)(2,1)} %get-tuple-element.58.g_ref), custom_call_target="tpu_custom_call" | custom-call | flops 25769803776 | bytes 35651584 | tf_op jit(solution)/shard_map/transposed_product/pallas_call | solution.py:1005
  360.6 86.9 %plane_sum.1 = (bf16[512,2048]{1,0:T(8,128)(2,1)}, bf16[768,2048]{1,0:T(8,128)(2,1)}) custom-call(bf16[4096,1536]{1,0:T(8,128)(2,1)} %get-tuple-element.58.g_ref, bf16[2048,1536]{1,0:T(8,128)(2,1)} %all-gather.5.cloned.1.call-done.w_ref, bf16[4096,768]{1,0:T(8,128)(2,1)} %get-tuple-element.59.h_ref.refs_7_, bf16[4096,2048]{1,0:T(8,128)(2,1)} %bitcast.52), custom_call_target="tpu_custom_call" | custom-call | tf_op jit(solution)/shard_map/plane_sum/pallas_call | solution.py:1180
  447.5 3.6 multiply_reduce_fusion
  451.6 5.8 fusion.9
  457.4 3.5 convolution_convert_fusion.2
  462.1 100.1 %attend_back.1 = (f32[1280,512]{1,0:T(8,128)}, f32[640,512]{1,0:T(8,128)}, bf16[512,2048]{1,0:T(8,128)(2,1)}) custom-call(s32[8,512]{1,0:T(8,128)} %copy-done.16, bf16[1280,512]{1,0:T(8,128)(2,1)} %copy-done.7, bf16[1280,512]{1,0:T(8,128)(2,1)} %bitcast.64, bf16[1280,512]{1,0:T(8,128)(2,1)} %copy-done.6, f32[5,8,512]{2,1,0:T(8,128)} %copy-done.17, ...), custom_call_target="tpu_custom_call" | custom-call | tf_op jit(solution)/shard_map/attend_back/pallas_call | solution.py:540
  564.0 4.3 add_convert_fusion
  569.3 2.9 prepare_back.1
  572.4 4.6 all-to-all-start
  577.0 8.8 %convolution_convert_fusion.1 = bf16[2048,2048]{1,0:T(8,128)(2,1)} fusion(bf16[2048,512]{1,0:T(8,128)(2,1)S(1)} %get-tuple-element.70.refs_2_, bf16[512,2048]{1,0:T(8,128)(2,1)} %bitcast.53, f32[2048]{0:T(1024)S(1)} %copy-done.30, f32[512]{0:T(512)S(1)} %bitcast.76), kind=kOutput, calls=%fused_computation.1 | convolution fusion | flops 4303355904 | bytes 12593152 | tf_op jit(solution)/shard_map/dot_general | solution.py:1383
  587.6 8.2 %convolution_convert_fusion = bf16[1536,2048]{1,0:T(8,128)(2,1)} fusion(bf16[1536,512]{1,0:T(8,128)(2,1)} %bitcast.63, bf16[512,2048]{1,0:T(8,128)(2,1)} %copy-done.23), kind=kOutput, calls=%fused_computation | convolution fusion | flops 3224371200 | bytes 9961472 | tf_op jit(solution)/shard_map/dot_general | solution.py:1263
  598.1 113.5 %sum_weights.1 = (f32[64,2048]{1,0:T(8,128)}, f32[48,2048]{1,0:T(8,128)}, f32[512,2048]{1,0:T(8,128)}, f32[64,12288]{1,0:T(8,128)}, f32[64,128]{1,0:T(8,128)}) custom-call(bf16[32,64,2048]{2,1,0:T(8,128)(2,1)} %dynamic_update_slice.3.refs_0_, bf16[32,48,2048]{2,1,0:T(8,128)(2,1)} %bitcast.60, bf16[2048,512]{1,0:T(8,128)(2,1)} %copy-done.10, ...), custom_call_target="tpu_custom_call" | custom-call | tf_op jit(solution)/shard_map/sum_weights/pallas_call | solution.py:927
  719.8 2.5 convert_element_type.136
  722.3 4.8 copy.44
  (134 shorter events, 38.0 us)
Async XLA Ops:
  7.2 69.1 %copy-start.19 = (bf16[2,256,2048]{2,1,0:T(8,128)(2,1)S(1)}, bf16[2,256,2048]{2,1,0:T(8,128)(2,1)}, u32[]{:S(2)}) copy-start(bf16[2,256,2048]{2,1,0:T(8,128)(2,1)} %param.10) | copy-start | bytes 6291460
  7.2 201.4 %all-gather.3.cloned.1.call-start = ((), (), s32[]{:S(2)}) async-start(), calls=%async_computation.3 | async-start | bytes 3932160 | tf_op jit(solution)/shard_map/all_gather | solution.py:1275
  9.2 68.6 %copy-start.31 = (s32[2,4]{1,0:T(2,128)S(1)}, s32[2,4]{1,0:T(2,128)}, u32[]{:S(2)}) copy-start(s32[2,4]{1,0:T(2,128)} %param.11) | copy-start | bytes 100
  73.8 215.3 %all-gather.5.cloned.1.call-start = ((), (), s32[]{:S(2)}) async-start(), calls=%async_computation.4 | async-start | bytes 7864320 | tf_op jit(solution)/shard_map/all_gather | solution.py:1275
  74.5 487.7 %reduce-scatter.3.cloned.1.call-start = ((), (), s32[]{:S(2)}) async-start(), calls=%async_computation.5 | async-start | bytes 7864320 | tf_op jit(solution)/shard_map/reduce_scatter | solution.py:1279
  76.3 9.6 %copy-start.29 = (f32[2048]{0:T(1024)}, f32[2048]{0:T(1024)S(1)}, u32[]{:S(2)}) copy-start(f32[2048]{0:T(1024)S(1)} %reshape.206) | copy-start | bytes 24580
  76.8 9.1 %copy-start.32 = (f32[1,2,2,128]{3,1,2,0:T(2,128)}, f32[1,2,2,128]{3,1,2,0:T(2,128)S(1)}, u32[]{:S(2)}) copy-start(f32[1,2,2,128]{3,1,2,0:T(2,128)S(1)} %copy.40) | copy-start | bytes 6148
  78.4 7.5 %copy-start.14 = (f32[32,512]{1,0:T(8,128)}, f32[32,512]{1,0:T(8,128)S(1)}, u32[]{:S(2)}) copy-start(f32[32,512]{1,0:T(8,128)S(1)} %get-tuple-element.88.cos_ref) | copy-start | bytes 196612
  90.4 98.6 %copy-start.7 = (bf16[1280,512]{1,0:T(8,128)(2,1)}, bf16[1280,512]{1,0:T(8,128)(2,1)S(1)}, u32[]{:S(2)}) copy-start(bf16[1280,512]{1,0:T(8,128)(2,1)S(1)} %get-tuple-element.47.q_ref.refs_1_) | copy-start | bytes 3932164
  90.4 103.1 %copy-start.8 = (bf16[640,512]{1,0:T(8,128)(2,1)}, bf16[640,512]{1,0:T(8,128)(2,1)S(1)}, u32[]{:S(2)}) copy-start(bf16[640,512]{1,0:T(8,128)(2,1)S(1)} %get-tuple-element.48.kv_ref.refs_5_) | copy-start | bytes 1966084
  90.4 115.0 %copy-start.16 = (s32[8,512]{1,0:T(8,128)}, s32[8,512]{1,0:T(8,128)S(1)}, u32[]{:S(2)}) copy-start(s32[8,512]{1,0:T(8,128)S(1)} %broadcast_in_dim.46.start_ref.refs_0_) | copy-start | bytes 49156
  193.5 11.9 %copy-start.6 = (bf16[1280,512]{1,0:T(8,128)(2,1)}, bf16[1280,512]{1,0:T(8,128)(2,1)S(1)}, u32[]{:S(2)}) copy-start(bf16[1280,512]{1,0:T(8,128)(2,1)S(1)} %get-tuple-element.50.refs_3_) | copy-start | bytes 3932164
  196.3 9.6 %copy-start.25 = (f32[2048]{0:T(1024)S(1)}, f32[2048]{0:T(1024)}, u32[]{:S(2)}) copy-start(f32[2048]{0:T(1024)} %reshape.208) | copy-start | bytes 24580
  360.5 359.3 %reduce-scatter.5.cloned.1.call-start = ((), (), s32[]{:S(2)}) async-start(), calls=%async_computation.6 | async-start | bytes 3932160 | tf_op jit(solution)/shard_map/reduce_scatter | solution.py:1279
  360.6 86.9 %copy-start.26 = (f32[2048]{0:T(1024)S(1)}, f32[2048]{0:T(1024)}, u32[]{:S(2)}) copy-start(f32[2048]{0:T(1024)} %reshape.208) | copy-start | bytes 24580
  447.5 9.8 %slice-start = ((s8[6291456]{0:T(1024)(128)(4,1)}), s8[4194304]{0:T(1024)(128)(4,1)S(1)}, s32[]{:S(2)}) async-start(s8[6291456]{0:T(1024)(128)(4,1)} %bitcast.47), calls=%async_computation.7 | async-start | bytes 8388608
  451.6 5.8 slice-start.1
  569.3 7.7 %copy-start.30 = (f32[2048]{0:T(1024)S(1)}, f32[2048]{0:T(1024)}, u32[]{:S(2)}) copy-start(f32[2048]{0:T(1024)} %copy-done.29) | copy-start | bytes 24580
  569.3 7.7 %copy-start.33 = (f32[1,2,2,128]{3,1,2,0:T(2,128)S(1)}, f32[1,2,2,128]{3,1,2,0:T(2,128)}, u32[]{:S(2)}) copy-start(f32[1,2,2,128]{3,1,2,0:T(2,128)} %copy-done.32) | copy-start | bytes 6148
  572.2 13.7 %copy-start.10 = (bf16[2048,512]{1,0:T(8,128)(2,1)}, bf16[2048,512]{1,0:T(8,128)(2,1)S(1)}, u32[]{:S(2)}) copy-start(bf16[2048,512]{1,0:T(8,128)(2,1)S(1)} %get-tuple-element.70.refs_2_) | copy-start | bytes 6291460
  572.4 25.6 %all-to-all-start = ((bf16[8,64,1536]{2,1,0:T(8,128)(2,1)}), bf16[8,64,1536]{2,1,0:T(8,128)(2,1)}, u32[]{:S(2)}, u32[]{:S(2)}) async-start(bf16[8,64,1536]{2,1,0:T(8,128)(2,1)} %bitcast.68), calls=%async_computation.1 | async-start | bytes 3145728 | tf_op jit(solution)/shard_map/all_to_all | solution.py:1375
  598.1 118.6 %copy-start.24 = (bf16[64,1920]{1,0:T(8,128)(2,1)S(1)}, bf16[64,1920]{1,0:T(8,128)(2,1)}, u32[]{:S(2)}) copy-start(bf16[64,1920]{1,0:T(8,128)(2,1)} %param.12) | copy-start | bytes 737284
  711.5 6.0 copy-start.34
  711.5 6.6 copy-start.35
  (19 other events, 61.9 us)
Sparse Core Ops, SparseCore 0:
  73.9 72.8 all-gather.2
  148.3 124.5 all-gather.4
  360.7 130.3 reduce-scatter.2
  562.4 74.5 reduce-scatter.4

commit v4 on v3

--- a/solution.py
+++ b/solution.py
@@ -57,9 +57,10 @@
     @pl.loop(0, KEY_VALUE_HEADS)
     def _(i):
         key, value = key_rows(i)
-        keys_in = p_ref[head_rows(QUERY_HEADS + 2 * i), :]
+        keys_in = p_ref[head_rows(QUERY_HEADS + i), :]
         kv_ref[key, :] = turned(keys_in, gain_ref[HEAD_SIZE:, :]).astype(BF16)
-        kv_ref[value, :] = p_ref[head_rows(QUERY_HEADS + 2 * i + 1), :].astype(BF16)
+        values_in = p_ref[head_rows(QUERY_HEADS + KEY_VALUE_HEADS + i), :]
+        kv_ref[value, :] = values_in.astype(BF16)
 
     @pl.loop(0, QUERY_HEADS)
     def _(i):
@@ -98,10 +99,10 @@
     @pl.loop(0, KEY_VALUE_HEADS)
     def _(i):
         key, value = key_rows(i)
-        rows = head_rows(QUERY_HEADS + 2 * i)
+        rows = head_rows(QUERY_HEADS + i)
         dv = back(p_ref[rows, :], gain_ref[HEAD_SIZE:, :], dkv_ref[key, :], slice(HEAD_SIZE, None))
         out_ref[rows, :] = dv.astype(BF16)
-        out_ref[head_rows(QUERY_HEADS + 2 * i + 1), :] = dkv_ref[value, :].astype(BF16)
+        out_ref[head_rows(QUERY_HEADS + KEY_VALUE_HEADS + i), :] = dkv_ref[value, :].astype(BF16)
 
     @pl.loop(0, QUERY_HEADS)
     def _(i):
@@ -188,11 +189,11 @@
 
     own = pltpu.make_async_copy(x_ref, out_ref.at[slots[0]], own_sem)
 
-    def begin():
-        own.start()
-        for h in (0, 1):
-            for k, peer in ((2, d_x), (4, d_y), (1, d_c)):
-                piece(k, h, peer).start()
+    def begin(h):
+        for k, peer in ((2, d_x), (4, d_y), (1, d_c)):
+            piece(k, h, peer).start()
+        if h:
+            own.start()
 
     def first():
         piece(4, 0, d_y).wait_recv()
@@ -255,10 +256,12 @@
     )
 
 
-def attend_kernel(n, rows, planes, start_ref, q_ref, kv_ref, *refs):
+def attend_kernel(n, rows, planes, out_rows, start_ref, q_ref, kv_ref, *refs):
     x_refs, refs = refs[:planes], refs[planes:]
     o_ref, lse_ref, held, *refs = refs
     out_refs, refs = refs[:planes], refs[planes:]
+    if planes:
+        full_ref, filled, *refs = refs
     o_acc, l_acc, sent, got, *refs = refs
     d, me = lax.axis_index("dp"), lax.axis_index("seq")
     length = q_ref.shape[1] // rows
@@ -287,7 +290,7 @@
             climb(step, head).start()
 
     def level(back):
-        @pl.loop(0, rows * KEY_VALUE_HEADS)
+        @pl.loop(0, rows * KEY_VALUE_HEADS, unroll=KEY_VALUE_HEADS)
         def _(i):
             tokens, wide, pair, head = spans(i, length)
             block = kv_ref[pair, tokens] if back == 0 else held[back - 1, pair, tokens]
@@ -309,7 +312,8 @@
 
     pl.when(me < n - 1)(lambda: climbs(1))
     for stages in each:
-        stages[0]()
+        stages[0](0)
+        stages[0](1)
     level(0)
     for back in range(1, n):
 
@@ -331,8 +335,22 @@
         for g in range(GROUP):
             line = slice(g, g + 1)
             part = pl.ds(wide.start + g * HEAD_SIZE, HEAD_SIZE)
-            o_ref[part, tokens] = (o_acc[part, tokens] / l_acc[head, line, tokens]).astype(BF16)
+            out = o_acc[part, tokens] / l_acc[head, line, tokens]
+            o_acc[part, tokens] = out
+            o_ref[part, tokens] = out.astype(BF16)
             lse_ref[head, line, tokens] = jnp.log(l_acc[head, line, tokens])
+
+    if planes:
+        tall = full_ref.shape[0] // 32
+        filled[...] = jnp.zeros_like(filled)
+
+        @pl.loop(0, 32)
+        def _(i):
+            src = pl.ds(pl.multiple_of(i * out_rows, 8), out_rows)
+            dst = pl.ds(pl.multiple_of(i * tall, 8), out_rows)
+            filled[dst, :] = o_acc[src, :]
+
+        full_ref[...] = filled[...].astype(BF16)
 
     for back in range(1, n):
         for head in heads:
@@ -343,7 +361,7 @@
         stages[3]()
 
 
-def attend(start, queries, pairs, rows, n, more):
+def attend(start, queries, pairs, rows, n, more, out_rows):
     vmem, dma = pl.BlockSpec(memory_space=pltpu.VMEM), pltpu.SemaphoreType.DMA
     anywhere = pl.BlockSpec(memory_space=pl.ANY)
     count = queries.shape[1]
@@ -353,7 +371,11 @@
         jax.ShapeDtypeStruct(lines, F32),
         jax.ShapeDtypeStruct((n - 1, *pairs.shape), BF16),
     ]
-    scratch = [
+    scratch, full = [], []
+    if more:
+        full = [(QW // out_rows * more[1].shape[1], count)]
+        scratch.append(pltpu.VMEM(full[0], F32))
+    scratch += [
         pltpu.VMEM(queries.shape, F32),
         pltpu.VMEM(lines, F32),
         dma((n - 1, KEY_VALUE_HEADS)),
@@ -362,14 +384,15 @@
     for extra in more:
         out_shape.append(jax.ShapeDtypeStruct((8, *extra.shape), BF16))
         scratch += [dma, dma((8, 2)), dma((8, 2))]
+    out_shape += [jax.ShapeDtypeStruct(shape, BF16) for shape in full]
     return pl.pallas_call(
-        functools.partial(attend_kernel, n, rows, len(more)),
+        functools.partial(attend_kernel, n, rows, len(more), out_rows),
         in_specs=[vmem] * 3 + [anywhere] * len(more),
-        out_specs=[vmem] * 3 + [anywhere] * len(more),
+        out_specs=[vmem] * 3 + [anywhere] * len(more) + [vmem] * len(full),
         out_shape=out_shape,
         scratch_shapes=scratch,
         compiler_params=pltpu.CompilerParams(
-            collective_id=2, has_side_effects=True, vmem_limit_bytes=40 * 2**20
+            collective_id=2, has_side_effects=True, vmem_limit_bytes=48 * 2**20
         ),
         name="attend",
     )(start, queries, pairs, *more)
@@ -385,7 +408,7 @@
 def attend_back_kernel(n, rows, summed, *refs):
     start_ref, q_ref, do_ref, o_ref, lse_ref, kv_ref, held, *refs = refs
     if summed:
-        h_ref, w_ref, *refs = refs
+        h_ref, w_ref, m_ref, *refs = refs
     dq_ref, dkv_ref, *refs = refs
     if summed:
         mixed_ref, *refs = refs
@@ -395,8 +418,9 @@
     if summed:
         place = places()
         d, me, d_c, d_x, d_y, _ = place
-        w_v, h_v, w_sem, h_sem, *refs = refs
+        w_v, h_v, m_v, w_sem, h_sem, m_sem, *refs = refs
         kept, leaving = refs[:2]
+        m_load = pltpu.make_async_copy(m_ref, m_v, m_sem)
         load, product = block_products(h_ref, h_v, h_sem, lambda h, span: dot(h, w_v[:, span]))
         load(0).start()
         w_load = pltpu.make_async_copy(w_ref, w_v, w_sem)
@@ -415,20 +439,22 @@
         def stage(i):
             if i == 0:
                 w_load.wait()
+                m_load.start()
                 pair(0, 3)
                 far()
+            elif i == 1:
                 pair(2, 1)
-            elif i == 1:
                 near(1)
                 pair(4, 2)
+                near(2)
                 pair(6, 0)
-                near(2)
                 near(0)
             elif i == 2:
                 pass_on()
             else:
                 end()
-                mixed_ref[...] = kept[0]
+                m_load.wait()
+                mixed_ref[...] = (kept[0].astype(F32) + m_v[...]).astype(BF16)
                 crossing(2, 0).wait_send()
                 crossing(0, 1).wait_send()
     else:
@@ -443,7 +469,7 @@
         )
 
     def level(back):
-        @pl.loop(0, rows * KEY_VALUE_HEADS)
+        @pl.loop(0, rows * KEY_VALUE_HEADS, unroll=2)
         def _(i):
             tokens, wide, pair, head = spans(i, length)
             block = kv_ref[pair, tokens] if back == 0 else held[back - 1, pair, tokens]
@@ -533,8 +559,10 @@
         scratch += [
             pltpu.VMEM((deep, width), BF16),
             pltpu.VMEM((2, block, deep), BF16),
+            pltpu.VMEM((block, width), F32),
             dma,
             dma((2,)),
+            dma,
             *sums_scratch(block, width),
         ]
     return pl.pallas_call(
@@ -726,25 +754,26 @@
     )(*arrays, wide)
 
 
-def weight_sums(g_ref, out_ref, refs, place):
-    kept, rcv_c, rcv_d, rcv_x, rcv_y, rcv_z, load, sent_c, got_c, sent_p, got_p, sent_z, got_z = refs
+def weight_sums(product, refs, place):
+    kept, leaving, rcv_c, rcv_d, rcv_x, rcv_y, rcv_z = refs[:7]
+    sent_c, got_c, sent_p, got_p, sent_z, got_z = refs[7:]
     d, s, d_c, d_x, d_y, line = place
     holders = (d, d_x, d_y, d_x + d_y - d)
     flip = d_c - d
     low, high = pl.ds(0, 2), pl.ds(2, 2)
 
-    def crossing(i):
-        src = g_ref.at[pl.ds((holders[i] + flip) * 4, 4)]
-        return remote(src, rcv_c.at[i], sent_c.at[i], got_c.at[i], (d_c, s))
-
-    def loading(i):
-        return pltpu.make_async_copy(
-            g_ref.at[pl.ds(holders[i] * 4, 4)], kept.at[i], load.at[i]
-        )
+    def crossing(i, slot):
+        return remote(leaving.at[slot], rcv_c.at[i], sent_c.at[i], got_c.at[i], (d_c, s))
+
+    def pair(i, slot, before=None):
+        if before is not None:
+            crossing(before, slot).wait_send()
+        product(holders[i] + flip, leaving.at[slot])
+        crossing(i, slot).start()
+        product(holders[i], kept.at[i])
 
     def merge(i):
-        loading(i).wait()
-        crossing(i).wait_recv()
+        crossing(i, 0).wait_recv()
         plus(kept.at[i], rcv_c.at[i])
 
     def push(i):
@@ -758,27 +787,22 @@
         )[i]
         return remote(src, dst, sent_p.at[i], got_p.at[i], (peer, s))
 
-    def up(b):
-        return remote(
-            kept.at[0, b], rcv_z.at[0, b], sent_z.at[0, b], got_z.at[0, b], (d, s + 1)
-        )
-
-    def down(b):
-        return remote(
-            kept.at[0, b], rcv_z.at[1, b], sent_z.at[1, b], got_z.at[1, b], (d, s - 1)
-        )
-
-    def begin():
-        for i in (3, 1, 2, 0):
-            crossing(i).start()
-            loading(i).start()
+    def straight(b):
+        return remote(kept.at[0, b], rcv_z.at[s], sent_z.at[b], got_z.at[s], (d, b))
+
+    def from_line(b):
+        return remote(kept.at[0, b], rcv_z.at[b], sent_z.at[b], got_z.at[b], (d, b))
 
     def far():
+        pair(3, 0)
+        pair(1, 1)
         merge(3)
         push(0).start()
         push(1).start()
 
     def near():
+        pair(2, 0, 3)
+        pair(0, 1, 1)
         merge(1)
         push(2).start()
         merge(2)
@@ -793,52 +817,30 @@
         plus(kept.at[1, high], rcv_d.at[high])
         push(5).start()
 
-    def send_up(b):
-        @pl.when(s > 0)
-        def _():
-            up(b).wait_recv()
-            plus(kept.at[0, b], rcv_z.at[0, b])
-
-        up(b).start()
-
-    def send_down(b):
-        @pl.when(s < 3)
-        def _():
-            down(b).wait_recv()
-            plus(kept.at[0, b], rcv_z.at[1, b])
-
-        down(b).start()
-
     def along():
         for i in (2, 3, 4, 5):
             push(i).wait_recv()
         plus(kept.at[0], rcv_x, rcv_y)
-        for b in (3, 2, 1):
-            pl.when(s < b)(functools.partial(send_up, b))
-            pl.when(s > 3 - b)(functools.partial(send_down, 3 - b))
-
-    def end():
+        for b in range(4):
+            pl.when(s != b)(lambda b=b: straight(b).start())
+
+    def end(out_ref):
         out_ref[...] = kept[0, s].astype(F32)
-
-        @pl.when(s > 0)
-        def _():
-            up(s).wait_recv()
-            out_ref[...] += rcv_z[0, s].astype(F32)
-
-        @pl.when(s < 3)
-        def _():
-            down(s).wait_recv()
-            out_ref[...] += rcv_z[1, s].astype(F32)
-
-        for b in (3, 2, 1):
-            pl.when(s < b)(lambda: up(b).wait_send())
-            pl.when(s > 3 - b)(lambda: down(3 - b).wait_send())
-        for i in range(4):
-            crossing(i).wait_send()
+        for b in range(4):
+
+            @pl.when(s != b)
+            def _(b=b):
+                from_line(b).wait_recv()
+                out_ref[...] += rcv_z[b].astype(F32)
+
+        for b in range(4):
+            pl.when(s != b)(lambda b=b: straight(b).wait_send())
+        crossing(2, 0).wait_send()
+        crossing(0, 1).wait_send()
         for i in range(6):
             push(i).wait_send()
 
-    return begin, far, near, pass_on, along, end
+    return far, near, pass_on, along, end
 
 
 def weight_sums_scratch(rows, columns):
@@ -846,18 +848,18 @@
     buffer = lambda *lead: pltpu.VMEM((*lead, rows, columns), BF16)
     return [
         buffer(4, 4),
+        buffer(2, 4),
         buffer(4, 4),
         buffer(4),
         buffer(4),
         buffer(4),
-        buffer(2, 4),
-        dma((4,)),
+        buffer(4),
         dma((4,)),
         dma((4,)),
         dma((6,)),
         dma((6,)),
-        dma((2, 4)),
-        dma((2, 4)),
+        dma((4,)),
+        dma((4,)),
     ]
 
 
@@ -868,128 +870,216 @@
     return inverse * (gy - x * jnp.mean(gy * x, axis=1, keepdims=True))
 
 
-def sum_weights_kernel(n, *refs):
-    g_refs, refs = refs[:n], refs[n:]
-    p_ref, w_ref, x_ref, dm_ref, gain_ref, back_ref, wide_ref, *refs = refs
-    out_refs, (dx_ref, wide_out, dg_ref), refs = refs[:n], refs[n : n + 3], refs[n + 3 :]
-    p_v, w_v, p_sem, w_sem, *refs = refs
+def sum_weights_kernel(n_ref, p_ref, h_ref, a_ref, few_ref, own_ref, *refs):
+    w_ref, x_ref, dm_ref, gain_ref, back_ref, wide_ref, *refs = refs
+    qkv_out, few_out, products_out, out_out, dx_ref, wide_out, dg_ref, *refs = refs
+    w_v, qkv_sum, back_v, w_sem, own_sem, sent_w, got_w, *refs = refs
     w_load = pltpu.make_async_copy(w_ref, w_v, w_sem)
-    p_load = pltpu.make_async_copy(p_ref, p_v, p_sem)
     w_load.start()
-    p_load.start()
     place = places()
     d, s, d_c, d_x, d_y, line = place
-    greet([(d_c, s), (d_x, s), (d_y, s)], (d, s))
-    each = [
-        weight_sums(g_refs[i], out_refs[i], refs[13 * i : 13 * i + 13], place) for i in range(n)
-    ]
+    flip, d_d = d_c - d, d_x + d_y - d
+    plane = (d, d_c, d_x, d_x + flip, d_y, d_y + flip, d_d, d_d + flip)
+    greet([(other, s) for other in plane[1:]] + [(d, (s + i) % 4) for i in (1, 2, 3)])
+
+    def exchange(k):
+        src, dst = back_ref.at[plane[k]], back_v.at[d]
+        if k == 0:
+            return pltpu.make_async_copy(src, dst, own_sem)
+        return remote(src, dst, sent_w.at[k], got_w.at[k], (plane[k], s))
+
+    width, chunk = p_ref.shape[0], 512
+
+    def chunks(make, dst):
+        @pl.loop(0, width // chunk)
+        def _(c):
+            span = pl.ds(pl.multiple_of(c * chunk, chunk), chunk)
+            dst[:, :, span] = make(span).astype(BF16).reshape(*dst.shape[:2], chunk)
+
+    def qkv_product(k, dst):
+        tall = dst.shape[0] * dst.shape[1]
+        rows = n_ref[:, pl.ds(pl.multiple_of(k * tall, tall), tall)].T
+        chunks(lambda span: back_product(rows, p_ref[span, :]), dst)
+        for b in range(4):
+            dst[b, :16, -128:] = few_ref[k * 4 + b]
+
+    def out_product(k, dst):
+        tall = dst.shape[0] * dst.shape[1]
+        rows = h_ref[pl.ds(pl.multiple_of(k * tall, 16), tall), :]
+        chunks(lambda span: dot(rows, a_ref[:, span]), dst)
+
+    far, near, pass_on, along, end = weight_sums(qkv_product, refs[:13], place)
+    far_2, near_2, pass_on_2, along_2, end_2 = weight_sums(out_product, refs[13:], place)
     block = 128
 
-    def body(x_tile, dm_tile, dx_tile):
-        i = pl.program_id(0) + offset
-        span = pl.ds(pl.multiple_of(i * block, block), block)
-        dy = back_product(p_v[:, span].T, w_v[...])
-        dx_tile[...] = dm_tile[...] + normed_back(dy, x_tile[...].astype(F32), gain_ref[...])
-
-    count = x_ref.shape[0] // block
-    half = count // 2
-    spec = lambda: pl.BlockSpec((block, x_ref.shape[1]), lambda i: (i + offset, 0))
-    for i in range(6):
-        for stages in each:
-            stages[i]()
-        if i == 0:
-            w_load.wait()
-            p_load.wait()
-        if i in (1, 2):
-            offset = (i - 1) * half
-            pltpu.emit_pipeline(
-                body, grid=(half,), in_specs=[spec(), spec()], out_specs=[spec()]
-            )(x_ref, dm_ref, dx_ref)
-        if i == 3:
-            part = back_ref.shape[2] // 2
-            total = jnp.zeros((dg_ref.shape[0], 1), F32)
-            for j in range(16):
-                half_j, holder = j // 8, j % 8
-                span = slice(j * part, (j + 1) * part)
-                grad = back_ref[holder, :, half_j * part : (half_j + 1) * part].astype(F32)
-                wide_out[:, span] = grad
-                total += jnp.sum(grad * wide_ref[:, span].astype(F32), axis=1, keepdims=True)
-            dg_ref[...] = jnp.broadcast_to(total, dg_ref.shape)
-
-
-def sum_weights(arrays, dprojected, w, x, dmiddle, gain, back, wide):
+    def token_grads(first, count):
+        def body(x_tile, dm_tile, dx_tile):
+            i = pl.program_id(0) + first
+            span = pl.ds(pl.multiple_of(i * block, block), block)
+            dy = back_product(p_ref[:, span].T, w_v[...])
+            dx_tile[...] = dm_tile[...] + normed_back(dy, x_tile[...].astype(F32), gain_ref[...])
+
+        spec = lambda: pl.BlockSpec((block, x_ref.shape[1]), lambda i: (i + first, 0))
+        pltpu.emit_pipeline(body, grid=(count,), in_specs=[spec(), spec()], out_specs=[spec()])(
+            x_ref, dm_ref, dx_ref
+        )
+
+    blocks = x_ref.shape[0] // block
+    far()
+    near()
+    w_load.wait()
+    token_grads(0, 1)
+    pass_on()
+    far_2()
+    near_2()
+    token_grads(1, 2)
+    along()
+    pass_on_2()
+    for k in range(8):
+        exchange(k).start()
+    token_grads(3, blocks - 3)
+    along_2()
+    end(qkv_sum)
+    exchange(0).wait()
+    for k in range(1, 8):
+        exchange(k).wait_recv()
+        exchange(k).wait_send()
+    part = back_v.shape[2] // 2
+    total = jnp.zeros((dg_ref.shape[0], 1), F32)
+    for j in range(16):
+        half_j, holder = j // 8, j % 8
+        span = slice(j * part, (j + 1) * part)
+        grad = back_v[holder, :, half_j * part : (half_j + 1) * part].astype(F32)
+        wide_out[:, span] = grad
+        total += jnp.sum(grad * wide_ref[:, span].astype(F32), axis=1, keepdims=True)
+    dg_ref[...] = jnp.broadcast_to(total, dg_ref.shape)
+    inner = QW + 2 * KW
+    total = jnp.sum(qkv_sum[:, :inner] * own_ref[:, :inner].astype(F32), axis=1, keepdims=True)
+    products_out[...] = jnp.broadcast_to(total, products_out.shape)
+    few_out[...] = qkv_sum[:16, inner:]
+    qkv_out[...] = qkv_sum[:, :inner]
+    end_2(out_out)
+
+
+def sum_weights(normed, dprojected, heads, dattend, few, own, w, x, dmiddle, gain, back, wide):
     dma, anywhere = pltpu.SemaphoreType.DMA, pl.BlockSpec(memory_space=pl.ANY)
     vmem = pl.BlockSpec(memory_space=pltpu.VMEM)
-    n = len(arrays)
-    scratch = [pltpu.VMEM(dprojected.shape, BF16), pltpu.VMEM(w.shape, BF16), dma, dma]
-    for g in arrays:
-        scratch += weight_sums_scratch(*g.shape[1:])
+    rows, width = own.shape
+    tall = heads.shape[0] // 32
+    scratch = [
+        pltpu.VMEM(w.shape, BF16),
+        pltpu.VMEM(own.shape, F32),
+        pltpu.VMEM(back.shape, BF16),
+        dma,
+        dma,
+        dma((8,)),
+        dma((8,)),
+    ]
+    scratch += weight_sums_scratch(rows, width) + weight_sums_scratch(tall, width)
     return pl.pallas_call(
-        functools.partial(sum_weights_kernel, n),
-        out_shape=[jax.ShapeDtypeStruct(g.shape[1:], F32) for g in arrays]
-        + [
+        sum_weights_kernel,
+        out_shape=[
+            jax.ShapeDtypeStruct((rows, QW + 2 * KW), F32),
+            jax.ShapeDtypeStruct((16, width - QW - 2 * KW), F32),
+            jax.ShapeDtypeStruct((rows, 128), F32),
+            jax.ShapeDtypeStruct((tall, width), F32),
             jax.ShapeDtypeStruct(dmiddle.shape, F32),
             jax.ShapeDtypeStruct(wide.shape, F32),
-            jax.ShapeDtypeStruct((wide.shape[0], 128), F32),
+            jax.ShapeDtypeStruct((rows, 128), F32),
         ],
-        in_specs=[anywhere] * (n + 4) + [vmem] * 3,
-        out_specs=[vmem] * n + [anywhere, vmem, vmem],
+        in_specs=[vmem] * 6 + [anywhere] * 3 + [vmem, anywhere, vmem],
+        out_specs=[vmem] * 4 + [anywhere, vmem, vmem],
         scratch_shapes=scratch,
         compiler_params=pltpu.CompilerParams(
-            collective_id=6, has_side_effects=True, vmem_limit_bytes=60 * 2**20
+            collective_id=6, has_side_effects=True, vmem_limit_bytes=63 * 2**20
         ),
         name="sum_weights",
-    )(*arrays, dprojected, w, x, dmiddle, gain, back, wide)
-
-
-def plane_kernel(x_ref, g_ref, w_ref, out_ref, dh_ref, w_v, w_sem, own_sem, sent, got):
+    )(normed, dprojected, heads, dattend, few, own, w, x, dmiddle, gain, back, wide)
+
+
+def plane_kernel(rows, heads_ref, w_ref, x_ref, gain_ref, g_ref, down_ref, *refs):
+    out_ref, dh_ref, mid_ref, w_v, x_v, down_v, mid_v, n_v, load, mid_sem, *refs = refs
     place = places()
     d, s, d_c, d_x, d_y, line = place
-    load = pltpu.make_async_copy(w_ref, w_v, w_sem)
-    load.start()
+    w_load = pltpu.make_async_copy(w_ref, w_v, load.at[0])
+    x_load = pltpu.make_async_copy(x_ref, x_v, load.at[1])
+    down_load = pltpu.make_async_copy(down_ref, down_v, load.at[2])
+    w_load.start()
+    x_load.start()
+    down_load.start()
     greet([(d_c, s), (d_x, s), (d_y, s)])
-    begin, first, second, end = plane_stages(x_ref, out_ref, own_sem, sent, got, place)
-    begin()
-    load.wait()
+    begin, first, second, end = plane_stages(n_v, out_ref, *refs, place)
+    w_load.wait()
+    x_load.wait()
+    width, chunk = mid_v.shape[1], 512
+
+    def stored(row):
+        tokens = pl.ds(row * (mid_v.shape[0] // rows), mid_v.shape[0] // rows)
+        return pltpu.make_async_copy(mid_v.at[tokens], mid_ref.at[tokens], mid_sem.at[row])
+
+    for row in range(rows):
+        tokens = slice(row * (mid_v.shape[0] // rows), (row + 1) * (mid_v.shape[0] // rows))
+        heads = heads_ref[:, tokens].T
+
+        @pl.loop(0, width // chunk)
+        def _(c):
+            span = pl.ds(pl.multiple_of(c * chunk, chunk), chunk)
+            weight = w_v[:, :, :, span].reshape(heads.shape[1], chunk)
+            mid_v[tokens, span] = x_v[tokens, span].astype(F32) + dot(heads, weight)
+
+        stored(row).start()
+        mid = mid_v[tokens, :]
+        inverse = lax.rsqrt(jnp.mean(mid * mid, axis=1, keepdims=True) + epsilon)
+        n_v[tokens, :] = (mid * inverse * gain_ref[...]).astype(BF16)
+        begin(row)
+    down_load.wait()
 
     def body(g_tile, dh_tile):
-        dh_tile[...] = back_product(g_tile[...], w_v[...]).astype(BF16)
-
-    def some(start, count):
-        pltpu.emit_pipeline(
-            body,
-            grid=(count,),
-            in_specs=[pl.BlockSpec((512, w_v.shape[1]), lambda i: (start + i, 0))],
-            out_specs=[pl.BlockSpec((512, w_v.shape[0]), lambda i: (start + i, 0))],
-        )(g_ref, dh_ref)
-
-    blocks = g_ref.shape[0] // 512
-    some(0, blocks)
+        dh_tile[...] = back_product(g_tile[...], down_v[...]).astype(BF16)
+
+    pltpu.emit_pipeline(
+        body,
+        grid=(g_ref.shape[0] // 512,),
+        in_specs=[pl.BlockSpec((512, down_v.shape[1]), lambda i: (i, 0))],
+        out_specs=[pl.BlockSpec((512, down_v.shape[0]), lambda i: (i, 0))],
+    )(g_ref, dh_ref)
     first()
     second()
     end()
-
-
-def plane_gather_now(x, g, w, n_dp, n_seq):
-    if (n_dp, n_seq) != (8, 4):
-        everyone = lax.all_gather(x, "dp", axis=0, tiled=True)
-        return everyone, back_product(g, w).astype(BF16)
+    for row in range(rows):
+        stored(row).wait()
+
+
+def plane_gather(heads, w, x, gain, g, down):
     dma, anywhere = pltpu.SemaphoreType.DMA, pl.BlockSpec(memory_space=pl.ANY)
-    everyone, dhidden = pl.pallas_call(
-        plane_kernel,
+    vmem = pl.BlockSpec(memory_space=pltpu.VMEM)
+    everyone, dhidden, middle = pl.pallas_call(
+        functools.partial(plane_kernel, 2),
         out_shape=[
-            jax.ShapeDtypeStruct((n_dp, *x.shape), x.dtype),
-            jax.ShapeDtypeStruct((g.shape[0], w.shape[0]), BF16),
+            jax.ShapeDtypeStruct((8, *x.shape), BF16),
+            jax.ShapeDtypeStruct((g.shape[0], down.shape[0]), BF16),
+            jax.ShapeDtypeStruct(x.shape, F32),
         ],
-        in_specs=[anywhere] * 3,
-        out_specs=[anywhere] * 2,
-        scratch_shapes=[pltpu.VMEM(w.shape, BF16), dma, dma, dma((8, 2)), dma((8, 2))],
+        in_specs=[vmem, anywhere, anywhere, vmem, anywhere, anywhere],
+        out_specs=[anywhere] * 3,
+        scratch_shapes=[
+            pltpu.VMEM(w.shape, BF16),
+            pltpu.VMEM(x.shape, BF16),
+            pltpu.VMEM(down.shape, BF16),
+            pltpu.VMEM(x.shape, F32),
+            pltpu.VMEM(x.shape, BF16),
+            dma((3,)),
+            dma((2,)),
+            dma,
+            dma((8, 2)),
+            dma((8, 2)),
+        ],
         compiler_params=pltpu.CompilerParams(
-            collective_id=4, has_side_effects=True, vmem_limit_bytes=40 * 2**20
+            collective_id=4, has_side_effects=True, vmem_limit_bytes=48 * 2**20
         ),
         name="plane_gather",
-    )(x, g, w)
-    return everyone.reshape(n_dp * x.shape[0], x.shape[1]), dhidden
+    )(heads, w, x, gain, g, down)
+    return everyone.reshape(8 * x.shape[0], x.shape[1]), dhidden, middle
 
 
 def transposed_kernel(x_ref, g_ref, out_ref):
@@ -1144,8 +1234,8 @@
     pair(2, 1)
     pair(4, 2)
     near(1)
+    near(2)
     pair(6, 0)
-    near(2)
     near(0)
     h_load.wait()
 
@@ -1299,14 +1389,11 @@
 
     full = (n_dp, n_seq) == (8, 4)
     qkv_w = w_qkv.shape[1]
-    paired = w_qkv[:, QW:].reshape(wr, 2, KEY_VALUE_HEADS, HEAD_SIZE).transpose(0, 2, 1, 3)
     spare = width - qkv_w
     gains = jnp.concatenate([attn_gain, ffn_gain])
     gains = [jnp.pad(g, (0, spare - g.shape[0]))[None] for g in (gains, head_gains)]
     gains.append(jnp.zeros((wr - 2, spare), BF16))
-    own_qkv = jnp.concatenate(
-        [w_qkv[:, :QW], paired.reshape(wr, 2 * KW), jnp.concatenate(gains, axis=0)], axis=1
-    )
+    own_qkv = jnp.concatenate([w_qkv, jnp.concatenate(gains, axis=0)], axis=1)
     out_rows = w_out.shape[0]
     own_out = jnp.pad(w_out, ((0, -out_rows % 16), (0, 0)))
     all_qkv, some_out, spread = gather_weights(own_qkv, [own_out], w_gate_up, n_dp, n_seq)
@@ -1327,22 +1414,25 @@
 
     queries, pairs = prepare(projected, head_full[:, None], cosine, sine)
     more = [cotangent_low, some_out] if full else []
-    heads_out, lse, held, *planes = attend(start, queries, pairs, rows, n_seq, more)
+    heads_out, lse, held, *planes = attend(start, queries, pairs, rows, n_seq, more, out_rows)
     gate_up_w = gather(spread.reshape(n_dp * wr, 2 * part), "seq")
     if full:
-        cotangent_all = planes[0].reshape(n_dp * count, width)
-        all_out = planes[1].reshape(n_dp * n_seq, -1, width)
+        cotangent_all, all_out, heads_full = planes
+        cotangent_all = cotangent_all.reshape(n_dp * count, width)
+        out_full = all_out.reshape(-1, width)
+        normed2_all, dhidden, middle = plane_gather(
+            heads_full, all_out, tokens.reshape(count, width), ffn_gain_full[None],
+            cotangent_all, down_w,
+        )
     else:
         cotangent_all, all_out = gather(cotangent_low, "dp"), some_out
-    out_full = all_out.reshape(-1, width)
-    fill = ((0, 0), (0, all_out.shape[1] - out_rows), (0, 0))
-    heads_full = jnp.pad(heads_out.reshape(n_dp * n_seq, out_rows, count), fill)
-    heads_full = heads_full.reshape(-1, count)
-    middle = x_rows + outer_sum(heads_full, out_full)
-    normed2, norm2_pull = jax.vjp(norm_rows, middle, ffn_gain_full)
-    normed2_all, dhidden = plane_gather_now(
-        normed2.astype(BF16), cotangent_all, down_w, n_dp, n_seq
-    )
+        out_full = all_out.reshape(-1, width)
+        fill = ((0, 0), (0, all_out.shape[1] - out_rows), (0, 0))
+        heads_full = jnp.pad(heads_out.reshape(n_dp * n_seq, out_rows, count), fill)
+        heads_full = heads_full.reshape(-1, count)
+        middle = x_rows + outer_sum(heads_full, out_full)
+        normed2_all = gather(norm_rows(middle, ffn_gain_full).astype(BF16), "dp")
+        dhidden = back_product(cotangent_all, down_w).astype(BF16)
     hidden, dgate_up = gate_up_product(normed2_all, dhidden, gate_up_w, n_dp, n_seq)
     gate_up_grad = transposed_product(normed2_all, dgate_up, n_dp, n_seq)
     gate_up_grad, dgate_up = lax.optimization_barrier((gate_up_grad, dgate_up))
@@ -1356,66 +1446,70 @@
         down_grad = outer_sum(hidden, cotangent_all).astype(BF16)
     dnormed2 = dnormed2.astype(F32)
 
-    dmiddle_norm = norm2_pull(dnormed2)[0]
-    dmiddle = cotangent_low.astype(F32) + dmiddle_norm
+    dmiddle = cotangent_low.astype(F32) + normed_back(dnormed2, middle, ffn_gain_full)
     dattend = dmiddle.astype(BF16)
     dheads = back_product(out_full, dattend).astype(BF16).reshape(n_dp * n_seq, -1, count)
     dheads = dheads[:, :out_rows].reshape(QW, count)
     if full:
         dqueries, dpairs, mixed = attend_back(
-            start, queries, dheads, heads_out, lse, pairs, held, rows, n_seq, [hidden, down_w]
+            start, queries, dheads, heads_out, lse, pairs, held, rows, n_seq,
+            [hidden, down_w, middle],
         )
     else:
         dqueries, dpairs = attend_back(
             start, queries, dheads, heads_out, lse, pairs, held, rows, n_seq, []
         )
-        mixed = scatter(mm(hidden, down_w).astype(BF16), "dp")
-    mixed = middle + mixed.astype(F32)
+        mixed = middle + scatter(mm(hidden, down_w).astype(BF16), "dp").astype(F32)
     gate_up_grad, dqueries = lax.optimization_barrier((gate_up_grad, dqueries))
-    gate_up_grad = lax.all_to_all(
-        gate_up_grad.reshape(n_dp, wr, 2 * part), "dp", 0, 0, tiled=True
-    )
+    gate_up_grad = gate_up_grad.reshape(n_dp, wr, 2 * part)
     down_grad, dqueries = lax.optimization_barrier((down_grad, dqueries))
     down_grad = scatter(down_grad, "seq")
     dprojected_low, head_grad = prepare_back(
         projected, head_full[:, None], cosine, sine, dqueries, dpairs
     )
-    qkv_grad = lax.dot_general(
-        normed_low, dprojected_low, (((0,), (1,)), ((), ())), preferred_element_type=F32
-    ).astype(BF16)
     few = head_gains.shape[0]
-    head_grad = head_grad.astype(BF16).reshape(n_dp * n_seq, 1, few)
-    qkv_grad = lax.dynamic_update_slice(
-        qkv_grad.reshape(n_dp * n_seq, wr, width), head_grad, (0, 0, qkv_w)
-    )
-    dattend, qkv_grad = lax.optimization_barrier((dattend, qkv_grad))
-    out_grads = mm(heads_full, dattend).astype(BF16).reshape(n_dp * n_seq, -1, width)
     if full:
-        qkv_grad, out_weight_grad, tokens_grad, gate_up_grad, ffn_products = sum_weights(
-            [qkv_grad, out_grads],
-            dprojected_low,
-            qkv_full,
-            tokens.reshape(count, width),
-            dmiddle,
-            attn_gain_full[None],
-            gate_up_grad,
-            w_gate_up,
+        few_rows = jnp.pad(head_grad.reshape(-1, few, 1), ((0, 0), (0, 16 - few), (0, 0)))
+        few_rows = jnp.broadcast_to(few_rows.astype(BF16), (n_dp * n_seq, 16, width - qkv_w))
+        qkv_grad, head_rows_out, qkv_products, out_weight_grad, tokens_grad, gate_up_grad, ffn_products = (
+            sum_weights(
+                normed_low,
+                dprojected_low,
+                heads_full,
+                dattend,
+                few_rows,
+                own_qkv,
+                qkv_full,
+                tokens.reshape(count, width),
+                dmiddle,
+                attn_gain_full[None],
+                gate_up_grad,
+                w_gate_up,
+            )
         )
-        ffn_products = ffn_products[:, 0]
+        head_out, ffn_products, qkv_products = (
+            head_rows_out[:few, 0], ffn_products[:, 0], qkv_products[:, 0]
+        )
     else:
+        qkv_grad = lax.dot_general(
+            normed_low, dprojected_low, (((0,), (1,)), ((), ())), preferred_element_type=F32
+        ).astype(BF16)
+        out_grads = mm(heads_full, dattend).astype(BF16)
         qkv_grad, out_weight_grad = (
-            scatter(scatter(g.reshape(-1, width), "dp"), "seq").astype(F32)
-            for g in (qkv_grad, out_grads)
+            scatter(scatter(g, "dp"), "seq").astype(F32) for g in (qkv_grad, out_grads)
         )
+        head_out = jnp.sum(
+            lax.all_to_all(head_grad.reshape(-1, few), BOTH, 0, 0, tiled=True), axis=0
+        )
+        qkv_products = jnp.sum(own_qkv[:, :qkv_w].astype(F32) * qkv_grad[:, :qkv_w], axis=1)
+        qkv_grad = qkv_grad[:, :qkv_w]
+        gate_up_grad = lax.all_to_all(gate_up_grad, "dp", 0, 0, tiled=True)
         gate_up_grad = gate_up_grad.reshape(n_dp, wr, 2, part).transpose(1, 2, 0, 3)
         gate_up_grad = gate_up_grad.reshape(wr, 2 * ff).astype(F32)
         ffn_products = jnp.sum(w_gate_up.astype(F32) * gate_up_grad, axis=1)
         dnormed = back_product(dprojected_low.T, qkv_full)
         tokens_grad = dmiddle + normed_back(dnormed, x_rows, attn_gain_full)
-    head_out = qkv_grad[0, qkv_w : qkv_w + few]
-    unpaired = qkv_grad[:, QW:qkv_w].reshape(wr, KEY_VALUE_HEADS, 2, HEAD_SIZE).transpose(0, 2, 1, 3)
-    qkv_grad = jnp.concatenate([qkv_grad[:, :QW], unpaired.reshape(wr, 2 * KW)], axis=1)
-    attn_gain_out = jnp.sum(w_qkv.astype(F32) * qkv_grad, axis=1) / attn_gain.astype(F32)
+    attn_gain_out = qkv_products / attn_gain.astype(F32)
     ffn_gain_out = ffn_products / ffn_gain.astype(F32)
     return (
         mixed.astype(BF16).reshape(rows, length, width),

time: 742 us -> 699 us (0.942)
  matrix products: 37 us -> 11.5 us
    dot_general x3 -> x0, matrix products: 26.1 us -> none  [the longest x1 9.02 us: outer_sum(): lax.dot_general(left, right, (((0,), (0,)), ((), ())), preferred_element_...]
    unnamed x81 -> x68, local copies, waits for them, and re-layouts: 19.8 us -> 22 us
  transfers between devices with their start and end apart: 5 -> 4, of which waited for: 1 -> 0; matrix products, arithmetic and copies ran while one was open for 10% -> 5% of each run, Pallas kernels for 65% -> 69%
where the time goes in v4:
time: 699 us; the launch traced here: 690 us
  Pallas kernels  608 us (87%)
  local copies, waits for them, and re-layouts  32.5 us (5%)
  other arithmetic  22.2 us (3%)
  between operations  14.6 us (2%)
  matrix products  11.5 us (2%)
    pallas_call x1, Pallas kernels, sum_weights(): pl.pallas_call(sum_weights_kernel, out_shape=[jax.ShapeDtypeStruct((rows,...  103 us
    pallas_call x1, Pallas kernels, attend_back(): pl.pallas_call(functools.partial(attend_back_kernel, n, rows, bool(more))...  101 us
    pallas_call x1, Pallas kernels, attend(): pl.pallas_call(functools.partial(attend_kernel, n, rows, len(more), out_r...  101 us
    pallas_call x1, Pallas kernels, plane_sum(): pl.pallas_call(plane_sum_kernel, out_shape=[jax.ShapeDtypeStruct((rows, w...  84.4 us
    pallas_call x1, Pallas kernels, plane_gather(): pl.pallas_call(functools.partial(plane_kernel, 2), out_shape=[jax.ShapeDt...  80.5 us
    pallas_call x1, Pallas kernels, gather_weights(): pl.pallas_call(functools.partial(weights_kernel, n), out_shape=[jax.Shape...  60.9 us
    pallas_call x1, Pallas kernels, gate_up_product(): pl.pallas_call(functools.partial(gate_up_kernel, n_dp, n_seq), grid=(toke...  37.6 us
    pallas_call x1, Pallas kernels, transposed_product(): pl.pallas_call(transposed_kernel, grid=(width // tall,), in_specs=[pl.Blo...  33.8 us
  transfers between devices with their start and end apart: 4, of which 0 were waited for; matrix products, arithmetic and copies ran while one was open for 5% of the time, Pallas kernels for 69%

profile of v4, /device:TPU:0, one launch (start us, length us, event | category | flops | bytes accessed | tf_op | source)
XLA Modules:
  0.0 689.9 jit_solution(4527851483153325874)
XLA Ops:
  7.2 1.7 pad.14.refs_1_
  9.8 1.7 maximum_maximum_fusion.refs_0_.own_ref
  11.4 60.9 %gather_weights.1 = (bf16[32,64,2048]{2,1,0:T(8,128)(2,1)}, bf16[4,48,2048]{2,1,0:T(8,128)(2,1)}, bf16[8,64,1536]{2,1,0:T(8,128)(2,1)}) custom-call(bf16[64,2048]{1,0:T(8,128)(2,1)} %maximum_maximum_fusion.refs_0_.own_ref, bf16[48,2048]{1,0:T(8,128)(2,1)} %pad.14.refs_1_, bf16[64,12288]{1,0:T(8,128)(2,1)} %refs_5_.1), custom_call_target="tpu_custom_call" | custom-call | tf_op jit(solution)/shard_map/gather_weights/pallas_call | solution.py:731
  78.3 8.0 %fusion.4.p_ref = f32[2048,512]{1,0:T(8,128)S(1)} fusion(bf16[2048,2048]{1,0:T(8,128)(2,1)} %bitcast.37, bf16[512,2048]{1,0:T(8,128)(2,1)S(1)} %multiply_convert_fusion.n_ref), kind=kOutput, calls=%fused_computation.33 | convolution fusion | flops 4294967296 | bytes 14680064 | tf_op jit(solution)/shard_map/dot_general | solution.py:1411
  86.3 2.4 prepare.1
  88.7 2.0 copy-done.1
  90.8 100.6 %attend.1 = (bf16[1280,512]{1,0:T(8,128)(2,1)S(1)}, f32[5,8,512]{2,1,0:T(8,128)S(1)}, bf16[3,640,512]{2,1,0:T(8,128)(2,1)}, bf16[8,512,2048]{2,1,0:T(8,128)(2,1)...) custom-call(s32[8,512]{1,0:T(8,128)S(1)} %broadcast_in_dim.29.start_ref.refs_0_, ...), custom_call_target="tpu_custom_call" | custom-call | tf_op jit(solution)/shard_map/attend/pallas_call | solution.py:388
  195.1 1.4 copy-done.4
  197.2 80.5 %plane_gather.1 = (bf16[8,512,2048]{2,1,0:T(8,128)(2,1)}, bf16[4096,768]{1,0:T(8,128)(2,1)}, f32[512,2048]{1,0:T(8,128)}) custom-call(bf16[1536,512]{1,0:T(8,128)(2,1)S(1)} %copy-done.4, bf16[8,4,48,2048]{3,2,1,0:T(8,128)(2,1)} %get-tuple-element.52.w_ref, bf16[512,2048]{1,0:T(8,128)(2,1)S(1)} %bitcast.34, f32[1,2048]{1,0:T(1,128)S(1)} %copy-done.16, ...), custom_call_target="tpu_custom_call" | custom-call | tf_op jit(solution)/shard_map/plane_gather/pallas_call | solution.py:1056
  277.8 37.6 %gate_up.1 = (bf16[4096,768]{1,0:T(8,128)(2,1)}, bf16[4096,1536]{1,0:T(8,128)(2,1)}) custom-call(bf16[4096,2048]{1,0:T(8,128)(2,1)} %bitcast.55, bf16[4096,768]{1,0:T(8,128)(2,1)} %get-tuple-element.58.dh_ref, bf16[2048,1536]{1,0:T(8,128)(2,1)} %all-gather.5.cloned.1.call-done.w_ref), custom_call_target="tpu_custom_call" | custom-call | flops 25769803776 | bytes 48234496 | tf_op jit(solution)/shard_map/gate_up/pallas_call | solution.py:1332
  315.4 33.8 %transposed_product.1 = bf16[4,8,64,1536]{3,2,1,0:T(8,128)(2,1)} custom-call(bf16[4096,2048]{1,0:T(8,128)(2,1)} %bitcast.56, bf16[4096,1536]{1,0:T(8,128)(2,1)} %get-tuple-element.61.g_ref), custom_call_target="tpu_custom_call" | custom-call | flops 25769803776 | bytes 35651584 | tf_op jit(solution)/shard_map/transposed_product/pallas_call | solution.py:1095
  350.8 2.5 multiply_reduce_fusion.1
  353.4 84.4 %plane_sum.1 = (bf16[512,2048]{1,0:T(8,128)(2,1)}, bf16[768,2048]{1,0:T(8,128)(2,1)}) custom-call(bf16[4096,1536]{1,0:T(8,128)(2,1)} %get-tuple-element.61.g_ref, bf16[2048,1536]{1,0:T(8,128)(2,1)} %all-gather.5.cloned.1.call-done.w_ref, bf16[4096,768]{1,0:T(8,128)(2,1)} %get-tuple-element.62.h_ref.refs_7_, bf16[4096,2048]{1,0:T(8,128)(2,1)} %bitcast.36), custom_call_target="tpu_custom_call" | custom-call | tf_op jit(solution)/shard_map/plane_sum/pallas_call | solution.py:1270
  437.8 3.8 multiply_reduce_fusion
  442.6 5.2 fusion.3
  447.8 3.5 convolution_convert_fusion
  452.5 101.1 %attend_back.1 = (f32[1280,512]{1,0:T(8,128)}, f32[640,512]{1,0:T(8,128)}, bf16[512,2048]{1,0:T(8,128)(2,1)}) custom-call(s32[8,512]{1,0:T(8,128)} %copy-done.14, bf16[1280,512]{1,0:T(8,128)(2,1)} %copy-done.5, bf16[1280,512]{1,0:T(8,128)(2,1)} %bitcast.44, bf16[1280,512]{1,0:T(8,128)(2,1)} %copy-done.9, f32[5,8,512]{2,1,0:T(8,128)} %copy-done.15, ...), custom_call_target="tpu_custom_call" | custom-call | tf_op jit(solution)/shard_map/attend_back/pallas_call | solution.py:568
  555.3 2.2 copy-done.2
  558.8 3.1 prepare_back.1
  564.3 103.2 %sum_weights.1 = (f32[64,1920]{1,0:T(8,128)}, f32[16,128]{1,0:T(8,128)}, f32[64,128]{1,0:T(8,128)}, f32[48,2048]{1,0:T(8,128)}, f32[512,2048]{1,0:T(8,128)}, /*index=5*/f32[64,12288]{1,0:T(8,128)}, f32[64,128]{1,0:T(8,128)}) custom-call(bf16[512,2048]{1,0:T(8,128)(2,1)} %copy-done.18, bf16[2048,512]{1,0:T(8,128)(2,1)} %copy-done.8, ...), custom_call_target="tpu_custom_call" | custom-call | tf_op jit(solution)/shard_map/sum_weights/pallas_call | solution.py:979
  667.5 1.9 slice.33
  673.5 2.6 convert_element_type.113
  677.4 2.1 copy.32
  681.2 1.7 copy.34
  (108 shorter events, 27.2 us)
Async XLA Ops:
  7.2 67.2 %copy-start = (bf16[2,256,2048]{2,1,0:T(8,128)(2,1)S(1)}, bf16[2,256,2048]{2,1,0:T(8,128)(2,1)}, u32[]{:S(2)}) copy-start(bf16[2,256,2048]{2,1,0:T(8,128)(2,1)} %param.10) | copy-start | bytes 6291460
  7.2 68.6 %copy-start.26 = (s32[2,4]{1,0:T(2,128)S(1)}, s32[2,4]{1,0:T(2,128)}, u32[]{:S(2)}) copy-start(s32[2,4]{1,0:T(2,128)} %param.11) | copy-start | bytes 100
  7.2 187.9 %all-gather.3.cloned.1.call-start = ((), (), s32[]{:S(2)}) async-start(), calls=%async_computation.2 | async-start | bytes 3932160 | tf_op jit(solution)/shard_map/all_gather | solution.py:1365
  72.4 205.3 %all-gather.5.cloned.1.call-start = ((), (), s32[]{:S(2)}) async-start(), calls=%async_computation.3 | async-start | bytes 7864320 | tf_op jit(solution)/shard_map/all_gather | solution.py:1365
  73.2 480.5 %reduce-scatter.3.cloned.1.call-start = ((), (), s32[]{:S(2)}) async-start(), calls=%async_computation.4 | async-start | bytes 7864320 | tf_op jit(solution)/shard_map/reduce_scatter | solution.py:1369
  77.7 8.6 %copy-start.12 = (f32[32,512]{1,0:T(8,128)}, f32[32,512]{1,0:T(8,128)S(1)}, u32[]{:S(2)}) copy-start(f32[32,512]{1,0:T(8,128)S(1)} %get-tuple-element.92.cos_ref) | copy-start | bytes 196612
  78.2 8.0 %copy-start.18 = (bf16[512,2048]{1,0:T(8,128)(2,1)}, bf16[512,2048]{1,0:T(8,128)(2,1)S(1)}, u32[]{:S(2)}) copy-start(bf16[512,2048]{1,0:T(8,128)(2,1)S(1)} %multiply_convert_fusion.n_ref) | copy-start | bytes 6291460
  86.3 4.4 copy-start.25
  86.3 4.4 copy-start.11
  90.7 187.0 %copy-start.5 = (bf16[1280,512]{1,0:T(8,128)(2,1)}, bf16[1280,512]{1,0:T(8,128)(2,1)S(1)}, u32[]{:S(2)}) copy-start(bf16[1280,512]{1,0:T(8,128)(2,1)S(1)} %get-tuple-element.49.q_ref.refs_1_) | copy-start | bytes 3932164
  90.7 187.0 %copy-start.14 = (s32[8,512]{1,0:T(8,128)}, s32[8,512]{1,0:T(8,128)S(1)}, u32[]{:S(2)}) copy-start(s32[8,512]{1,0:T(8,128)S(1)} %broadcast_in_dim.29.start_ref.refs_0_) | copy-start | bytes 49156
  349.3 324.2 %reduce-scatter.5.cloned.1.call-start = ((), (), s32[]{:S(2)}) async-start(), calls=%async_computation.5 | async-start | bytes 3932160 | tf_op jit(solution)/shard_map/reduce_scatter | solution.py:1369
  437.8 4.2 copy-start.17
  437.8 4.8 copy-start.20
  437.8 10.0 %slice-start = ((s8[6291456]{0:T(1024)(128)(4,1)}), s8[4194304]{0:T(1024)(128)(4,1)S(1)}, s32[]{:S(2)}) async-start(s8[6291456]{0:T(1024)(128)(4,1)} %bitcast.41), calls=%async_computation.6 | async-start | bytes 8388608
  442.6 5.2 slice-start.1
  447.8 3.5 copy-start.19
  452.5 101.8 %copy-start.13 = (f32[32,512]{1,0:T(8,128)S(1)}, f32[32,512]{1,0:T(8,128)}, u32[]{:S(2)}) copy-start(f32[32,512]{1,0:T(8,128)} %copy-done.12) | copy-start | bytes 196612
  555.3 2.2 copy-start.2
  564.3 108.1 %copy-start.27 = (bf16[64]{0:T(256)(128)(2,1)S(1)}, bf16[64]{0:T(256)(128)(2,1)}, u32[]{:S(2)}) copy-start(bf16[64]{0:T(256)(128)(2,1)} %param.17) | copy-start | bytes 388
  564.3 108.6 %copy-start.28 = (bf16[64]{0:T(256)(128)(2,1)S(1)}, bf16[64]{0:T(256)(128)(2,1)}, u32[]{:S(2)}) copy-start(bf16[64]{0:T(256)(128)(2,1)} %param.16) | copy-start | bytes 388
  667.5 8.6 %copy-start.23 = (bf16[512,2048]{1,0:T(8,128)(2,1)S(1)}, bf16[512,2048]{1,0:T(8,128)(2,1)}, u32[]{:S(2)}) copy-start(bf16[512,2048]{1,0:T(8,128)(2,1)} %get-tuple-element.67) | copy-start | bytes 6291460
  673.5 3.9 copy-start.21
  677.4 3.7 copy-start.22
  (11 other events, 14.3 us)
Sparse Core Ops, SparseCore 0:
  72.5 72.7 all-gather.2
  146.9 124.2 all-gather.4
  349.4 127.4 reduce-scatter.2
  553.8 69.7 reduce-scatter.4

commit v5 on v4

--- a/solution.py
+++ b/solution.py
@@ -870,8 +870,42 @@
     return inverse * (gy - x * jnp.mean(gy * x, axis=1, keepdims=True))
 
 
+def middle_back_kernel(out_rows, dy_ref, mid_ref, g_ref, gain_ref, w_ref, dm_ref, low_ref, dh_ref, acc):
+    dm = g_ref[...].astype(F32)
+    dm += normed_back(dy_ref[...].astype(F32), mid_ref[...], gain_ref[...])
+    dm_ref[...] = dm
+    low = dm.astype(BF16)
+    low_ref[...] = low
+    tall = w_ref.shape[0] // 32
+    heads = back_product(w_ref[...], low)
+    for i in range(32):
+        acc[i * out_rows : (i + 1) * out_rows, :] = heads[i * tall : i * tall + out_rows]
+    dh_ref[...] = acc[...].astype(BF16)
+
+
+def middle_back(dy, middle, g, gain, w, out_rows):
+    count, width = middle.shape
+    block = 256
+    rows = pl.BlockSpec((block, width), lambda i: (i, 0))
+    whole = lambda x: pl.BlockSpec(x.shape, lambda i: (0, 0))
+    return pl.pallas_call(
+        functools.partial(middle_back_kernel, out_rows),
+        grid=(count // block,),
+        in_specs=[rows] * 3 + [whole(gain), whole(w)],
+        out_specs=[rows, rows, pl.BlockSpec((32 * out_rows, block), lambda i: (0, i))],
+        out_shape=[
+            jax.ShapeDtypeStruct((count, width), F32),
+            jax.ShapeDtypeStruct((count, width), BF16),
+            jax.ShapeDtypeStruct((32 * out_rows, count), BF16),
+        ],
+        scratch_shapes=[pltpu.VMEM((32 * out_rows, block), F32)],
+        compiler_params=pltpu.CompilerParams(vmem_limit_bytes=56 * 2**20),
+        name="middle_back",
+    )(dy, middle, g, gain, w)
+
+
 def sum_weights_kernel(n_ref, p_ref, h_ref, a_ref, few_ref, own_ref, *refs):
-    w_ref, x_ref, dm_ref, gain_ref, back_ref, wide_ref, *refs = refs
+    w_ref, x_ref, dm_ref, back_0_ref, back_1_ref, gain_ref, wide_ref, *refs = refs
     qkv_out, few_out, products_out, out_out, dx_ref, wide_out, dg_ref, *refs = refs
     w_v, qkv_sum, back_v, w_sem, own_sem, sent_w, got_w, *refs = refs
     w_load = pltpu.make_async_copy(w_ref, w_v, w_sem)
@@ -882,11 +916,11 @@
     plane = (d, d_c, d_x, d_x + flip, d_y, d_y + flip, d_d, d_d + flip)
     greet([(other, s) for other in plane[1:]] + [(d, (s + i) % 4) for i in (1, 2, 3)])
 
-    def exchange(k):
-        src, dst = back_ref.at[plane[k]], back_v.at[d]
+    def exchange(k, i):
+        src, dst = (back_0_ref, back_1_ref)[i].at[plane[k]], back_v.at[i, d]
         if k == 0:
-            return pltpu.make_async_copy(src, dst, own_sem)
-        return remote(src, dst, sent_w.at[k], got_w.at[k], (plane[k], s))
+            return pltpu.make_async_copy(src, dst, own_sem.at[i])
+        return remote(src, dst, sent_w.at[k, i], got_w.at[k, i], (plane[k], s))
 
     width, chunk = p_ref.shape[0], 512
 
@@ -936,20 +970,22 @@
     along()
     pass_on_2()
     for k in range(8):
-        exchange(k).start()
+        exchange(k, 0).start()
+        exchange(k, 1).start()
     token_grads(3, blocks - 3)
     along_2()
     end(qkv_sum)
-    exchange(0).wait()
-    for k in range(1, 8):
-        exchange(k).wait_recv()
-        exchange(k).wait_send()
-    part = back_v.shape[2] // 2
+    for i in (0, 1):
+        exchange(0, i).wait()
+        for k in range(1, 8):
+            exchange(k, i).wait_recv()
+            exchange(k, i).wait_send()
+    part = back_v.shape[3]
     total = jnp.zeros((dg_ref.shape[0], 1), F32)
     for j in range(16):
         half_j, holder = j // 8, j % 8
         span = slice(j * part, (j + 1) * part)
-        grad = back_v[holder, :, half_j * part : (half_j + 1) * part].astype(F32)
+        grad = back_v[half_j, holder].astype(F32)
         wide_out[:, span] = grad
         total += jnp.sum(grad * wide_ref[:, span].astype(F32), axis=1, keepdims=True)
     dg_ref[...] = jnp.broadcast_to(total, dg_ref.shape)
@@ -961,7 +997,7 @@
     end_2(out_out)
 
 
-def sum_weights(normed, dprojected, heads, dattend, few, own, w, x, dmiddle, gain, back, wide):
+def sum_weights(normed, dprojected, heads, dattend, few, own, w, x, dmiddle, gain, back, back_1, wide):
     dma, anywhere = pltpu.SemaphoreType.DMA, pl.BlockSpec(memory_space=pl.ANY)
     vmem = pl.BlockSpec(memory_space=pltpu.VMEM)
     rows, width = own.shape
@@ -969,11 +1005,11 @@
     scratch = [
         pltpu.VMEM(w.shape, BF16),
         pltpu.VMEM(own.shape, F32),
-        pltpu.VMEM(back.shape, BF16),
+        pltpu.VMEM((2, *back.shape), BF16),
         dma,
-        dma,
-        dma((8,)),
-        dma((8,)),
+        dma((2,)),
+        dma((8, 2)),
+        dma((8, 2)),
     ]
     scratch += weight_sums_scratch(rows, width) + weight_sums_scratch(tall, width)
     return pl.pallas_call(
@@ -987,14 +1023,14 @@
             jax.ShapeDtypeStruct(wide.shape, F32),
             jax.ShapeDtypeStruct((rows, 128), F32),
         ],
-        in_specs=[vmem] * 6 + [anywhere] * 3 + [vmem, anywhere, vmem],
+        in_specs=[vmem] * 6 + [anywhere] * 5 + [vmem] * 2,
         out_specs=[vmem] * 4 + [anywhere, vmem, vmem],
         scratch_shapes=scratch,
         compiler_params=pltpu.CompilerParams(
             collective_id=6, has_side_effects=True, vmem_limit_bytes=63 * 2**20
         ),
         name="sum_weights",
-    )(normed, dprojected, heads, dattend, few, own, w, x, dmiddle, gain, back, wide)
+    )(normed, dprojected, heads, dattend, few, own, w, x, dmiddle, back, back_1, gain, wide)
 
 
 def plane_kernel(rows, heads_ref, w_ref, x_ref, gain_ref, g_ref, down_ref, *refs):
@@ -1089,8 +1125,8 @@
         out_ref[i % n_seq, i // n_seq] = total[i * rows : (i + 1) * rows].astype(BF16)
 
 
-def transposed_product(x, g, n_dp, n_seq):
-    (tokens, width), wide = x.shape, g.shape[1]
+def transposed_product(x, g, n_dp, n_seq, parts):
+    (tokens, width), wide = x.shape, g.shape[1] // parts
     rows, tall = width // (n_dp * n_seq), 512
     return pl.pallas_call(
         transposed_kernel,
@@ -1205,7 +1241,9 @@
     return load, product
 
 
-def plane_sum_kernel(g_ref, w_ref, h_ref, t_ref, out_ref, grad_ref, w_v, g_v, h_v, *refs):
+def plane_sum_kernel(
+    g_ref, w_ref, h_ref, t_ref, x_ref, out_ref, grad_ref, wide_ref, w_v, g_v, h_v, *refs
+):
     w_sem, g_sem, h_sem, out_sem, *refs = refs
     place = places()
     d, s, d_c, d_x, d_y, line = place
@@ -1253,9 +1291,26 @@
             out_specs=[pl.BlockSpec((deep, wide), lambda i: (0, first + i))],
         )(t_ref, grad_ref)
 
+    def wide_body(x_tile, wide_tile):
+        total = outer_sum(x_tile[...], h_v[...])
+        high = wide_tile.shape[2]
+        for j in range(4):
+            wide_tile[j, 0] = total[j * high : (j + 1) * high].astype(BF16)
+
     grad_tiles(0, 2)
     pass_on()
     grad_tiles(2, t_ref.shape[1] // wide - 2)
+    h_load = pltpu.make_async_copy(g_ref.at[:, pl.ds(deep, deep)], h_v, h_sem)
+    h_load.start()
+    h_load.wait()
+    pltpu.emit_pipeline(
+        wide_body,
+        grid=(8,),
+        in_specs=[pl.BlockSpec((tokens, x_ref.shape[1] // 8), lambda i: (0, i))],
+        out_specs=[
+            pl.BlockSpec((4, 1, x_ref.shape[1] // 32, deep), lambda i: (0, i, 0, 0))
+        ],
+    )(x_ref, wide_ref)
     end()
     out = pltpu.make_async_copy(kept.at[0], out_ref, out_sem)
     out.start()
@@ -1264,7 +1319,7 @@
     out.wait()
 
 
-def plane_sum(g, w, h, t, rows):
+def plane_sum(g, w, h, t, x, rows):
     dma, anywhere = pltpu.SemaphoreType.DMA, pl.BlockSpec(memory_space=pl.ANY)
     width, deep = w.shape
     return pl.pallas_call(
@@ -1272,9 +1327,10 @@
         out_shape=[
             jax.ShapeDtypeStruct((rows, width), BF16),
             jax.ShapeDtypeStruct((h.shape[1], t.shape[1]), BF16),
+            jax.ShapeDtypeStruct((4, 8, width // 32, h.shape[1]), BF16),
         ],
-        in_specs=[anywhere] * 4,
-        out_specs=[anywhere] * 2,
+        in_specs=[anywhere] * 5,
+        out_specs=[anywhere] * 3,
         scratch_shapes=[
             pltpu.VMEM((width, deep), BF16),
             pltpu.VMEM((2, rows, deep), BF16),
@@ -1289,7 +1345,7 @@
             collective_id=5, has_side_effects=True, vmem_limit_bytes=62 * 2**20
         ),
         name="plane_sum",
-    )(g, w, h, t)
+    )(g, w, h, t, x)
 
 
 def sigmoid(v):
@@ -1434,22 +1490,30 @@
         normed2_all = gather(norm_rows(middle, ffn_gain_full).astype(BF16), "dp")
         dhidden = back_product(cotangent_all, down_w).astype(BF16)
     hidden, dgate_up = gate_up_product(normed2_all, dhidden, gate_up_w, n_dp, n_seq)
-    gate_up_grad = transposed_product(normed2_all, dgate_up, n_dp, n_seq)
-    gate_up_grad, dgate_up = lax.optimization_barrier((gate_up_grad, dgate_up))
-    gate_up_grad = scatter(gate_up_grad.reshape(width, 2 * part), "seq")
+    gate_grad = transposed_product(normed2_all, dgate_up, n_dp, n_seq, 2 if full else 1)
+    gate_grad, dgate_up = lax.optimization_barrier((gate_grad, dgate_up))
+    gate_grad = scatter(gate_grad.reshape(width, -1), "seq")
     if full:
-        dnormed2, down_grad = plane_sum(dgate_up, gate_up_w, hidden, cotangent_all, count)
+        dnormed2, down_grad, up_grad = plane_sum(
+            dgate_up, gate_up_w, hidden, cotangent_all, normed2_all, count
+        )
+        gate_grad, up_grad, dnormed2 = lax.optimization_barrier((gate_grad, up_grad, dnormed2))
+        up_grad = scatter(up_grad.reshape(width, part), "seq")
     else:
         ordered = gate_up_w.reshape(n_seq, n_dp, wr, 2 * part).transpose(1, 0, 2, 3)
         ordered = ordered.reshape(width, 2 * part)
         dnormed2 = scatter(back_product(dgate_up, ordered).astype(BF16), "dp")
         down_grad = outer_sum(hidden, cotangent_all).astype(BF16)
-    dnormed2 = dnormed2.astype(F32)
-
-    dmiddle = cotangent_low.astype(F32) + normed_back(dnormed2, middle, ffn_gain_full)
-    dattend = dmiddle.astype(BF16)
-    dheads = back_product(out_full, dattend).astype(BF16).reshape(n_dp * n_seq, -1, count)
-    dheads = dheads[:, :out_rows].reshape(QW, count)
+    if full:
+        dmiddle, dattend, dheads = middle_back(
+            dnormed2, middle, cotangent_low, ffn_gain_full[None], out_full, out_rows
+        )
+    else:
+        dmiddle = cotangent_low.astype(F32)
+        dmiddle += normed_back(dnormed2.astype(F32), middle, ffn_gain_full)
+        dattend = dmiddle.astype(BF16)
+        dheads = back_product(out_full, dattend).astype(BF16).reshape(n_dp * n_seq, -1, count)
+        dheads = dheads[:, :out_rows].reshape(QW, count)
     if full:
         dqueries, dpairs, mixed = attend_back(
             start, queries, dheads, heads_out, lse, pairs, held, rows, n_seq,
@@ -1460,8 +1524,10 @@
             start, queries, dheads, heads_out, lse, pairs, held, rows, n_seq, []
         )
         mixed = middle + scatter(mm(hidden, down_w).astype(BF16), "dp").astype(F32)
-    gate_up_grad, dqueries = lax.optimization_barrier((gate_up_grad, dqueries))
-    gate_up_grad = gate_up_grad.reshape(n_dp, wr, 2 * part)
+    if full:
+        gate_grad, up_grad, dqueries = lax.optimization_barrier((gate_grad, up_grad, dqueries))
+        up_grad = up_grad.reshape(n_dp, wr, part)
+    gate_grad = gate_grad.reshape(n_dp, wr, -1)
     down_grad, dqueries = lax.optimization_barrier((down_grad, dqueries))
     down_grad = scatter(down_grad, "seq")
     dprojected_low, head_grad = prepare_back(
@@ -1483,7 +1549,8 @@
                 tokens.reshape(count, width),
                 dmiddle,
                 attn_gain_full[None],
-                gate_up_grad,
+                gate_grad,
+                up_grad,
                 w_gate_up,
             )
         )
@@ -1503,7 +1570,7 @@
         )
         qkv_products = jnp.sum(own_qkv[:, :qkv_w].astype(F32) * qkv_grad[:, :qkv_w], axis=1)
         qkv_grad = qkv_grad[:, :qkv_w]
-        gate_up_grad = lax.all_to_all(gate_up_grad, "dp", 0, 0, tiled=True)
+        gate_up_grad = lax.all_to_all(gate_grad, "dp", 0, 0, tiled=True)
         gate_up_grad = gate_up_grad.reshape(n_dp, wr, 2, part).transpose(1, 2, 0, 3)
         gate_up_grad = gate_up_grad.reshape(wr, 2 * ff).astype(F32)
         ffn_products = jnp.sum(w_gate_up.astype(F32) * gate_up_grad, axis=1)

time: 699 us -> 678 us (0.970)
  other arithmetic: 22.2 us -> 10.7 us
    pallas_call x1, Pallas kernels: 33.8 us -> 18.9 us  [transposed_product(): pl.pallas_call(transposed_kernel, grid=(width // tall,), in_specs=[pl.Blo...]
    pallas_call x0 -> x1, Pallas kernels: none -> 10.7 us  [middle_back(): pl.pallas_call(functools.partial(middle_back_kernel, out_rows), grid=(cou...]
    pallas_call x1, Pallas kernels: 101 us -> 109 us  [attend_back(): pl.pallas_call(functools.partial(attend_back_kernel, n, rows, bool(more))...]
    unnamed x68 -> x58, local copies, waits for them, and re-layouts: 22 us -> 20 us
  transfers between devices with their start and end apart: 4 -> 5, of which waited for: 0 -> 0; matrix products, arithmetic and copies ran while one was open for 5% -> 3% of each run, Pallas kernels for 69% -> 73%
where the time goes in v5:
time: 678 us; the launch traced here: 669 us
  Pallas kernels  605 us (89%)
  local copies, waits for them, and re-layouts  29.2 us (4%)
  between operations  14.6 us (2%)
  other arithmetic  10.7 us (2%)
  matrix products  8.01 us (1%)
    pallas_call x1, Pallas kernels, attend_back(): pl.pallas_call(functools.partial(attend_back_kernel, n, rows, bool(more))...  109 us
    pallas_call x1, Pallas kernels, attend(): pl.pallas_call(functools.partial(attend_kernel, n, rows, len(more), out_r...  101 us
    pallas_call x1, Pallas kernels, sum_weights(): pl.pallas_call(sum_weights_kernel, out_shape=[jax.ShapeDtypeStruct((rows,...  96.8 us
    pallas_call x1, Pallas kernels, plane_sum(): pl.pallas_call(plane_sum_kernel, out_shape=[jax.ShapeDtypeStruct((rows, w...  84.4 us
    pallas_call x1, Pallas kernels, plane_gather(): pl.pallas_call(functools.partial(plane_kernel, 2), out_shape=[jax.ShapeDt...  80.5 us
    pallas_call x1, Pallas kernels, gather_weights(): pl.pallas_call(functools.partial(weights_kernel, n), out_shape=[jax.Shape...  60.9 us
    pallas_call x1, Pallas kernels, gate_up_product(): pl.pallas_call(functools.partial(gate_up_kernel, n_dp, n_seq), grid=(toke...  37.7 us
    unnamed x58, local copies, waits for them, and re-layouts  20 us
  transfers between devices with their start and end apart: 5, of which 0 were waited for; matrix products, arithmetic and copies ran while one was open for 3% of the time, Pallas kernels for 73%

profile of v5, /device:TPU:0, one launch (start us, length us, event | category | flops | bytes accessed | tf_op | source)
XLA Modules:
  0.0 668.9 jit_solution(11033663647217604546)
XLA Ops:
  7.2 1.7 pad.14.refs_1_
  9.8 1.7 maximum_maximum_fusion.refs_0_.own_ref
  11.4 60.9 %gather_weights.1 = (bf16[32,64,2048]{2,1,0:T(8,128)(2,1)}, bf16[4,48,2048]{2,1,0:T(8,128)(2,1)}, bf16[8,64,1536]{2,1,0:T(8,128)(2,1)}) custom-call(bf16[64,2048]{1,0:T(8,128)(2,1)} %maximum_maximum_fusion.refs_0_.own_ref, bf16[48,2048]{1,0:T(8,128)(2,1)} %pad.14.refs_1_, bf16[64,12288]{1,0:T(8,128)(2,1)} %refs_6_.1), custom_call_target="tpu_custom_call" | custom-call | tf_op jit(solution)/shard_map/gather_weights/pallas_call | solution.py:731
  78.3 8.0 %fusion.2.p_ref = f32[2048,512]{1,0:T(8,128)S(1)} fusion(bf16[2048,2048]{1,0:T(8,128)(2,1)} %bitcast.36, bf16[512,2048]{1,0:T(8,128)(2,1)S(1)} %multiply_convert_fusion.n_ref), kind=kOutput, calls=%fused_computation.24 | convolution fusion | flops 4294967296 | bytes 14680064 | tf_op jit(solution)/shard_map/dot_general | solution.py:1467
  86.3 2.4 prepare.1
  88.8 2.0 copy-done.1
  90.8 100.7 %attend.1 = (bf16[1280,512]{1,0:T(8,128)(2,1)S(1)}, f32[5,8,512]{2,1,0:T(8,128)S(1)}, bf16[3,640,512]{2,1,0:T(8,128)(2,1)}, bf16[8,512,2048]{2,1,0:T(8,128)(2,1)...) custom-call(s32[8,512]{1,0:T(8,128)S(1)} %broadcast_in_dim.50.start_ref.refs_0_, ...), custom_call_target="tpu_custom_call" | custom-call | tf_op jit(solution)/shard_map/attend/pallas_call | solution.py:388
  195.1 1.4 copy-done.4
  197.3 80.5 %plane_gather.1 = (bf16[8,512,2048]{2,1,0:T(8,128)(2,1)}, bf16[4096,768]{1,0:T(8,128)(2,1)}, f32[512,2048]{1,0:T(8,128)}) custom-call(bf16[1536,512]{1,0:T(8,128)(2,1)S(1)} %copy-done.4, bf16[8,4,48,2048]{3,2,1,0:T(8,128)(2,1)} %get-tuple-element.61.w_ref, bf16[512,2048]{1,0:T(8,128)(2,1)S(1)} %bitcast.29, f32[1,2048]{1,0:T(1,128)S(1)} %copy-done.16, ...), custom_call_target="tpu_custom_call" | custom-call | tf_op jit(solution)/shard_map/plane_gather/pallas_call | solution.py:1092
  277.8 37.7 %gate_up.1 = (bf16[4096,768]{1,0:T(8,128)(2,1)}, bf16[4096,1536]{1,0:T(8,128)(2,1)}) custom-call(bf16[4096,2048]{1,0:T(8,128)(2,1)} %bitcast.33, bf16[4096,768]{1,0:T(8,128)(2,1)} %get-tuple-element.65.dh_ref, bf16[2048,1536]{1,0:T(8,128)(2,1)} %all-gather.5.cloned.1.call-done.w_ref), custom_call_target="tpu_custom_call" | custom-call | flops 25769803776 | bytes 48234496 | tf_op jit(solution)/shard_map/gate_up/pallas_call | solution.py:1388
  315.5 18.9 %transposed_product.1 = bf16[4,8,64,768]{3,2,1,0:T(8,128)(2,1)} custom-call(bf16[4096,2048]{1,0:T(8,128)(2,1)} %bitcast.34, bf16[4096,1536]{1,0:T(8,128)(2,1)} %get-tuple-element.69.g_ref), custom_call_target="tpu_custom_call" | custom-call | flops 12884901888 | bytes 26214400 | tf_op jit(solution)/shard_map/transposed_product/pallas_call | solution.py:1131
  334.8 84.4 %plane_sum.1 = (bf16[512,2048]{1,0:T(8,128)(2,1)}, bf16[768,2048]{1,0:T(8,128)(2,1)}, bf16[4,8,64,768]{3,2,1,0:T(8,128)(2,1)}) custom-call(bf16[4096,1536]{1,0:T(8,128)(2,1)} %get-tuple-element.69.g_ref, bf16[2048,1536]{1,0:T(8,128)(2,1)} %all-gather.5.cloned.1.call-done.w_ref, bf16[4096,768]{1,0:T(8,128)(2,1)} %get-tuple-element.70.h_ref.refs_7_, ...), custom_call_target="tpu_custom_call" | custom-call | tf_op jit(solution)/shard_map/plane_sum/pallas_call | solution.py:1325
  419.3 10.7 %middle_back.1 = (f32[512,2048]{1,0:T(8,128)}, bf16[512,2048]{1,0:T(8,128)(2,1)}, bf16[1280,512]{1,0:T(8,128)(2,1)}) custom-call(bf16[512,2048]{1,0:T(8,128)(2,1)} %get-tuple-element.73.dy_ref, f32[512,2048]{1,0:T(8,128)} %get-tuple-element.74.mid_ref.refs_9_, bf16[512,2048]{1,0:T(8,128)(2,1)} %bitcast.39, f32[1,2048]{1,0:T(1,128)} %reshape.158.gain_ref, ...), custom_call_target="tpu_custom_call" | custom-call | tf_op jit(solution)/shard_map/middle_back/pallas_call | solution.py:891
  430.0 108.8 %attend_back.1 = (f32[1280,512]{1,0:T(8,128)}, f32[640,512]{1,0:T(8,128)}, bf16[512,2048]{1,0:T(8,128)(2,1)}) custom-call(s32[8,512]{1,0:T(8,128)} %copy-done.14, bf16[1280,512]{1,0:T(8,128)(2,1)} %copy-done.5, bf16[1280,512]{1,0:T(8,128)(2,1)} %get-tuple-element.75.refs_2_, bf16[1280,512]{1,0:T(8,128)(2,1)} %copy-done.9, f32[5,8,512]{2,1,0:T(8,128)} %copy-done.15, ...), custom_call_target="tpu_custom_call" | custom-call | tf_op jit(solution)/shard_map/attend_back/pallas_call | solution.py:568
  540.6 2.2 copy-done.2
  542.8 1.3 copy-done.10
  544.1 3.1 prepare_back.1
  547.3 1.3 copy-done.8
  549.7 96.8 %sum_weights.1 = (f32[64,1920]{1,0:T(8,128)}, f32[16,128]{1,0:T(8,128)}, f32[64,128]{1,0:T(8,128)}, f32[48,2048]{1,0:T(8,128)}, f32[512,2048]{1,0:T(8,128)}, /*index=5*/f32[64,12288]{1,0:T(8,128)}, f32[64,128]{1,0:T(8,128)}) custom-call(bf16[512,2048]{1,0:T(8,128)(2,1)} %copy-done.17, bf16[2048,512]{1,0:T(8,128)(2,1)} %copy-done.8, ...), custom_call_target="tpu_custom_call" | custom-call | tf_op jit(solution)/shard_map/sum_weights/pallas_call | solution.py:1015
  646.5 1.9 slice.29
  652.5 2.6 convert_element_type.89
  655.1 1.3 copy.31
  656.4 2.1 copy.32
  660.2 1.7 copy.34
  (93 shorter events, 20.0 us)
Async XLA Ops:
  7.2 66.0 %copy-start.23 = (s32[2,4]{1,0:T(2,128)S(1)}, s32[2,4]{1,0:T(2,128)}, u32[]{:S(2)}) copy-start(s32[2,4]{1,0:T(2,128)} %param.11) | copy-start | bytes 100
  7.2 68.0 %copy-start = (bf16[2,256,2048]{2,1,0:T(8,128)(2,1)S(1)}, bf16[2,256,2048]{2,1,0:T(8,128)(2,1)}, u32[]{:S(2)}) copy-start(bf16[2,256,2048]{2,1,0:T(8,128)(2,1)} %param.10) | copy-start | bytes 6291460
  7.2 187.9 %all-gather.3.cloned.1.call-start = ((), (), s32[]{:S(2)}) async-start(), calls=%async_computation.3 | async-start | bytes 3932160 | tf_op jit(solution)/shard_map/all_gather | solution.py:1421
  72.4 205.4 %all-gather.5.cloned.1.call-start = ((), (), s32[]{:S(2)}) async-start(), calls=%async_computation.4 | async-start | bytes 7864320 | tf_op jit(solution)/shard_map/all_gather | solution.py:1421
  73.2 346.1 %reduce-scatter.4.cloned.1.call-start = ((), (), s32[]{:S(2)}) async-start(), calls=%async_computation.5 | async-start | bytes 3932160 | tf_op jit(solution)/shard_map/reduce_scatter | solution.py:1425
  77.7 8.6 %copy-start.12 = (f32[32,512]{1,0:T(8,128)}, f32[32,512]{1,0:T(8,128)S(1)}, u32[]{:S(2)}) copy-start(f32[32,512]{1,0:T(8,128)S(1)} %get-tuple-element.104.cos_ref) | copy-start | bytes 196612
  78.3 8.0 %copy-start.17 = (bf16[512,2048]{1,0:T(8,128)(2,1)}, bf16[512,2048]{1,0:T(8,128)(2,1)S(1)}, u32[]{:S(2)}) copy-start(bf16[512,2048]{1,0:T(8,128)(2,1)S(1)} %multiply_convert_fusion.n_ref) | copy-start | bytes 6291460
  86.3 4.4 copy-start.22
  86.3 4.4 copy-start.11
  88.7 2.0 copy-start.1
  90.7 187.1 %copy-start.5 = (bf16[1280,512]{1,0:T(8,128)(2,1)}, bf16[1280,512]{1,0:T(8,128)(2,1)S(1)}, u32[]{:S(2)}) copy-start(bf16[1280,512]{1,0:T(8,128)(2,1)S(1)} %get-tuple-element.57.q_ref.refs_1_) | copy-start | bytes 3932164
  90.7 187.1 %copy-start.14 = (s32[8,512]{1,0:T(8,128)}, s32[8,512]{1,0:T(8,128)S(1)}, u32[]{:S(2)}) copy-start(s32[8,512]{1,0:T(8,128)S(1)} %broadcast_in_dim.50.start_ref.refs_0_) | copy-start | bytes 49156
  195.1 1.4 copy-start.4
  334.4 204.5 %reduce-scatter.6.cloned.1.call-start = ((), (), s32[]{:S(2)}) async-start(), calls=%async_computation.6 | async-start | bytes 3932160 | tf_op jit(solution)/shard_map/reduce_scatter | solution.py:1425
  419.3 233.2 %reduce-scatter.8.cloned.1.call-start = ((), (), s32[]{:S(2)}) async-start(), calls=%async_computation.7 | async-start | bytes 3932160 | tf_op jit(solution)/shard_map/reduce_scatter | solution.py:1425
  538.9 1.8 copy-start.7
  538.9 1.8 copy-start.13
  540.6 2.2 copy-start.2
  549.6 101.8 %copy-start.24 = (bf16[64]{0:T(256)(128)(2,1)S(1)}, bf16[64]{0:T(256)(128)(2,1)}, u32[]{:S(2)}) copy-start(bf16[64]{0:T(256)(128)(2,1)} %param.16) | copy-start | bytes 388
  549.6 102.3 %copy-start.25 = (bf16[64]{0:T(256)(128)(2,1)S(1)}, bf16[64]{0:T(256)(128)(2,1)}, u32[]{:S(2)}) copy-start(bf16[64]{0:T(256)(128)(2,1)} %param.17) | copy-start | bytes 388
  646.5 8.6 %copy-start.20 = (bf16[512,2048]{1,0:T(8,128)(2,1)S(1)}, bf16[512,2048]{1,0:T(8,128)(2,1)}, u32[]{:S(2)}) copy-start(bf16[512,2048]{1,0:T(8,128)(2,1)} %get-tuple-element.79) | copy-start | bytes 6291460
  652.5 3.9 copy-start.18
  656.4 2.1 copy-start.21
  656.4 3.7 copy-start.19
  (7 other events, 7.0 us)
Sparse Core Ops, SparseCore 0:
  72.5 72.7 all-gather.2
  146.9 124.2 all-gather.4
  334.5 76.9 reduce-scatter.3
  419.4 100.1 reduce-scatter.5
  539.1 64.1 reduce-scatter.7

commit v6 on v5

--- a/solution.py
+++ b/solution.py
@@ -54,7 +54,7 @@
             [first * cosine - second * sine, second * cosine + first * sine], axis=0
         )
 
-    @pl.loop(0, KEY_VALUE_HEADS)
+    @pl.loop(0, KEY_VALUE_HEADS, unroll=KEY_VALUE_HEADS)
     def _(i):
         key, value = key_rows(i)
         keys_in = p_ref[head_rows(QUERY_HEADS + i), :]
@@ -62,7 +62,7 @@
         values_in = p_ref[head_rows(QUERY_HEADS + KEY_VALUE_HEADS + i), :]
         kv_ref[value, :] = values_in.astype(BF16)
 
-    @pl.loop(0, QUERY_HEADS)
+    @pl.loop(0, QUERY_HEADS, unroll=KEY_VALUE_HEADS)
     def _(i):
         rows = head_rows(i)
         queries = turned(p_ref[rows, :], gain_ref[:HEAD_SIZE, :]) * HEAD_SIZE**-0.5
@@ -82,54 +82,80 @@
     )(projected, gains, cosine, sine)
 
 
-def prepare_back_kernel(p_ref, gain_ref, cos_ref, sin_ref, dq_ref, dkv_ref, out_ref, dg_ref, acc):
+def prepare_back_kernel(
+    p_ref, gain_ref, cos_ref, sin_ref, dq_ref, dkv_ref, out_ref, dg_ref, acc_q, acc_k
+):
     cosine, sine = cos_ref[...], sin_ref[...]
-    acc[...] = jnp.zeros_like(acc)
-
-    def back(v, gain, dy, lines):
+    step = pl.program_id(0)
+
+    @pl.when(step == 0)
+    def _():
+        acc_q[...] = jnp.zeros_like(acc_q)
+        acc_k[...] = jnp.zeros_like(acc_k)
+
+    def back(v, gain, dy, acc):
         u, inverse = unit(v)
         first, second = dy[: HEAD_SIZE // 2], dy[HEAD_SIZE // 2 :]
         dz = jnp.concatenate(
             [first * cosine + second * sine, second * cosine - first * sine], axis=0
         )
-        acc[lines, :] += dz * u
+        acc[...] += dz * u
         du = dz * gain
         return inverse * (du - u * jnp.mean(du * u, axis=0, keepdims=True))
 
-    @pl.loop(0, KEY_VALUE_HEADS)
+    @pl.loop(0, KEY_VALUE_HEADS, unroll=KEY_VALUE_HEADS)
     def _(i):
         key, value = key_rows(i)
         rows = head_rows(QUERY_HEADS + i)
-        dv = back(p_ref[rows, :], gain_ref[HEAD_SIZE:, :], dkv_ref[key, :], slice(HEAD_SIZE, None))
+        dv = back(p_ref[rows, :], gain_ref[HEAD_SIZE:, :], dkv_ref[key, :], acc_k)
         out_ref[rows, :] = dv.astype(BF16)
         out_ref[head_rows(QUERY_HEADS + KEY_VALUE_HEADS + i), :] = dkv_ref[value, :].astype(BF16)
 
-    @pl.loop(0, QUERY_HEADS)
+    @pl.loop(0, QUERY_HEADS, unroll=KEY_VALUE_HEADS)
     def _(i):
         rows = head_rows(i)
         dy = dq_ref[rows, :] * HEAD_SIZE**-0.5
-        dv = back(p_ref[rows, :], gain_ref[:HEAD_SIZE, :], dy, slice(0, HEAD_SIZE))
+        dv = back(p_ref[rows, :], gain_ref[:HEAD_SIZE, :], dy, acc_q)
         out_ref[rows, :] = dv.astype(BF16)
 
     rest = out_ref.shape[0] - QW - 2 * KW
     out_ref[QW + 2 * KW :, :] = jnp.zeros((rest, out_ref.shape[1]), BF16)
-    total = jnp.sum(acc[...], axis=1, keepdims=True)
-    dg_ref[...] = jnp.broadcast_to(total, dg_ref.shape)
-
-
-def prepare_back(projected, gains, cosine, sine, dqueries, dpairs):
+
+    @pl.when(step == pl.num_programs(0) - 1)
+    def _():
+        few = 2 * HEAD_SIZE // dg_ref.shape[0]
+        dg_ref[...] = jnp.zeros_like(dg_ref)
+        for half, acc in enumerate((acc_q, acc_k)):
+            total = jnp.sum(acc[...], axis=1, keepdims=True)
+            total = jnp.broadcast_to(total, (HEAD_SIZE, dg_ref.shape[2]))
+            for i in range(HEAD_SIZE // few):
+                dg_ref[half * (HEAD_SIZE // few) + i, :few, :] = total[i * few : (i + 1) * few]
+
+
+def prepare_back(projected, gains, cosine, sine, dqueries, dpairs, width, devices):
     tokens = projected.shape[1]
-    dprojected, dgains = pl.pallas_call(
+    block = min(256, tokens)
+    some = lambda x, rows=None: pl.BlockSpec((rows or x.shape[0], block), lambda i: (0, i))
+    return pl.pallas_call(
         prepare_back_kernel,
+        grid=(tokens // block,),
+        in_specs=[
+            some(projected, QW + 2 * KW),
+            pl.BlockSpec(gains.shape, lambda i: (0, 0)),
+            *[some(x) for x in (cosine, sine, dqueries, dpairs)],
+        ],
+        out_specs=[
+            pl.BlockSpec((width, block), lambda i: (0, i)),
+            pl.BlockSpec((devices, 16, 128), lambda i: (0, 0, 0)),
+        ],
         out_shape=[
-            jax.ShapeDtypeStruct(projected.shape, BF16),
-            jax.ShapeDtypeStruct((2 * HEAD_SIZE, 128), F32),
+            jax.ShapeDtypeStruct((width, tokens), BF16),
+            jax.ShapeDtypeStruct((devices, 16, 128), F32),
         ],
-        scratch_shapes=[pltpu.VMEM((2 * HEAD_SIZE, tokens), F32)],
-        compiler_params=pltpu.CompilerParams(vmem_limit_bytes=40 * 2**20),
+        scratch_shapes=[pltpu.VMEM((HEAD_SIZE, block), F32)] * 2,
+        compiler_params=pltpu.CompilerParams(vmem_limit_bytes=62 * 2**20),
         name="prepare_back",
     )(projected, gains, cosine, sine, dqueries, dpairs)
-    return dprojected, dgains[:, 0]
 
 
 def dot(a, b):
@@ -596,7 +622,7 @@
             return pltpu.make_async_copy(src, dst, own_w.at[half])
         return remote(src, dst, sent_w.at[k, half], got_w.at[k, half], (plane[k], s))
 
-    def copies(slot, sent, got, peer, own=False, many=1):
+    def copies(slot, sent, got, peer, own=False, arrays=(0,)):
         return [
             remote(
                 x_refs[i] if own else out_refs[i].at[slot if i == 0 else slot % 4],
@@ -605,7 +631,7 @@
                 got(i),
                 peer,
             )
-            for i in range(many)
+            for i in arrays
         ]
 
     def start(group):
@@ -626,9 +652,9 @@
     def got(k, b):
         return lambda i: recv.at[i, k, b]
 
-    def arrived(k, b):
-        many = 1 if k else n
-        for one in copies(d * 4 + b, lambda i: send_x.at[i, b], got(k, b), (d_x, s), many=many):
+    def arrived(k, b, arrays=(0,)):
+        group = copies(d * 4 + b, lambda i: send_x.at[i, b], got(k, b), (d_x, s), arrays=arrays)
+        for one in group:
             one.wait_recv()
 
     own = [
@@ -637,11 +663,11 @@
     ]
     start(own)
 
-    def up(b, own=False):
-        return copies(d * 4 + b, lambda i: send_z.at[i, 0, b], got(0, b), (d, s + 1), own, n)
-
-    def down(b, own=False):
-        return copies(d * 4 + b, lambda i: send_z.at[i, 1, b], got(0, b), (d, s - 1), own, n)
+    def up(b, own=False, arrays=(0,)):
+        return copies(d * 4 + b, lambda i: send_z.at[i, 0, b], got(0, b), (d, s + 1), own, arrays)
+
+    def down(b, own=False, arrays=(0,)):
+        return copies(d * 4 + b, lambda i: send_z.at[i, 1, b], got(0, b), (d, s - 1), own, arrays)
 
     def spread(b, own=False):
         return (
@@ -650,15 +676,24 @@
             + copies(d * 4 + b, lambda i: send_c.at[i, 0, b], got(1, b), (d_c, s), own)
         )
 
-    def column_block(b, direction):
+    others = tuple(range(1, n))
+
+    def line_block(b, direction, arrays):
         own = direction == 0
         if direction:
-            arrived(0, b)
+            arrived(0, b, arrays)
         if direction >= 0:
-            pl.when(s < 3)(lambda: start(up(b, own)))
+            pl.when(s < 3)(lambda: start(up(b, own, arrays)))
         if direction <= 0:
-            pl.when(s > 0)(lambda: start(down(b, own)))
-        start(spread(b, own))
+            pl.when(s > 0)(lambda: start(down(b, own, arrays)))
+
+    def column_block(b, direction):
+        line_block(b, direction, (0,))
+        start(spread(b, direction == 0))
+
+    def other_block(b, direction):
+        if direction:
+            line_block(b, direction, others)
 
     def start_columns():
         for k in range(8):
@@ -666,6 +701,7 @@
                 columns(k, half).start()
 
     each(column_block, start_columns)
+    line_block(s, 0, others)
 
     def over_y(b):
         return copies(d_x * 4 + b, lambda i: send_d.at[i, b], got(6, b), (d_y, s))
@@ -692,15 +728,16 @@
         arrived(6, b)
         start(to_core(3, d_d, b))
 
+    each(other_block)
     each(far_block)
 
     def finish(b, direction):
         for k in (1, 3, 5, 7):
             arrived(k, b)
         if direction >= 0:
-            pl.when(s < 3)(lambda: sent(up(b)))
+            pl.when(s < 3)(lambda: sent(up(b, arrays=range(n))))
         if direction <= 0:
-            pl.when(s > 0)(lambda: sent(down(b)))
+            pl.when(s > 0)(lambda: sent(down(b, arrays=range(n))))
         sent(spread(b))
         sent(over_y(b))
         sent(to_core(1, d_x, b))
@@ -906,8 +943,8 @@
 
 def sum_weights_kernel(n_ref, p_ref, h_ref, a_ref, few_ref, own_ref, *refs):
     w_ref, x_ref, dm_ref, back_0_ref, back_1_ref, gain_ref, wide_ref, *refs = refs
-    qkv_out, few_out, products_out, out_out, dx_ref, wide_out, dg_ref, *refs = refs
-    w_v, qkv_sum, back_v, w_sem, own_sem, sent_w, got_w, *refs = refs
+    qkv_out, small_out, out_out, dx_ref, wide_out, *refs = refs
+    w_v, qkv_sum, out_sum, back_v, w_sem, own_sem, sent_w, got_w, *refs = refs
     w_load = pltpu.make_async_copy(w_ref, w_v, w_sem)
     w_load.start()
     place = places()
@@ -935,7 +972,7 @@
         rows = n_ref[:, pl.ds(pl.multiple_of(k * tall, tall), tall)].T
         chunks(lambda span: back_product(rows, p_ref[span, :]), dst)
         for b in range(4):
-            dst[b, :16, -128:] = few_ref[k * 4 + b]
+            dst[b, :16, -128:] = few_ref[k * 4 + b].astype(BF16)
 
     def out_product(k, dst):
         tall = dst.shape[0] * dst.shape[1]
@@ -981,23 +1018,30 @@
             exchange(k, i).wait_recv()
             exchange(k, i).wait_send()
     part = back_v.shape[3]
-    total = jnp.zeros((dg_ref.shape[0], 1), F32)
+    total = jnp.zeros((wide_out.shape[0], 1), F32)
     for j in range(16):
         half_j, holder = j // 8, j % 8
         span = slice(j * part, (j + 1) * part)
         grad = back_v[half_j, holder].astype(F32)
         wide_out[:, span] = grad
         total += jnp.sum(grad * wide_ref[:, span].astype(F32), axis=1, keepdims=True)
-    dg_ref[...] = jnp.broadcast_to(total, dg_ref.shape)
+    tall = wide_out.shape[0]
+
+    def as_row(column):
+        return jnp.broadcast_to(column, (column.shape[0], 128)).T[0:1]
+
+    small_out[...] = jnp.zeros_like(small_out)
+    small_out[1:2, :tall] = as_row(total)
     inner = QW + 2 * KW
     total = jnp.sum(qkv_sum[:, :inner] * own_ref[:, :inner].astype(F32), axis=1, keepdims=True)
-    products_out[...] = jnp.broadcast_to(total, products_out.shape)
-    few_out[...] = qkv_sum[:16, inner:]
+    small_out[0:1, :tall] = as_row(total)
+    small_out[2:3, :16] = as_row(qkv_sum[:16, inner : inner + 1])
     qkv_out[...] = qkv_sum[:, :inner]
-    end_2(out_out)
-
-
-def sum_weights(normed, dprojected, heads, dattend, few, own, w, x, dmiddle, gain, back, back_1, wide):
+    end_2(out_sum)
+    out_out[...] = out_sum[: out_out.shape[0]]
+
+
+def sum_weights(normed, dprojected, heads, dattend, few, own, w, x, dmiddle, gain, back, back_1, wide, out_rows):
     dma, anywhere = pltpu.SemaphoreType.DMA, pl.BlockSpec(memory_space=pl.ANY)
     vmem = pl.BlockSpec(memory_space=pltpu.VMEM)
     rows, width = own.shape
@@ -1005,6 +1049,7 @@
     scratch = [
         pltpu.VMEM(w.shape, BF16),
         pltpu.VMEM(own.shape, F32),
+        pltpu.VMEM((tall, width), F32),
         pltpu.VMEM((2, *back.shape), BF16),
         dma,
         dma((2,)),
@@ -1016,15 +1061,13 @@
         sum_weights_kernel,
         out_shape=[
             jax.ShapeDtypeStruct((rows, QW + 2 * KW), F32),
-            jax.ShapeDtypeStruct((16, width - QW - 2 * KW), F32),
-            jax.ShapeDtypeStruct((rows, 128), F32),
-            jax.ShapeDtypeStruct((tall, width), F32),
+            jax.ShapeDtypeStruct((8, 128), F32),
+            jax.ShapeDtypeStruct((out_rows, width), F32),
             jax.ShapeDtypeStruct(dmiddle.shape, F32),
             jax.ShapeDtypeStruct(wide.shape, F32),
-            jax.ShapeDtypeStruct((rows, 128), F32),
         ],
         in_specs=[vmem] * 6 + [anywhere] * 5 + [vmem] * 2,
-        out_specs=[vmem] * 4 + [anywhere, vmem, vmem],
+        out_specs=[vmem] * 3 + [anywhere, vmem],
         scratch_shapes=scratch,
         compiler_params=pltpu.CompilerParams(
             collective_id=6, has_side_effects=True, vmem_limit_bytes=63 * 2**20
@@ -1458,6 +1501,10 @@
     ffn_gain_full = all_qkv[:, 0, qkv_w + wr : qkv_w + 2 * wr].reshape(-1).astype(F32)
     head_full = all_qkv[:, 1, qkv_w : qkv_w + head_gains.shape[0]].reshape(-1).astype(F32)
 
+    attn_gain_full, ffn_gain_full, head_full = lax.optimization_barrier(
+        (attn_gain_full[None], ffn_gain_full[None], head_full)
+    )
+
     w_down, qkv_full = lax.optimization_barrier((w_down, qkv_full))
     down_w = gather(w_down, "seq")
     cotangent_low = out_grad.reshape(count, width)
@@ -1477,7 +1524,7 @@
         cotangent_all = cotangent_all.reshape(n_dp * count, width)
         out_full = all_out.reshape(-1, width)
         normed2_all, dhidden, middle = plane_gather(
-            heads_full, all_out, tokens.reshape(count, width), ffn_gain_full[None],
+            heads_full, all_out, tokens.reshape(count, width), ffn_gain_full,
             cotangent_all, down_w,
         )
     else:
@@ -1506,7 +1553,7 @@
         down_grad = outer_sum(hidden, cotangent_all).astype(BF16)
     if full:
         dmiddle, dattend, dheads = middle_back(
-            dnormed2, middle, cotangent_low, ffn_gain_full[None], out_full, out_rows
+            dnormed2, middle, cotangent_low, ffn_gain_full, out_full, out_rows
         )
     else:
         dmiddle = cotangent_low.astype(F32)
@@ -1531,32 +1578,29 @@
     down_grad, dqueries = lax.optimization_barrier((down_grad, dqueries))
     down_grad = scatter(down_grad, "seq")
     dprojected_low, head_grad = prepare_back(
-        projected, head_full[:, None], cosine, sine, dqueries, dpairs
+        projected, head_full[:, None], cosine, sine, dqueries, dpairs, width, n_dp * n_seq
     )
     few = head_gains.shape[0]
     if full:
-        few_rows = jnp.pad(head_grad.reshape(-1, few, 1), ((0, 0), (0, 16 - few), (0, 0)))
-        few_rows = jnp.broadcast_to(few_rows.astype(BF16), (n_dp * n_seq, 16, width - qkv_w))
-        qkv_grad, head_rows_out, qkv_products, out_weight_grad, tokens_grad, gate_up_grad, ffn_products = (
+        qkv_grad, small, out_weight_grad, tokens_grad, gate_up_grad = (
             sum_weights(
                 normed_low,
                 dprojected_low,
                 heads_full,
                 dattend,
-                few_rows,
+                head_grad,
                 own_qkv,
                 qkv_full,
                 tokens.reshape(count, width),
                 dmiddle,
-                attn_gain_full[None],
+                attn_gain_full,
                 gate_grad,
                 up_grad,
                 w_gate_up,
+                out_rows,
             )
         )
-        head_out, ffn_products, qkv_products = (
-            head_rows_out[:few, 0], ffn_products[:, 0], qkv_products[:, 0]
-        )
+        qkv_products, ffn_products, head_out = small[0, :wr], small[1, :wr], small[2, :few]
     else:
         qkv_grad = lax.dot_general(
             normed_low, dprojected_low, (((0,), (1,)), ((), ())), preferred_element_type=F32
@@ -1566,7 +1610,7 @@
             scatter(scatter(g, "dp"), "seq").astype(F32) for g in (qkv_grad, out_grads)
         )
         head_out = jnp.sum(
-            lax.all_to_all(head_grad.reshape(-1, few), BOTH, 0, 0, tiled=True), axis=0
+            lax.all_to_all(head_grad[:, :few, 0], BOTH, 0, 0, tiled=True), axis=0
         )
         qkv_products = jnp.sum(own_qkv[:, :qkv_w].astype(F32) * qkv_grad[:, :qkv_w], axis=1)
         qkv_grad = qkv_grad[:, :qkv_w]

time: 678 us -> 670 us (0.988)
  local copies, waits for them, and re-layouts: 29.2 us -> 17.4 us
    unnamed x58 -> x55, local copies, waits for them, and re-layouts: 20 us -> 13.9 us
  transfers between devices with their start and end apart: 5 -> 5, of which waited for: 0 -> 0; matrix products, arithmetic and copies ran while one was open for 3% -> 2% of each run, Pallas kernels for 73% -> 74%
where the time goes in v6:
time: 670 us; the launch traced here: 660 us
  Pallas kernels  609 us (91%)
  local copies, waits for them, and re-layouts  17.4 us (3%)
  between operations  14.6 us (2%)
  other arithmetic  9.9 us (1%)
  matrix products  7.96 us (1%)
    pallas_call x1, Pallas kernels, attend_back(): pl.pallas_call(functools.partial(attend_back_kernel, n, rows, bool(more))...  110 us
    pallas_call x1, Pallas kernels, attend(): pl.pallas_call(functools.partial(attend_kernel, n, rows, len(more), out_r...  101 us
    pallas_call x1, Pallas kernels, sum_weights(): pl.pallas_call(sum_weights_kernel, out_shape=[jax.ShapeDtypeStruct((rows,...  97.2 us
    pallas_call x1, Pallas kernels, plane_sum(): pl.pallas_call(plane_sum_kernel, out_shape=[jax.ShapeDtypeStruct((rows, w...  84.6 us
    pallas_call x1, Pallas kernels, plane_gather(): pl.pallas_call(functools.partial(plane_kernel, 2), out_shape=[jax.ShapeDt...  80.4 us
    pallas_call x1, Pallas kernels, gather_weights(): pl.pallas_call(functools.partial(weights_kernel, n), out_shape=[jax.Shape...  61.5 us
    pallas_call x1, Pallas kernels, gate_up_product(): pl.pallas_call(functools.partial(gate_up_kernel, n_dp, n_seq), grid=(toke...  37.6 us
    pallas_call x1, Pallas kernels, transposed_product(): pl.pallas_call(transposed_kernel, grid=(width // tall,), in_specs=[pl.Blo...  18.9 us
  transfers between devices with their start and end apart: 5, of which 0 were waited for; matrix products, arithmetic and copies ran while one was open for 2% of the time, Pallas kernels for 74%

profile of v6, /device:TPU:0, one launch (start us, length us, event | category | flops | bytes accessed | tf_op | source)
XLA Modules:
  0.0 660.4 jit_solution(10752754556457404052)
XLA Ops:
  7.2 1.7 pad.9.refs_1_
  9.8 1.7 maximum_maximum_fusion.refs_0_.own_ref
  11.4 61.5 %gather_weights.1 = (bf16[32,64,2048]{2,1,0:T(8,128)(2,1)}, bf16[4,48,2048]{2,1,0:T(8,128)(2,1)}, bf16[8,64,1536]{2,1,0:T(8,128)(2,1)}) custom-call(bf16[64,2048]{1,0:T(8,128)(2,1)} %maximum_maximum_fusion.refs_0_.own_ref, bf16[48,2048]{1,0:T(8,128)(2,1)} %pad.9.refs_1_, bf16[64,12288]{1,0:T(8,128)(2,1)} %refs_6_.1), custom_call_target="tpu_custom_call" | custom-call | tf_op jit(solution)/shard_map/gather_weights/pallas_call | solution.py:768
  77.9 8.0 %fusion.p_ref = f32[2048,512]{1,0:T(8,128)S(1)} fusion(bf16[2048,2048]{1,0:T(8,128)(2,1)} %bitcast.41, bf16[512,2048]{1,0:T(8,128)(2,1)S(1)} %multiply_convert_fusion.n_ref), kind=kOutput, calls=%fused_computation.18 | convolution fusion | flops 4294967296 | bytes 14680064 | tf_op jit(solution)/shard_map/dot_general | solution.py:1514
  85.9 1.2 prepare.1
  87.1 2.0 copy-done.1
  89.0 100.7 %attend.1 = (bf16[1280,512]{1,0:T(8,128)(2,1)S(1)}, f32[5,8,512]{2,1,0:T(8,128)S(1)}, bf16[3,640,512]{2,1,0:T(8,128)(2,1)}, bf16[8,512,2048]{2,1,0:T(8,128)(2,1)...) custom-call(s32[8,512]{1,0:T(8,128)S(1)} %broadcast_in_dim.43.start_ref.refs_0_, ...), custom_call_target="tpu_custom_call" | custom-call | tf_op jit(solution)/shard_map/attend/pallas_call | solution.py:414
  189.7 1.1 copy-done.2
  191.7 1.0 copy-done.6
  193.4 1.4 copy-done.3
  194.8 80.4 %plane_gather.1 = (bf16[8,512,2048]{2,1,0:T(8,128)(2,1)}, bf16[4096,768]{1,0:T(8,128)(2,1)}, f32[512,2048]{1,0:T(8,128)}) custom-call(bf16[1536,512]{1,0:T(8,128)(2,1)S(1)} %copy-done.3, bf16[8,4,48,2048]{3,2,1,0:T(8,128)(2,1)} %get-tuple-element.64.w_ref, bf16[512,2048]{1,0:T(8,128)(2,1)S(1)} %bitcast.34, f32[1,2048]{1,0:T(1,128)S(1)} %reshape.144.gain_ref, ...), custom_call_target="tpu_custom_call" | custom-call | tf_op jit(solution)/shard_map/plane_gather/pallas_call | solution.py:1135
  275.3 37.6 %gate_up.1 = (bf16[4096,768]{1,0:T(8,128)(2,1)}, bf16[4096,1536]{1,0:T(8,128)(2,1)}) custom-call(bf16[4096,2048]{1,0:T(8,128)(2,1)} %bitcast.38, bf16[4096,768]{1,0:T(8,128)(2,1)} %get-tuple-element.69.dh_ref, bf16[2048,1536]{1,0:T(8,128)(2,1)} %all-gather.5.cloned.1.call-done.w_ref), custom_call_target="tpu_custom_call" | custom-call | flops 25769803776 | bytes 48234496 | tf_op jit(solution)/shard_map/gate_up/pallas_call | solution.py:1431
  312.9 18.9 %transposed_product.1 = bf16[4,8,64,768]{3,2,1,0:T(8,128)(2,1)} custom-call(bf16[4096,2048]{1,0:T(8,128)(2,1)} %bitcast.39, bf16[4096,1536]{1,0:T(8,128)(2,1)} %get-tuple-element.73.g_ref), custom_call_target="tpu_custom_call" | custom-call | flops 12884901888 | bytes 26214400 | tf_op jit(solution)/shard_map/transposed_product/pallas_call | solution.py:1174
  332.3 84.6 %plane_sum.1 = (bf16[512,2048]{1,0:T(8,128)(2,1)}, bf16[768,2048]{1,0:T(8,128)(2,1)}, bf16[4,8,64,768]{3,2,1,0:T(8,128)(2,1)}) custom-call(bf16[4096,1536]{1,0:T(8,128)(2,1)} %get-tuple-element.73.g_ref, bf16[2048,1536]{1,0:T(8,128)(2,1)} %all-gather.5.cloned.1.call-done.w_ref, bf16[4096,768]{1,0:T(8,128)(2,1)} %get-tuple-element.74.h_ref.refs_7_, ...), custom_call_target="tpu_custom_call" | custom-call | tf_op jit(solution)/shard_map/plane_sum/pallas_call | solution.py:1368
  417.0 10.7 %middle_back.1 = (f32[512,2048]{1,0:T(8,128)}, bf16[512,2048]{1,0:T(8,128)(2,1)}, bf16[1280,512]{1,0:T(8,128)(2,1)}) custom-call(bf16[512,2048]{1,0:T(8,128)(2,1)} %get-tuple-element.77.dy_ref, f32[512,2048]{1,0:T(8,128)} %get-tuple-element.78.mid_ref.refs_9_, bf16[512,2048]{1,0:T(8,128)(2,1)} %bitcast.44, f32[1,2048]{1,0:T(1,128)} %copy-done.13, ...), custom_call_target="tpu_custom_call" | custom-call | tf_op jit(solution)/shard_map/middle_back/pallas_call | solution.py:928
  427.7 110.3 %attend_back.1 = (f32[1280,512]{1,0:T(8,128)}, f32[640,512]{1,0:T(8,128)}, bf16[512,2048]{1,0:T(8,128)(2,1)}) custom-call(s32[8,512]{1,0:T(8,128)} %copy-done.11, bf16[1280,512]{1,0:T(8,128)(2,1)} %copy-done.4, bf16[1280,512]{1,0:T(8,128)(2,1)} %get-tuple-element.79.refs_2_, bf16[1280,512]{1,0:T(8,128)(2,1)} %copy-done.6, f32[5,8,512]{2,1,0:T(8,128)} %copy-done.12, ...), custom_call_target="tpu_custom_call" | custom-call | tf_op jit(solution)/shard_map/attend_back/pallas_call | solution.py:594
  538.0 6.1 prepare_back.1
  544.1 97.2 %sum_weights.1 = (f32[64,1920]{1,0:T(8,128)}, f32[8,128]{1,0:T(8,128)}, f32[40,2048]{1,0:T(8,128)}, f32[512,2048]{1,0:T(8,128)}, f32[64,12288]{1,0:T(8,128)}) custom-call(bf16[512,2048]{1,0:T(8,128)(2,1)} %copy-done.14, bf16[2048,512]{1,0:T(8,128)(2,1)} %get-tuple-element.91.p_ref, bf16[1536,512]{1,0:T(8,128)(2,1)} %copy-done.2, ...), custom_call_target="tpu_custom_call" | custom-call | tf_op jit(solution)/shard_map/sum_weights/pallas_call | solution.py:1060
  641.3 1.3 slice_bitcast_fusion
  642.7 1.3 bitcast_divide_fusion
  643.9 2.6 convert_element_type.71
  646.5 1.3 copy.32
  647.9 2.1 copy.33
  651.7 1.7 copy.36
  (81 shorter events, 9.5 us)
Async XLA Ops:
  7.2 66.6 %copy-start.21 = (s32[2,4]{1,0:T(2,128)S(1)}, s32[2,4]{1,0:T(2,128)}, u32[]{:S(2)}) copy-start(s32[2,4]{1,0:T(2,128)} %param.11) | copy-start | bytes 100
  7.2 69.1 %copy-start = (bf16[2,256,2048]{2,1,0:T(8,128)(2,1)S(1)}, bf16[2,256,2048]{2,1,0:T(8,128)(2,1)}, u32[]{:S(2)}) copy-start(bf16[2,256,2048]{2,1,0:T(8,128)(2,1)} %param.10) | copy-start | bytes 6291460
  7.2 186.2 %all-gather.3.cloned.1.call-start = ((), (), s32[]{:S(2)}) async-start(), calls=%async_computation.3 | async-start | bytes 3932160 | tf_op jit(solution)/shard_map/all_gather | solution.py:1464
  73.0 202.3 %all-gather.5.cloned.1.call-start = ((), (), s32[]{:S(2)}) async-start(), calls=%async_computation.4 | async-start | bytes 7864320 | tf_op jit(solution)/shard_map/all_gather | solution.py:1464
  73.7 343.2 %reduce-scatter.4.cloned.1.call-start = ((), (), s32[]{:S(2)}) async-start(), calls=%async_computation.5 | async-start | bytes 3932160 | tf_op jit(solution)/shard_map/reduce_scatter | solution.py:1468
  75.2 2.7 copy-start.20
  75.3 118.1 %copy-start.13 = (f32[1,2048]{1,0:T(1,128)}, f32[1,2048]{1,0:T(1,128)S(1)}, u32[]{:S(2)}) copy-start(f32[1,2048]{1,0:T(1,128)S(1)} %reshape.144.gain_ref) | copy-start | bytes 24580
  76.9 9.0 %copy-start.8 = (f32[128,1]{1,0:T(8,128)}, f32[128,1]{1,0:T(8,128)S(1)}, u32[]{:S(2)}) copy-start(f32[128,1]{1,0:T(8,128)S(1)} %copy.23.gain_ref) | copy-start | bytes 1540
  77.2 8.6 %copy-start.9 = (f32[32,512]{1,0:T(8,128)}, f32[32,512]{1,0:T(8,128)S(1)}, u32[]{:S(2)}) copy-start(f32[32,512]{1,0:T(8,128)S(1)} %get-tuple-element.107.sin_ref) | copy-start | bytes 196612
  77.3 8.6 %copy-start.10 = (f32[32,512]{1,0:T(8,128)}, f32[32,512]{1,0:T(8,128)S(1)}, u32[]{:S(2)}) copy-start(f32[32,512]{1,0:T(8,128)S(1)} %get-tuple-element.108.cos_ref) | copy-start | bytes 196612
  77.8 8.0 %copy-start.14 = (bf16[512,2048]{1,0:T(8,128)(2,1)}, bf16[512,2048]{1,0:T(8,128)(2,1)S(1)}, u32[]{:S(2)}) copy-start(bf16[512,2048]{1,0:T(8,128)(2,1)S(1)} %multiply_convert_fusion.n_ref) | copy-start | bytes 6291460
  85.8 3.2 copy-start.7
  87.0 2.0 copy-start.1
  89.0 186.2 %copy-start.4 = (bf16[1280,512]{1,0:T(8,128)(2,1)}, bf16[1280,512]{1,0:T(8,128)(2,1)S(1)}, u32[]{:S(2)}) copy-start(bf16[1280,512]{1,0:T(8,128)(2,1)S(1)} %get-tuple-element.60.q_ref.refs_1_) | copy-start | bytes 3932164
  89.0 186.2 %copy-start.11 = (s32[8,512]{1,0:T(8,128)}, s32[8,512]{1,0:T(8,128)S(1)}, u32[]{:S(2)}) copy-start(s32[8,512]{1,0:T(8,128)S(1)} %broadcast_in_dim.43.start_ref.refs_0_) | copy-start | bytes 49156
  331.8 206.2 %reduce-scatter.6.cloned.1.call-start = ((), (), s32[]{:S(2)}) async-start(), calls=%async_computation.6 | async-start | bytes 3932160 | tf_op jit(solution)/shard_map/reduce_scatter | solution.py:1468
  416.9 227.0 %reduce-scatter.8.cloned.1.call-start = ((), (), s32[]{:S(2)}) async-start(), calls=%async_computation.7 | async-start | bytes 3932160 | tf_op jit(solution)/shard_map/reduce_scatter | solution.py:1468
  544.1 98.6 %copy-start.22 = (bf16[64]{0:T(256)(128)(2,1)S(1)}, bf16[64]{0:T(256)(128)(2,1)}, u32[]{:S(2)}) copy-start(bf16[64]{0:T(256)(128)(2,1)} %param.17) | copy-start | bytes 388
  544.1 98.6 %copy-start.23 = (bf16[64]{0:T(256)(128)(2,1)S(1)}, bf16[64]{0:T(256)(128)(2,1)}, u32[]{:S(2)}) copy-start(bf16[64]{0:T(256)(128)(2,1)} %param.16) | copy-start | bytes 388
  641.3 5.2 copy-start.17
  643.9 3.9 copy-start.15
  647.9 2.1 copy-start.18
  647.9 2.9 copy-start.19
  647.9 3.8 copy-start.16
  (5 other events, 5.1 us)
Sparse Core Ops, SparseCore 0:
  73.1 72.2 all-gather.2
  147.0 124.4 all-gather.4
  331.9 78.6 reduce-scatter.3
  417.0 101.5 reduce-scatter.5
  538.2 65.5 reduce-scatter.7

commit v7 on v6

--- a/solution.py
+++ b/solution.py
@@ -355,7 +355,7 @@
             for stages in each:
                 stages[back]()
 
-    @pl.loop(0, rows * KEY_VALUE_HEADS)
+    @pl.loop(0, rows * KEY_VALUE_HEADS, unroll=KEY_VALUE_HEADS)
     def _(i):
         tokens, wide, pair, head = spans(i, length)
         for g in range(GROUP):
@@ -370,7 +370,7 @@
         tall = full_ref.shape[0] // 32
         filled[...] = jnp.zeros_like(filled)
 
-        @pl.loop(0, 32)
+        @pl.loop(0, 32, unroll=8)
         def _(i):
             src = pl.ds(pl.multiple_of(i * out_rows, 8), out_rows)
             dst = pl.ds(pl.multiple_of(i * tall, 8), out_rows)
@@ -533,7 +533,7 @@
     stage(0)
     dq_ref[...] = jnp.zeros_like(dq_ref)
 
-    @pl.loop(0, rows * KEY_VALUE_HEADS)
+    @pl.loop(0, rows * KEY_VALUE_HEADS, unroll=KEY_VALUE_HEADS)
     def _(i):
         tokens, wide, pair, head = spans(i, length)
         for g in range(GROUP):
@@ -962,7 +962,7 @@
     width, chunk = p_ref.shape[0], 512
 
     def chunks(make, dst):
-        @pl.loop(0, width // chunk)
+        @pl.loop(0, width // chunk, unroll=2)
         def _(c):
             span = pl.ds(pl.multiple_of(c * chunk, chunk), chunk)
             dst[:, :, span] = make(span).astype(BF16).reshape(*dst.shape[:2], chunk)
@@ -1276,7 +1276,7 @@
         load(turn).wait()
         chunk = 512
 
-        @pl.loop(0, dst.shape[1] // chunk)
+        @pl.loop(0, dst.shape[1] // chunk, unroll=2)
         def _(c):
             span = pl.ds(pl.multiple_of(c * chunk, chunk), chunk)
             dst[:, span] = multiply(g_v[turn % 2], span).astype(BF16)

time: 670 us -> 668 us (level)
  no operation moved by 1% of the time
where the time goes in v7:
time: 668 us; the launch traced here: 658 us
  Pallas kernels  607 us (91%)
  local copies, waits for them, and re-layouts  17.4 us (3%)
  between operations  14.5 us (2%)
  other arithmetic  9.9 us (1%)
  matrix products  7.97 us (1%)
    pallas_call x1, Pallas kernels, attend_back(): pl.pallas_call(functools.partial(attend_back_kernel, n, rows, bool(more))...  110 us
    pallas_call x1, Pallas kernels, attend(): pl.pallas_call(functools.partial(attend_kernel, n, rows, len(more), out_r...  101 us
    pallas_call x1, Pallas kernels, sum_weights(): pl.pallas_call(sum_weights_kernel, out_shape=[jax.ShapeDtypeStruct((rows,...  96.1 us
    pallas_call x1, Pallas kernels, plane_sum(): pl.pallas_call(plane_sum_kernel, out_shape=[jax.ShapeDtypeStruct((rows, w...  83.9 us
    pallas_call x1, Pallas kernels, plane_gather(): pl.pallas_call(functools.partial(plane_kernel, 2), out_shape=[jax.ShapeDt...  80.5 us
    pallas_call x1, Pallas kernels, gather_weights(): pl.pallas_call(functools.partial(weights_kernel, n), out_shape=[jax.Shape...  61.5 us
    pallas_call x1, Pallas kernels, gate_up_product(): pl.pallas_call(functools.partial(gate_up_kernel, n_dp, n_seq), grid=(toke...  37.6 us
    pallas_call x1, Pallas kernels, transposed_product(): pl.pallas_call(transposed_kernel, grid=(width // tall,), in_specs=[pl.Blo...  18.9 us
  transfers between devices with their start and end apart: 5, of which 0 were waited for; matrix products, arithmetic and copies ran while one was open for 2% of the time, Pallas kernels for 74%

profile of v7, /device:TPU:0, one launch (start us, length us, event | category | flops | bytes accessed | tf_op | source)
XLA Modules:
  0.0 658.2 jit_solution(13835157549345892104)
XLA Ops:
  7.2 1.7 pad.9.refs_1_
  9.8 1.7 maximum_maximum_fusion.refs_0_.own_ref
  11.4 61.5 %gather_weights.1 = (bf16[32,64,2048]{2,1,0:T(8,128)(2,1)}, bf16[4,48,2048]{2,1,0:T(8,128)(2,1)}, bf16[8,64,1536]{2,1,0:T(8,128)(2,1)}) custom-call(bf16[64,2048]{1,0:T(8,128)(2,1)} %maximum_maximum_fusion.refs_0_.own_ref, bf16[48,2048]{1,0:T(8,128)(2,1)} %pad.9.refs_1_, bf16[64,12288]{1,0:T(8,128)(2,1)} %refs_6_.1), custom_call_target="tpu_custom_call" | custom-call | tf_op jit(solution)/shard_map/gather_weights/pallas_call | solution.py:768
  77.9 8.0 %fusion.p_ref = f32[2048,512]{1,0:T(8,128)S(1)} fusion(bf16[2048,2048]{1,0:T(8,128)(2,1)} %bitcast.41, bf16[512,2048]{1,0:T(8,128)(2,1)S(1)} %multiply_convert_fusion.n_ref), kind=kOutput, calls=%fused_computation.18 | convolution fusion | flops 4294967296 | bytes 14680064 | tf_op jit(solution)/shard_map/dot_general | solution.py:1514
  85.9 1.2 prepare.1
  87.1 2.0 copy-done.1
  89.0 100.7 %attend.1 = (bf16[1280,512]{1,0:T(8,128)(2,1)S(1)}, f32[5,8,512]{2,1,0:T(8,128)S(1)}, bf16[3,640,512]{2,1,0:T(8,128)(2,1)}, bf16[8,512,2048]{2,1,0:T(8,128)(2,1)...) custom-call(s32[8,512]{1,0:T(8,128)S(1)} %broadcast_in_dim.43.start_ref.refs_0_, ...), custom_call_target="tpu_custom_call" | custom-call | tf_op jit(solution)/shard_map/attend/pallas_call | solution.py:414
  189.7 1.1 copy-done.2
  191.7 1.0 copy-done.6
  193.4 1.4 copy-done.3
  194.8 80.5 %plane_gather.1 = (bf16[8,512,2048]{2,1,0:T(8,128)(2,1)}, bf16[4096,768]{1,0:T(8,128)(2,1)}, f32[512,2048]{1,0:T(8,128)}) custom-call(bf16[1536,512]{1,0:T(8,128)(2,1)S(1)} %copy-done.3, bf16[8,4,48,2048]{3,2,1,0:T(8,128)(2,1)} %get-tuple-element.64.w_ref, bf16[512,2048]{1,0:T(8,128)(2,1)S(1)} %bitcast.34, f32[1,2048]{1,0:T(1,128)S(1)} %reshape.144.gain_ref, ...), custom_call_target="tpu_custom_call" | custom-call | tf_op jit(solution)/shard_map/plane_gather/pallas_call | solution.py:1135
  275.3 37.6 %gate_up.1 = (bf16[4096,768]{1,0:T(8,128)(2,1)}, bf16[4096,1536]{1,0:T(8,128)(2,1)}) custom-call(bf16[4096,2048]{1,0:T(8,128)(2,1)} %bitcast.38, bf16[4096,768]{1,0:T(8,128)(2,1)} %get-tuple-element.69.dh_ref, bf16[2048,1536]{1,0:T(8,128)(2,1)} %all-gather.5.cloned.1.call-done.w_ref), custom_call_target="tpu_custom_call" | custom-call | flops 25769803776 | bytes 48234496 | tf_op jit(solution)/shard_map/gate_up/pallas_call | solution.py:1431
  312.9 18.9 %transposed_product.1 = bf16[4,8,64,768]{3,2,1,0:T(8,128)(2,1)} custom-call(bf16[4096,2048]{1,0:T(8,128)(2,1)} %bitcast.39, bf16[4096,1536]{1,0:T(8,128)(2,1)} %get-tuple-element.73.g_ref), custom_call_target="tpu_custom_call" | custom-call | flops 12884901888 | bytes 26214400 | tf_op jit(solution)/shard_map/transposed_product/pallas_call | solution.py:1174
  332.1 83.9 %plane_sum.1 = (bf16[512,2048]{1,0:T(8,128)(2,1)}, bf16[768,2048]{1,0:T(8,128)(2,1)}, bf16[4,8,64,768]{3,2,1,0:T(8,128)(2,1)}) custom-call(bf16[4096,1536]{1,0:T(8,128)(2,1)} %get-tuple-element.73.g_ref, bf16[2048,1536]{1,0:T(8,128)(2,1)} %all-gather.5.cloned.1.call-done.w_ref, bf16[4096,768]{1,0:T(8,128)(2,1)} %get-tuple-element.74.h_ref.refs_7_, ...), custom_call_target="tpu_custom_call" | custom-call | tf_op jit(solution)/shard_map/plane_sum/pallas_call | solution.py:1368
  416.1 10.7 %middle_back.1 = (f32[512,2048]{1,0:T(8,128)}, bf16[512,2048]{1,0:T(8,128)(2,1)}, bf16[1280,512]{1,0:T(8,128)(2,1)}) custom-call(bf16[512,2048]{1,0:T(8,128)(2,1)} %get-tuple-element.77.dy_ref, f32[512,2048]{1,0:T(8,128)} %get-tuple-element.78.mid_ref.refs_9_, bf16[512,2048]{1,0:T(8,128)(2,1)} %bitcast.44, f32[1,2048]{1,0:T(1,128)} %copy-done.13, ...), custom_call_target="tpu_custom_call" | custom-call | tf_op jit(solution)/shard_map/middle_back/pallas_call | solution.py:928
  426.8 110.4 %attend_back.1 = (f32[1280,512]{1,0:T(8,128)}, f32[640,512]{1,0:T(8,128)}, bf16[512,2048]{1,0:T(8,128)(2,1)}) custom-call(s32[8,512]{1,0:T(8,128)} %copy-done.11, bf16[1280,512]{1,0:T(8,128)(2,1)} %copy-done.4, bf16[1280,512]{1,0:T(8,128)(2,1)} %get-tuple-element.79.refs_2_, bf16[1280,512]{1,0:T(8,128)(2,1)} %copy-done.6, f32[5,8,512]{2,1,0:T(8,128)} %copy-done.12, ...), custom_call_target="tpu_custom_call" | custom-call | tf_op jit(solution)/shard_map/attend_back/pallas_call | solution.py:594
  537.3 5.8 prepare_back.1
  543.1 96.1 %sum_weights.1 = (f32[64,1920]{1,0:T(8,128)}, f32[8,128]{1,0:T(8,128)}, f32[40,2048]{1,0:T(8,128)}, f32[512,2048]{1,0:T(8,128)}, f32[64,12288]{1,0:T(8,128)}) custom-call(bf16[512,2048]{1,0:T(8,128)(2,1)} %copy-done.14, bf16[2048,512]{1,0:T(8,128)(2,1)} %get-tuple-element.91.p_ref, bf16[1536,512]{1,0:T(8,128)(2,1)} %copy-done.2, ...), custom_call_target="tpu_custom_call" | custom-call | tf_op jit(solution)/shard_map/sum_weights/pallas_call | solution.py:1060
  639.2 1.3 slice_bitcast_fusion
  640.6 1.3 bitcast_divide_fusion
  641.8 2.6 convert_element_type.71
  644.4 1.3 copy.32
  645.8 2.1 copy.33
  649.6 1.7 copy.36
  (81 shorter events, 9.3 us)
Async XLA Ops:
  7.2 66.6 %copy-start.21 = (s32[2,4]{1,0:T(2,128)S(1)}, s32[2,4]{1,0:T(2,128)}, u32[]{:S(2)}) copy-start(s32[2,4]{1,0:T(2,128)} %param.11) | copy-start | bytes 100
  7.2 69.1 %copy-start = (bf16[2,256,2048]{2,1,0:T(8,128)(2,1)S(1)}, bf16[2,256,2048]{2,1,0:T(8,128)(2,1)}, u32[]{:S(2)}) copy-start(bf16[2,256,2048]{2,1,0:T(8,128)(2,1)} %param.10) | copy-start | bytes 6291460
  7.2 186.2 %all-gather.3.cloned.1.call-start = ((), (), s32[]{:S(2)}) async-start(), calls=%async_computation.3 | async-start | bytes 3932160 | tf_op jit(solution)/shard_map/all_gather | solution.py:1464
  73.0 202.3 %all-gather.5.cloned.1.call-start = ((), (), s32[]{:S(2)}) async-start(), calls=%async_computation.4 | async-start | bytes 7864320 | tf_op jit(solution)/shard_map/all_gather | solution.py:1464
  73.7 342.3 %reduce-scatter.4.cloned.1.call-start = ((), (), s32[]{:S(2)}) async-start(), calls=%async_computation.5 | async-start | bytes 3932160 | tf_op jit(solution)/shard_map/reduce_scatter | solution.py:1468
  75.2 2.7 copy-start.20
  75.3 118.1 %copy-start.13 = (f32[1,2048]{1,0:T(1,128)}, f32[1,2048]{1,0:T(1,128)S(1)}, u32[]{:S(2)}) copy-start(f32[1,2048]{1,0:T(1,128)S(1)} %reshape.144.gain_ref) | copy-start | bytes 24580
  76.9 9.0 %copy-start.8 = (f32[128,1]{1,0:T(8,128)}, f32[128,1]{1,0:T(8,128)S(1)}, u32[]{:S(2)}) copy-start(f32[128,1]{1,0:T(8,128)S(1)} %copy.23.gain_ref) | copy-start | bytes 1540
  77.2 8.6 %copy-start.9 = (f32[32,512]{1,0:T(8,128)}, f32[32,512]{1,0:T(8,128)S(1)}, u32[]{:S(2)}) copy-start(f32[32,512]{1,0:T(8,128)S(1)} %get-tuple-element.107.sin_ref) | copy-start | bytes 196612
  77.3 8.6 %copy-start.10 = (f32[32,512]{1,0:T(8,128)}, f32[32,512]{1,0:T(8,128)S(1)}, u32[]{:S(2)}) copy-start(f32[32,512]{1,0:T(8,128)S(1)} %get-tuple-element.108.cos_ref) | copy-start | bytes 196612
  77.8 8.0 %copy-start.14 = (bf16[512,2048]{1,0:T(8,128)(2,1)}, bf16[512,2048]{1,0:T(8,128)(2,1)S(1)}, u32[]{:S(2)}) copy-start(bf16[512,2048]{1,0:T(8,128)(2,1)S(1)} %multiply_convert_fusion.n_ref) | copy-start | bytes 6291460
  85.8 3.2 copy-start.7
  87.1 2.0 copy-start.1
  89.0 186.2 %copy-start.4 = (bf16[1280,512]{1,0:T(8,128)(2,1)}, bf16[1280,512]{1,0:T(8,128)(2,1)S(1)}, u32[]{:S(2)}) copy-start(bf16[1280,512]{1,0:T(8,128)(2,1)S(1)} %get-tuple-element.60.q_ref.refs_1_) | copy-start | bytes 3932164
  89.0 186.2 %copy-start.11 = (s32[8,512]{1,0:T(8,128)}, s32[8,512]{1,0:T(8,128)S(1)}, u32[]{:S(2)}) copy-start(s32[8,512]{1,0:T(8,128)S(1)} %broadcast_in_dim.43.start_ref.refs_0_) | copy-start | bytes 49156
  331.8 205.4 %reduce-scatter.6.cloned.1.call-start = ((), (), s32[]{:S(2)}) async-start(), calls=%async_computation.6 | async-start | bytes 3932160 | tf_op jit(solution)/shard_map/reduce_scatter | solution.py:1468
  416.1 225.8 %reduce-scatter.8.cloned.1.call-start = ((), (), s32[]{:S(2)}) async-start(), calls=%async_computation.7 | async-start | bytes 3932160 | tf_op jit(solution)/shard_map/reduce_scatter | solution.py:1468
  543.1 97.5 %copy-start.22 = (bf16[64]{0:T(256)(128)(2,1)S(1)}, bf16[64]{0:T(256)(128)(2,1)}, u32[]{:S(2)}) copy-start(bf16[64]{0:T(256)(128)(2,1)} %param.17) | copy-start | bytes 388
  543.1 97.5 %copy-start.23 = (bf16[64]{0:T(256)(128)(2,1)S(1)}, bf16[64]{0:T(256)(128)(2,1)}, u32[]{:S(2)}) copy-start(bf16[64]{0:T(256)(128)(2,1)} %param.16) | copy-start | bytes 388
  639.2 5.2 copy-start.17
  641.8 3.9 copy-start.15
  645.8 2.1 copy-start.18
  645.8 2.9 copy-start.19
  645.8 3.8 copy-start.16
  (5 other events, 5.1 us)
Sparse Core Ops, SparseCore 0:
  73.1 72.2 all-gather.2
  147.0 124.4 all-gather.4
  332.0 78.4 reduce-scatter.3
  416.2 102.2 reduce-scatter.5
  537.4 72.1 reduce-scatter.7
